TPU v7x, 256 devices: a whole 4x4x8 slice. The times are simulated.
256 devices in a mesh: gz: 4 (over y_hi, core), xy: 64 (over y_lo, z, x).
Axes of the slice: x: 4, y: 4 (y_hi: 2, y_lo: 2; y = y_hi * 2 + y_lo), z: 8, core: 2. Of those that a mesh axis runs over, the one named last changes fastest.
Arguments:
- images: bfloat16 [64, 8192, 256], P('gz', 'xy')
- offsets: int32 [128, 4, 2], P('xy'), may hold values from 0 to 63, as said below
- gaps: int32 [64], P('gz'), may hold values from 1 to 2
Outputs:
- smoothed_field: float32 [2, 64, 128, 4], P(None, 'gz', 'xy')
- composed_field: float32 [2, 64, 128, 4], P(None, 'gz', 'xy')
Inputs may be any that keep to these rules, and one draw needn't show every extreme that they name: `offsets`: for patch rows r with r mod 2 == 0 the row offset is below 16; for r mod 2 == 1 it is 48 or more.
All inputs are finite; a program needn't handle non-finite values.
Results may differ from a plain program's by a relative error of at most 0.0043.
Values may be sent and summed in bfloat16 or wider, within the bound.
No kernel may reach another device: no remote copies, remote signals or barrier semaphores. Data moves between devices by JAX's collectives and lax.ppermute only.
A program may use at most 64 MiB of HBM per device.

v0:
```python
from functools import partial
import math

import jax
import jax.numpy as jnp
from jax import lax
from jax.sharding import PartitionSpec as P

P_SIZE = 64
HALF = 32


SHARPNESS = 16.0


def shifted(value, axis, steps):
    count = lax.axis_size(axis)
    initial, last = (max(0, -steps), min(count, count - steps))
    return lax.ppermute(value, axis, [(source, source + steps) for source in range(initial, last)])


def padded_2(block, sides, width):
    for axis, dim in sides:
        count = lax.axis_size(axis)
        forward = [(i, i + 1) for i in range(count - 1)]
        backward = [(target, source) for source, target in forward]
        low = lax.ppermute(
            lax.slice_in_dim(block, block.shape[dim] - width, None, axis=dim), axis, forward
        )
        high = lax.ppermute(lax.slice_in_dim(block, 0, width, axis=dim), axis, backward)
        block = jnp.concatenate([low, block, high], axis=dim)
    return block


def carried_in(part, axis, combine, identity):
    place = lax.axis_index(axis)
    gathered = lax.all_gather(part, axis)
    state = jnp.zeros_like(part) + jnp.asarray(identity, part.dtype)

    def one(step, state):
        return combine(state, lax.dynamic_index_in_dim(gathered, step, 0, False))

    return lax.fori_loop(0, place, one, state)


def tables():
    indices = jnp.arange(P_SIZE, dtype=jnp.int32)
    product = indices[:, None] * indices[None, :] % P_SIZE
    angles = product.astype(jnp.float32) * (2.0 * math.pi / P_SIZE)
    return (jnp.cos(angles).astype(jnp.bfloat16), jnp.sin(angles).astype(jnp.bfloat16))


def cut_patches(padded, offsets):
    grid_rows = offsets.shape[0]
    grid_cols = offsets.shape[1]
    row_start = jnp.arange(grid_rows, dtype=jnp.int32)[:, None] * P_SIZE + offsets[:, :, 0]
    col_start = jnp.arange(grid_cols, dtype=jnp.int32)[None, :] * P_SIZE + offsets[:, :, 1]

    def take_patch(row_at, col_at):
        return lax.dynamic_slice(padded, (row_at, col_at), (P_SIZE, P_SIZE))

    return jax.vmap(take_patch)(row_start.reshape(-1), col_start.reshape(-1))


def forward(patches, cos_t, sin_t):
    total = patches.shape[0]
    row_pair = jnp.concatenate([cos_t, sin_t], 1)
    segment_one = jnp.dot(
        patches.reshape(total * P_SIZE, P_SIZE), row_pair, preferred_element_type=jnp.float32
    )
    segment_one = segment_one.astype(jnp.bfloat16).reshape(total, P_SIZE, 2 * P_SIZE)
    col_pair = jnp.concatenate([cos_t, sin_t], 0)
    blocks = jnp.einsum("kp,npq->nkq", col_pair, segment_one, preferred_element_type=jnp.float32)
    real_part = blocks[:, :P_SIZE, :P_SIZE] - blocks[:, P_SIZE:, P_SIZE:]
    imag_part = -(blocks[:, :P_SIZE, P_SIZE:] + blocks[:, P_SIZE:, :P_SIZE])
    return jnp.concatenate([real_part, imag_part], -1).astype(jnp.bfloat16)


def correlate(partner, current, cos_t, sin_t):
    total = partner.shape[0]
    part_re = partner[:, :, :P_SIZE].astype(jnp.float32)
    part_im = partner[:, :, P_SIZE:].astype(jnp.float32)
    own_re = current[:, :, :P_SIZE].astype(jnp.float32)
    own_im = current[:, :, P_SIZE:].astype(jnp.float32)
    cross_re = part_re * own_re + part_im * own_im
    cross_im = part_re * own_im - part_im * own_re
    cross = jnp.concatenate([cross_re, cross_im], -1).astype(jnp.bfloat16)
    col_pair = jnp.concatenate([cos_t, sin_t], 0)
    blocks = jnp.einsum("kp,npq->nkq", col_pair, cross, preferred_element_type=jnp.float32)
    mixed_re = blocks[:, :P_SIZE, :P_SIZE] - blocks[:, P_SIZE:, P_SIZE:]
    mixed_im = blocks[:, :P_SIZE, P_SIZE:] + blocks[:, P_SIZE:, :P_SIZE]
    segment_two = jnp.concatenate([mixed_re, mixed_im], -1).astype(jnp.bfloat16)
    back_table = jnp.concatenate([cos_t, -sin_t], 0)
    correlation = jnp.dot(
        segment_two.reshape(total * P_SIZE, 2 * P_SIZE),
        back_table,
        preferred_element_type=jnp.float32,
    )
    scores = correlation.reshape(total, P_SIZE * P_SIZE) * (
        SHARPNESS / (P_SIZE * P_SIZE * P_SIZE * P_SIZE)
    )
    weights = jax.nn.softmax(scores, axis=-1).reshape(total, P_SIZE, P_SIZE)
    indices = jnp.arange(P_SIZE, dtype=jnp.int32)
    signed = jnp.where(indices < HALF, indices, indices - P_SIZE).astype(jnp.float32)
    shift_rows = jnp.sum(jnp.sum(weights, axis=2) * signed[None, :], axis=1) / 8.0
    shift_cols = jnp.sum(jnp.sum(weights, axis=1) * signed[None, :], axis=1) / 8.0
    return (shift_rows, shift_cols)


def relaxed_step(extended):
    middle = extended[:, :, 1:-1]
    widened = jnp.pad(middle, ((0, 0), (0, 0), (0, 0), (1, 1)))
    beside_all = (
        extended[:, :, :-2] + extended[:, :, 2:] + widened[:, :, :, :-2] + widened[:, :, :, 2:]
    )
    return 0.5 * middle + 0.125 * beside_all


def add_fields(earlier, later):
    return earlier + later


def local(images, offsets, gaps):
    sections_here = images.shape[0]
    grid_rows = offsets.shape[0]
    grid_cols = offsets.shape[1]
    cos_t, sin_t = tables()
    prior_images = shifted(images[sections_here - 2 :], "gz", 1)
    strips = jnp.concatenate([prior_images, images], 0)
    padded = padded_2(strips, (("xy", 1),), HALF)
    padded = jnp.pad(padded, ((0, 0), (0, 0), (HALF, HALF)))
    patches = jax.vmap(partial(cut_patches, offsets=offsets))(padded)
    stacked_count = patches.shape[0]
    patch_count = patches.shape[1]
    spectra = forward(patches.reshape(stacked_count * patch_count, P_SIZE, P_SIZE), cos_t, sin_t)
    spectra = spectra.reshape(stacked_count, patch_count, P_SIZE, 2 * P_SIZE)
    current = spectra[2:]
    newer_spec = spectra[1:-1]
    older_spec = spectra[:-2]
    partner = jnp.where((gaps == 1)[:, None, None, None], newer_spec, older_spec)
    total = sections_here * patch_count
    shift_rows, shift_cols = correlate(
        partner.reshape(total, P_SIZE, 2 * P_SIZE),
        current.reshape(total, P_SIZE, 2 * P_SIZE),
        cos_t,
        sin_t,
    )
    measured = jnp.stack([shift_rows, shift_cols]).reshape(2, sections_here, grid_rows, grid_cols)
    smoothed = measured
    for sweep in range(2):
        bordered = padded_2(smoothed, (("xy", 2),), 1)
        smoothed = relaxed_step(bordered)
    running = jnp.cumsum(smoothed, axis=1)
    zeros_field = jnp.zeros((2, grid_rows, grid_cols), jnp.float32)
    earlier_sum = carried_in(running[:, sections_here - 1], "gz", add_fields, zeros_field)
    composed = running + earlier_sum[:, None]
    return (smoothed, composed)


def solution(mesh):
    in_specs = (P("gz", "xy", None), P("xy", None, None), P("gz"))
    out_specs = (P(None, "gz", "xy", None), P(None, "gz", "xy", None))
    return jax.shard_map(local, mesh=mesh, in_specs=in_specs, out_specs=out_specs, check_vma=False)
```

profile of v0, /device:TPU:25, one launch (start us, length us, event | category | flops | bytes accessed | tf_op | source)
XLA Modules:
  0.0 134.2 jit_solution(16284704817769339390)
XLA Ops:
  7.4 3.1 %collective-permute-start.1 = (bf16[18,32,256]{2,1,0:T(8,128)(2,1)S(1)}, bf16[18,32,256]{2,1,0:T(8,128)(2,1)S(1)}, u32[]{:S(2)}, u32[]{:S(2)}) collective-permute-start(bf16[18,32,256]{2,1,0:T(8,128)(2,1)S(1)} %get-tuple-element.80), channel_id=1, source_target_pairs={{0,1},{1,2},{2,3},{3,4},{4,5},{5,6},{6,7},{7,8},{8,9},{9,10},{10,1... | collective-permute-start | bytes 884744 | tf_op jit(solution)/shard_map/ppermute | solution.py:27
  10.5 8.7 %collective-permute-start.2 = (bf16[18,32,256]{2,1,0:T(8,128)(2,1)S(1)}, bf16[18,32,256]{2,1,0:T(8,128)(2,1)S(1)}, u32[]{:S(2)}, u32[]{:S(2)}) collective-permute-start(bf16[18,32,256]{2,1,0:T(8,128)(2,1)S(1)} %get-tuple-element.81), channel_id=1, source_target_pairs={{1,0},{2,1},{3,2},{4,3},{5,4},{6,5},{7,6},{8,7},{9,8},{10,9},{11,1... | collective-permute-start | bytes 884744 | tf_op jit(solution)/shard_map/ppermute | solution.py:30
  22.8 1.8 %fusion.15 = bf16[18,192,320]{2,1,0:T(8,128)(2,1)S(1)} fusion(bf16[18,32,256]{2,1,0:T(8,128)(2,1)S(1)} %collective-permute-done.2, bf16[18,128,256]{2,1,0:T(8,128)(2,1)S(1)} %constant_dynamic-update-slice_fusion, bf16[18,32,256]{2,1,0:T(8,128)(2,1)S(1)} %collective-permute-done.1), kind=kLoop, calls=%fused_computation.33 | loop fusion | flops 13271040 | bytes 3981312 | tf_op jit(solution)/shard_map/concatenate | solution.py:31
  24.6 28.7 %while.12 = (s32[]{:T(128)}, bf16[18,192,320]{2,1,0:T(8,128)(2,1)S(1)}, s32[8,2]{0,1:T(2,128)}, bf16[8,18,64,64]{3,2,1,0:T(8,128)(2,1)}, s32[]{:T(128)}) while((s32[]{:T(128)}, bf16[18,192,320]{2,1,0:T(8,128)(2,1)S(1)}, s32[8,2]{0,1:T(2,128)}, bf16[8,18,64,64]{3,2,1,0:T(8,128)(2,1)}, s32[]{:T(128)}) %tuple.53), condition=%wide.while_cond, body=%wide.while_body.sunk | while | flops 2 | bytes 444001 | solution.py:60
  26.0 2.2 %bitcast_dynamic-update-slice_fusion.2 = bf16[8,18,64,64]{3,2,1,0:T(8,128)(2,1)} fusion(bf16[8,18,64,64]{3,2,1,0:T(8,128)(2,1)} %get-tuple-element.155, s32[]{:T(128)} %get-tuple-element.152, bf16[18,192,320]{2,1,0:T(8,128)(2,1)S(1)} %get-tuple-element.158, s32[]{:T(128)} %bitcast.36, s32[]{:T(128)} %bitcast.37), kind=kLoop, calls=%fused_computation.1.clone.1 | loop fusion | bytes 443904 | tf_op jit(solution)/shard_map/vmap(vmap())/gather
  29.5 2.2 %bitcast_dynamic-update-slice_fusion.2 = bf16[8,18,64,64]{3,2,1,0:T(8,128)(2,1)} fusion(bf16[8,18,64,64]{3,2,1,0:T(8,128)(2,1)} %get-tuple-element.155, s32[]{:T(128)} %get-tuple-element.152, bf16[18,192,320]{2,1,0:T(8,128)(2,1)S(1)} %get-tuple-element.158, s32[]{:T(128)} %bitcast.36, s32[]{:T(128)} %bitcast.37), kind=kLoop, calls=%fused_computation.1.clone.1 | loop fusion | bytes 443904 | tf_op jit(solution)/shard_map/vmap(vmap())/gather
  33.1 2.2 %bitcast_dynamic-update-slice_fusion.2 = bf16[8,18,64,64]{3,2,1,0:T(8,128)(2,1)} fusion(bf16[8,18,64,64]{3,2,1,0:T(8,128)(2,1)} %get-tuple-element.155, s32[]{:T(128)} %get-tuple-element.152, bf16[18,192,320]{2,1,0:T(8,128)(2,1)S(1)} %get-tuple-element.158, s32[]{:T(128)} %bitcast.36, s32[]{:T(128)} %bitcast.37), kind=kLoop, calls=%fused_computation.1.clone.1 | loop fusion | bytes 443904 | tf_op jit(solution)/shard_map/vmap(vmap())/gather
  36.7 2.2 %bitcast_dynamic-update-slice_fusion.2 = bf16[8,18,64,64]{3,2,1,0:T(8,128)(2,1)} fusion(bf16[8,18,64,64]{3,2,1,0:T(8,128)(2,1)} %get-tuple-element.155, s32[]{:T(128)} %get-tuple-element.152, bf16[18,192,320]{2,1,0:T(8,128)(2,1)S(1)} %get-tuple-element.158, s32[]{:T(128)} %bitcast.36, s32[]{:T(128)} %bitcast.37), kind=kLoop, calls=%fused_computation.1.clone.1 | loop fusion | bytes 443904 | tf_op jit(solution)/shard_map/vmap(vmap())/gather
  40.3 2.2 %bitcast_dynamic-update-slice_fusion.2 = bf16[8,18,64,64]{3,2,1,0:T(8,128)(2,1)} fusion(bf16[8,18,64,64]{3,2,1,0:T(8,128)(2,1)} %get-tuple-element.155, s32[]{:T(128)} %get-tuple-element.152, bf16[18,192,320]{2,1,0:T(8,128)(2,1)S(1)} %get-tuple-element.158, s32[]{:T(128)} %bitcast.36, s32[]{:T(128)} %bitcast.37), kind=kLoop, calls=%fused_computation.1.clone.1 | loop fusion | bytes 443904 | tf_op jit(solution)/shard_map/vmap(vmap())/gather
  43.9 2.2 %bitcast_dynamic-update-slice_fusion.2 = bf16[8,18,64,64]{3,2,1,0:T(8,128)(2,1)} fusion(bf16[8,18,64,64]{3,2,1,0:T(8,128)(2,1)} %get-tuple-element.155, s32[]{:T(128)} %get-tuple-element.152, bf16[18,192,320]{2,1,0:T(8,128)(2,1)S(1)} %get-tuple-element.158, s32[]{:T(128)} %bitcast.36, s32[]{:T(128)} %bitcast.37), kind=kLoop, calls=%fused_computation.1.clone.1 | loop fusion | bytes 443904 | tf_op jit(solution)/shard_map/vmap(vmap())/gather
  47.4 2.2 %bitcast_dynamic-update-slice_fusion.2 = bf16[8,18,64,64]{3,2,1,0:T(8,128)(2,1)} fusion(bf16[8,18,64,64]{3,2,1,0:T(8,128)(2,1)} %get-tuple-element.155, s32[]{:T(128)} %get-tuple-element.152, bf16[18,192,320]{2,1,0:T(8,128)(2,1)S(1)} %get-tuple-element.158, s32[]{:T(128)} %bitcast.36, s32[]{:T(128)} %bitcast.37), kind=kLoop, calls=%fused_computation.1.clone.1 | loop fusion | bytes 443904 | tf_op jit(solution)/shard_map/vmap(vmap())/gather
  51.0 2.3 %bitcast_dynamic-update-slice_fusion.2 = bf16[8,18,64,64]{3,2,1,0:T(8,128)(2,1)} fusion(bf16[8,18,64,64]{3,2,1,0:T(8,128)(2,1)} %get-tuple-element.155, s32[]{:T(128)} %get-tuple-element.152, bf16[18,192,320]{2,1,0:T(8,128)(2,1)S(1)} %get-tuple-element.158, s32[]{:T(128)} %bitcast.36, s32[]{:T(128)} %bitcast.37), kind=kLoop, calls=%fused_computation.1.clone.1 | loop fusion | bytes 443904 | tf_op jit(solution)/shard_map/vmap(vmap())/gather
  53.3 3.5 %copy.16 = bf16[18,8,64,64]{2,1,0,3:T(8,128)(2,1)S(1)} copy(bf16[18,8,64,64]{3,2,0,1:T(8,128)(2,1)} %bitcast.39) | data formatting | bytes 2359296 | tf_op jit(solution)/shard_map/vmap(vmap())/gather | solution.py:60
  56.8 1.6 %reshape_reshape.3 = bf16[9216,64]{0,1:T(8,128)(2,1)S(1)} reshape(bf16[18,8,64,64]{2,1,0,3:T(8,128)(2,1)S(1)} %copy.16) | data formatting | bytes 2359296 | tf_op jit(solution)/shard_map/reshape;reshape | solution.py:69
  58.5 1.6 %convolution_convert_fusion = bf16[9216,128]{1,0:T(8,128)(2,1)S(1)} fusion(bf16[9216,64]{0,1:T(8,128)(2,1)S(1)} %reshape_reshape.3, bf16[64,64]{0,1:T(8,128)(2,1)} %get-tuple-element.90, bf16[64,64]{0,1:T(8,128)(2,1)S(1)} %get-tuple-element.91), kind=kOutput, calls=%fused_computation.3 | convolution fusion | flops 152207360 | bytes 3555328 | tf_op jit(solution)/shard_map/dot_general | solution.py:68
  61.6 2.6 %fusion.3 = (bf16[144,64,64]{2,1,0:T(8,128)(2,1)S(1)}, bf16[144,64,64]{2,1,0:T(8,128)(2,1)S(1)}) fusion(f32[144,128,128]{2,1,0:T(8,128)S(1)} %convolution_bitcast_fusion), kind=kLoop, calls=%fused_computation.16 | loop fusion | flops 2949120 | bytes 11796480 | tf_op jit(solution)/shard_map/convert.6
  64.3 3.9 %fusion.17 = bf16[128,64,128]{2,1,0:T(8,128)(2,1)S(1)} fusion(bf16[144,64,64]{2,1,0:T(8,128)(2,1)S(1)} %get-tuple-element.74, bf16[144,64,64]{2,1,0:T(8,128)(2,1)S(1)} %get-tuple-element.75, pred[128]{0:T(512)(128)(4,1)S(1)} %copy-done.3), kind=kLoop, calls=%fused_computation.37 | loop fusion | flops 9437184 | bytes 4456576 | tf_op jit(solution)/shard_map/jit(_where)/select_n | solution.py:140
  68.2 2.1 %fusion.5 = (bf16[128,64,64]{2,1,0:T(8,128)(2,1)S(1)}, bf16[128,64,64]{2,1,0:T(8,128)(2,1)S(1)}) fusion(bf16[144,64,64]{2,1,0:T(8,128)(2,1)S(1)} %get-tuple-element.75, bf16[128,64,128]{2,1,0:T(8,128)(2,1)S(1)} %fusion.17, bf16[144,64,64]{2,1,0:T(8,128)(2,1)S(1)} %get-tuple-element.74), kind=kLoop, calls=%fused_computation.18 | loop fusion | flops 6291456 | bytes 6291456 | tf_op jit(solution)/shard_map/convert.4
  70.3 2.1 %convolution_bitcast_fusion.1 = f32[128,128,128]{1,2,0:T(8,128)S(1)} fusion(bf16[128,64,64]{2,1,0:T(8,128)(2,1)S(1)} %get-tuple-element.79, bf16[128,64,64]{2,1,0:T(8,128)(2,1)S(1)} %get-tuple-element.78, bf16[64,64]{0,1:T(8,128)(2,1)S(1)} %copy-done, bf16[64,64]{0,1:T(8,128)(2,1)S(1)} %get-tuple-element.91), kind=kOutput, calls=%fused_computation.28 | convolution fusion | flops 272662528 | bytes 10502144 | tf_op jit(solution)/shard_map/kp,npq->nkq/dot_general | solution.py:89
  72.4 2.6 %fusion.9 = (bf16[128,64,64]{1,2,0:T(8,128)(2,1)S(1)}, bf16[128,64,64]{1,2,0:T(8,128)(2,1)S(1)}) fusion(f32[128,128,128]{1,2,0:T(8,128)S(1)} %convolution_bitcast_fusion.1), kind=kLoop, calls=%fused_computation.24 | loop fusion | flops 2097152 | bytes 10485760 | tf_op jit(solution)/shard_map/convert.3
  75.0 2.7 %copy.17 = bf16[128,64,64]{1,0,2:T(8,128)(2,1)} copy(bf16[128,64,64]{1,2,0:T(8,128)(2,1)S(1)} %get-tuple-element.76) | data formatting | bytes 2097152 | tf_op jit(solution)/shard_map/convert.3
  77.7 3.3 %concatenate.58 = bf16[8192,64]{0,1:T(8,128)(2,1)S(1)} reshape(bf16[128,64,64]{1,0,2:T(8,128)(2,1)} %copy.17) | data formatting | bytes 2097152 | tf_op jit(solution)/shard_map/concatenate | solution.py:92
  81.0 2.7 %copy.18 = bf16[128,64,64]{1,0,2:T(8,128)(2,1)} copy(bf16[128,64,64]{1,2,0:T(8,128)(2,1)S(1)} %get-tuple-element.77) | data formatting | bytes 2097152 | tf_op jit(solution)/shard_map/convert.2
  83.7 4.2 %concatenate.59 = bf16[8192,64]{0,1:T(8,128)(2,1)} reshape(bf16[128,64,64]{1,0,2:T(8,128)(2,1)} %copy.18) | data formatting | bytes 2097152 | tf_op jit(solution)/shard_map/concatenate | solution.py:92
  87.9 1.8 %fusion.58 = (f32[8192]{0:T(1024)S(1)}, f32[8192,64]{0,1:T(8,128)S(1)}) fusion(bf16[8192,64]{0,1:T(8,128)(2,1)} %concatenate.59, bf16[8192,64]{0,1:T(8,128)(2,1)S(1)} %concatenate.58, bf16[64,64]{0,1:T(8,128)(2,1)S(1)} %copy-done.1, bf16[64,64]{0,1:T(8,128)(2,1)S(1)} %get-tuple-element.91), kind=kOutput, calls=%fused_computation.118 | convolution fusion | flops 139485184 | bytes 4243456 | tf_op jit(solution)/shard_map/dot_general | solution.py:94
  89.7 3.0 %mul.143 = f32[128,64,64]{1,0,2:T(8,128)} reshape(f32[8192,64]{0,1:T(8,128)S(1)} %get-tuple-element.87) | data formatting | bytes 4194304 | tf_op jit(solution)/shard_map/mul | solution.py:99
  93.6 3.4 %fusion.10 = f32[128,64]{0,1:T(8,128)S(1)} fusion(f32[128,64,64]{1,0,2:T(8,128)} %mul.143, f32[128]{0:T(128)S(1)} %reduce_sum.56, f32[128]{0:T(128)S(1)} %reduce_max.18), kind=kLoop, calls=%fused_computation.26 | loop fusion | flops 1564672 | bytes 2130944 | tf_op jit(solution)/shard_map/reduce_sum | solution.py:106
  98.3 1.9 %collective-permute-start.3 = (f32[2,16,1,4]{1,3,2,0:T(4,128)S(1)}, f32[2,16,1,4]{1,3,2,0:T(4,128)S(1)}, u32[]{:S(2)}, u32[]{:S(2)}) collective-permute-start(f32[2,16,1,4]{1,3,2,0:T(4,128)S(1)} %get-tuple-element.84), channel_id=1, source_target_pairs={{0,1},{1,2},{2,3},{3,4},{4,5},{5,6},{6,7},{7,8},{8,9},{9,10},{10,1... | collective-permute-start | bytes 1544 | tf_op jit(solution)/shard_map/ppermute | solution.py:27
  100.2 8.0 %collective-permute-start.4 = (f32[2,16,1,4]{1,3,2,0:T(4,128)S(1)}, f32[2,16,1,4]{1,3,2,0:T(4,128)S(1)}, u32[]{:S(2)}, u32[]{:S(2)}) collective-permute-start(f32[2,16,1,4]{1,3,2,0:T(4,128)S(1)} %get-tuple-element.85), channel_id=1, source_target_pairs={{1,0},{2,1},{3,2},{4,3},{5,4},{6,5},{7,6},{8,7},{9,8},{10,9},{11,1... | collective-permute-start | bytes 1544 | tf_op jit(solution)/shard_map/ppermute | solution.py:30
  109.0 1.9 %collective-permute-start.5 = (f32[2,16,1,4]{1,3,2,0:T(4,128)S(1)}, f32[2,16,1,4]{1,3,2,0:T(4,128)S(1)}, u32[]{:S(2)}, u32[]{:S(2)}) collective-permute-start(f32[2,16,1,4]{1,3,2,0:T(4,128)S(1)} %get-tuple-element.82), channel_id=1, source_target_pairs={{0,1},{1,2},{2,3},{3,4},{4,5},{5,6},{6,7},{7,8},{8,9},{9,10},{10,1... | collective-permute-start | bytes 1544 | tf_op jit(solution)/shard_map/ppermute | solution.py:27
  110.9 7.8 %collective-permute-start.6 = (f32[2,16,1,4]{1,3,2,0:T(4,128)S(1)}, f32[2,16,1,4]{1,3,2,0:T(4,128)S(1)}, u32[]{:S(2)}, u32[]{:S(2)}) collective-permute-start(f32[2,16,1,4]{1,3,2,0:T(4,128)S(1)} %get-tuple-element.83), channel_id=1, source_target_pairs={{1,0},{2,1},{3,2},{4,3},{5,4},{6,5},{7,6},{8,7},{9,8},{10,9},{11,1... | collective-permute-start | bytes 1544 | tf_op jit(solution)/shard_map/ppermute | solution.py:30
  119.7 13.6 %all-gather = f32[8,1,2,4]{3,2,1,0:T(2,128)S(1)} all-gather(f32[2,1,2,4]{3,2,1,0:T(2,128)S(1)} %slice.175), channel_id=2, replica_groups=mesh['gz'=4,'xy'=64] {'gz'}, dimensions={0}, use_global_device_ids=true | all-gather | bytes 320 | tf_op jit(solution)/shard_map/all_gather | solution.py:37
  (91 shorter events, 27.2 us)
Async XLA Ops:
  1.5 4.4 %collective-permute-start = (bf16[2,128,256]{2,1,0:T(8,128)(2,1)S(1)}, bf16[2,128,256]{2,1,0:T(8,128)(2,1)S(1)}, u32[]{:S(2)}, u32[]{:S(2)}) collective-permute-start(bf16[2,128,256]{2,1,0:T(8,128)(2,1)S(1)} %slice.108), channel_id=1, source_target_pairs={{0,64},{64,128},{128,192},{1,65},{65,129},{129,193},{2,66},{66,130... | collective-permute-start | bytes 393224 | tf_op jit(solution)/shard_map/ppermute | solution.py:19
  7.4 14.0 %collective-permute-start.1 = (bf16[18,32,256]{2,1,0:T(8,128)(2,1)S(1)}, bf16[18,32,256]{2,1,0:T(8,128)(2,1)S(1)}, u32[]{:S(2)}, u32[]{:S(2)}) collective-permute-start(bf16[18,32,256]{2,1,0:T(8,128)(2,1)S(1)} %get-tuple-element.80), channel_id=1, source_target_pairs={{0,1},{1,2},{2,3},{3,4},{4,5},{5,6},{6,7},{7,8},{8,9},{9,10},{10,1... | collective-permute-start | bytes 884744 | tf_op jit(solution)/shard_map/ppermute | solution.py:27
  10.5 12.3 %collective-permute-start.2 = (bf16[18,32,256]{2,1,0:T(8,128)(2,1)S(1)}, bf16[18,32,256]{2,1,0:T(8,128)(2,1)S(1)}, u32[]{:S(2)}, u32[]{:S(2)}) collective-permute-start(bf16[18,32,256]{2,1,0:T(8,128)(2,1)S(1)} %get-tuple-element.81), channel_id=1, source_target_pairs={{1,0},{2,1},{3,2},{4,3},{5,4},{6,5},{7,6},{8,7},{9,8},{10,9},{11,1... | collective-permute-start | bytes 884744 | tf_op jit(solution)/shard_map/ppermute | solution.py:30
  58.5 1.6 %copy-start = (bf16[64,64]{0,1:T(8,128)(2,1)S(1)}, bf16[64,64]{0,1:T(8,128)(2,1)}, u32[]{:S(2)}) copy-start(bf16[64,64]{0,1:T(8,128)(2,1)} %get-tuple-element.90) | copy-start | bytes 24580
  61.6 2.7 %copy-start.3 = (pred[128]{0:T(512)(128)(4,1)S(1)}, pred[128]{0:T(512)(128)(4,1)}, u32[]{:S(2)}) copy-start(pred[128]{0:T(512)(128)(4,1)} %broadcast_in_dim.13) | copy-start | bytes 388
  83.7 4.2 %copy-start.1 = (bf16[64,64]{0,1:T(8,128)(2,1)S(1)}, bf16[64,64]{0,1:T(8,128)(2,1)}, u32[]{:S(2)}) copy-start(bf16[64,64]{0,1:T(8,128)(2,1)} %fusion.47) | copy-start | bytes 24580
  93.6 4.2 %copy-start.4 = (f32[64]{0:T(128)S(1)}, f32[64]{0:T(128)}, u32[]{:S(2)}) copy-start(f32[64]{0:T(128)} %fusion.50) | copy-start | bytes 772
  98.3 10.0 %collective-permute-start.3 = (f32[2,16,1,4]{1,3,2,0:T(4,128)S(1)}, f32[2,16,1,4]{1,3,2,0:T(4,128)S(1)}, u32[]{:S(2)}, u32[]{:S(2)}) collective-permute-start(f32[2,16,1,4]{1,3,2,0:T(4,128)S(1)} %get-tuple-element.84), channel_id=1, source_target_pairs={{0,1},{1,2},{2,3},{3,4},{4,5},{5,6},{6,7},{7,8},{8,9},{9,10},{10,1... | collective-permute-start | bytes 1544 | tf_op jit(solution)/shard_map/ppermute | solution.py:27
  100.2 8.8 %collective-permute-start.4 = (f32[2,16,1,4]{1,3,2,0:T(4,128)S(1)}, f32[2,16,1,4]{1,3,2,0:T(4,128)S(1)}, u32[]{:S(2)}, u32[]{:S(2)}) collective-permute-start(f32[2,16,1,4]{1,3,2,0:T(4,128)S(1)} %get-tuple-element.85), channel_id=1, source_target_pairs={{1,0},{2,1},{3,2},{4,3},{5,4},{6,5},{7,6},{8,7},{9,8},{10,9},{11,1... | collective-permute-start | bytes 1544 | tf_op jit(solution)/shard_map/ppermute | solution.py:30
  109.0 9.8 %collective-permute-start.5 = (f32[2,16,1,4]{1,3,2,0:T(4,128)S(1)}, f32[2,16,1,4]{1,3,2,0:T(4,128)S(1)}, u32[]{:S(2)}, u32[]{:S(2)}) collective-permute-start(f32[2,16,1,4]{1,3,2,0:T(4,128)S(1)} %get-tuple-element.82), channel_id=1, source_target_pairs={{0,1},{1,2},{2,3},{3,4},{4,5},{5,6},{6,7},{7,8},{8,9},{9,10},{10,1... | collective-permute-start | bytes 1544 | tf_op jit(solution)/shard_map/ppermute | solution.py:27
  110.9 8.6 %collective-permute-start.6 = (f32[2,16,1,4]{1,3,2,0:T(4,128)S(1)}, f32[2,16,1,4]{1,3,2,0:T(4,128)S(1)}, u32[]{:S(2)}, u32[]{:S(2)}) collective-permute-start(f32[2,16,1,4]{1,3,2,0:T(4,128)S(1)} %get-tuple-element.83), channel_id=1, source_target_pairs={{1,0},{2,1},{3,2},{4,3},{5,4},{6,5},{7,6},{8,7},{9,8},{10,9},{11,1... | collective-permute-start | bytes 1544 | tf_op jit(solution)/shard_map/ppermute | solution.py:30
  119.5 14.6 %copy-start.2 = (f32[2,16,2,4]{1,3,2,0:T(4,128)}, f32[2,16,2,4]{1,3,2,0:T(4,128)S(1)}, u32[]{:S(2)}) copy-start(f32[2,16,2,4]{1,3,2,0:T(4,128)S(1)} %fusion.44) | copy-start | bytes 3076
where the time goes:
time: 135 us; the launch traced here: 134 us
  local copies, waits for them, and re-layouts  55.7 us (41%)
  starting transfers between devices  32.8 us (24%)
  other arithmetic  20.9 us (15%)
  blocking collectives  13.6 us (10%)
  matrix products  6.97 us (5%)
  waiting for transfers between devices  3.06 us (2%)
    gather x24, local copies, waits for them, and re-layouts  28.7 us
    ppermute x3, starting transfers between devices, padded_2(): lax.ppermute(lax.slice_in_dim(block, 0, width, axis=dim), axis, backward)  24.5 us
    all_gather x1, blocking collectives, carried_in(): gathered = lax.all_gather(part, axis)  13.6 us
    concatenate x2, local copies, waits for them, and re-layouts, correlate(): segment_two = jnp.concatenate([mixed_re, mixed_im], -1).astype(jnp.bfloat16)  7.48 us
    another operation x3, other arithmetic  7.32 us
    ppermute x3, starting transfers between devices, padded_2(): lax.ppermute(lax.slice_in_dim(block, block.shape[dim] - width, None, axis...  6.96 us
    another operation x3, local copies, waits for them, and re-layouts  5.41 us
    select_n x1, other arithmetic, local(): jnp.where((gaps == 1)[:, None, None, None], newer_spec, older_spec)  3.93 us
  transfers between devices with their start and end apart: 7, of which 4 were waited for; matrix products, arithmetic and copies ran while one was open for 4% of the time, Pallas kernels for 0%

commit v1 on v0

v1 whole, which is shorter than its diff:
```python
import math

import jax
import jax.numpy as jnp
import ml_dtypes
import numpy as np
from jax import lax
from jax.experimental import pallas as pl
from jax.experimental.pallas import tpu as pltpu
from jax.sharding import PartitionSpec as P

P_SIZE = 64
HALF = 32
SHARPNESS = 16.0
WIN = 128
GR = 2
GC = 4
PATCHES = GR * GC


def shifted(value, axis, steps):
    count = lax.axis_size(axis)
    initial, last = (max(0, -steps), min(count, count - steps))
    return lax.ppermute(value, axis, [(source, source + steps) for source in range(initial, last)])


def tables():
    indices = np.arange(P_SIZE)
    angles = (indices[:, None] * indices[None, :] % P_SIZE) * (2.0 * math.pi / P_SIZE)
    cos_t = np.cos(angles).astype(np.float32).astype(ml_dtypes.bfloat16).astype(np.float32)
    sin_t = np.sin(angles).astype(np.float32).astype(ml_dtypes.bfloat16).astype(np.float32)
    sin_t = np.where(np.abs(sin_t) < 1e-6, np.float32(0), sin_t)
    return cos_t, sin_t


def make_constants():
    cos_t, sin_t = tables()
    zero = np.zeros((P_SIZE, P_SIZE), np.float32)
    cols = np.zeros((2 * P_SIZE, 256), np.float32)
    cols[:P_SIZE, :P_SIZE] = cos_t
    cols[P_SIZE:, :P_SIZE] = sin_t
    from_u = np.concatenate([cos_t, -sin_t, -sin_t, cos_t], 1)
    from_v = np.concatenate([-sin_t, -cos_t, -cos_t, -sin_t], 1)
    edge = np.zeros((P_SIZE, 256), np.float32)
    rows = np.stack([np.concatenate([t, edge], 0) for t in (from_u, from_v)])
    to_re = np.concatenate([cos_t, cos_t, -sin_t, sin_t], 0)
    to_im = np.concatenate([sin_t, sin_t, cos_t, -cos_t], 0)
    blank = np.zeros_like(to_re)
    back_k = np.concatenate(
        [
            np.concatenate([to_re, blank, to_im, blank], 1),
            np.concatenate([blank, to_re, blank, to_im], 1),
        ],
        0,
    )
    scale = SHARPNESS / P_SIZE**4
    back_l = np.concatenate([cos_t, -sin_t], 1) * np.float32(scale)
    bf = ml_dtypes.bfloat16
    return cols, rows, back_k.astype(bf), back_l.astype(bf)


def patch_kernel(
    off_ref, gap_ref, own_ref, prior_ref, low_ref, high_ref, cols_ref, rows_ref, back_k_ref, back_l_ref,
    out_ref, m_ref, x_ref, w_ref, z_ref, ab_ref, g_ref, max_ref, sum_ref, mom_ref,
):
    sections = own_ref.shape[0]
    stacked = sections + 2
    f32 = jnp.float32
    bf16 = jnp.bfloat16
    lane = lax.broadcasted_iota(jnp.int32, (2 * P_SIZE, 256), 1)
    for r in range(GR):
        for c in range(GC):
            i = r * GC + c
            row_at = off_ref[r, c, 0]
            start = c * P_SIZE - HALF + off_ref[r, c, 1]
            turn = jnp.where(start < 0, start + 256, start)
            turned = pltpu.roll(cols_ref[...], turn, 1)
            inside = (lane >= start) & (lane < start + P_SIZE)
            m_ref[r, c * 128 : (c + 1) * 128, :] = jnp.where(inside, turned, 0.0).astype(bf16)
            for half in range(2):
                w_ref[i, half * WIN : (half + 1) * WIN, :] = pltpu.roll(rows_ref[half], row_at, 0).astype(bf16)

    def window(r, t):
        image = prior_ref.at[t] if t < 2 else own_ref.at[t - 2]
        if r == 0:
            return [low_ref[t], image[: WIN - HALF]]
        return [image[HALF:], high_ref[t]]

    for r in range(GR):
        for pair in range(stacked // 2):
            both = jnp.concatenate(window(r, 2 * pair) + window(r, 2 * pair + 1), 0)
            first = lax.dot_general(m_ref[r], both, (((1,), (1,)), ((), ())), preferred_element_type=f32)
            first = first.astype(bf16)
            for c in range(GC):
                for half in range(2):
                    for k in range(2):
                        t = 2 * pair + k
                        x_ref[r * GC + c, t * 64 : (t + 1) * 64, half * WIN : (half + 1) * WIN] = first[
                            c * 128 + half * 64 : c * 128 + (half + 1) * 64, k * WIN : (k + 1) * WIN
                        ]

    signed = lax.broadcasted_iota(jnp.int32, (P_SIZE, sections * P_SIZE), 0)
    signed = jnp.where(signed < HALF, signed, signed - P_SIZE).astype(f32)

    def one_patch(i, carry):
        z_ref[...] = jnp.dot(x_ref[i], w_ref[i], preferred_element_type=f32).astype(bf16)
        for s in range(sections):
            at = pl.multiple_of((s + 2 - gap_ref[s]) * 64, 64)
            partner = z_ref[pl.ds(at, 64), 0:128]
            row, col = (s // 2) * 64, (s % 2) * 256
            ab_ref[row : row + 64, col : col + 128] = partner * z_ref[(s + 2) * 64 : (s + 3) * 64, 0:128]
            ab_ref[row : row + 64, col + 128 : col + 256] = partner * z_ref[(s + 2) * 64 : (s + 3) * 64, 128:256]
        mixed = jnp.dot(ab_ref[...], back_k_ref[...], preferred_element_type=f32).astype(bf16)
        for pair in range(sections // 2):
            g_ref[0:64, pair * 128 : (pair + 1) * 128] = mixed[pair * 64 : (pair + 1) * 64, 0:128]
            g_ref[64:128, pair * 128 : (pair + 1) * 128] = mixed[pair * 64 : (pair + 1) * 64, 128:256]
        scores = jnp.dot(back_l_ref[...], g_ref[...], preferred_element_type=f32)
        top = jnp.max(scores, axis=0, keepdims=True)
        weights = jnp.exp(scores - top)
        max_ref[pl.ds(i, 1), :] = top
        sum_ref[pl.ds(i, 1), :] = jnp.sum(weights, axis=0, keepdims=True)
        mom_ref[pl.ds(i, 1), :] = jnp.sum(weights * signed, axis=0, keepdims=True)
        return carry

    lax.fori_loop(0, PATCHES, one_patch, 0)

    lane = lax.broadcasted_iota(jnp.int32, (PATCHES, 128), 1)
    left = lane < 64
    shift = lane % 64
    shift = jnp.where(shift < HALF, shift, shift - P_SIZE).astype(f32)
    place = lax.broadcasted_iota(jnp.int32, (PATCHES, sections), 1)
    rows_out = jnp.zeros((PATCHES, sections), f32)
    cols_out = jnp.zeros((PATCHES, sections), f32)
    for pair in range(sections // 2):
        part = slice(pair * 128, (pair + 1) * 128)
        top = max_ref[:, part]
        top_a = jnp.max(jnp.where(left, top, -jnp.inf), axis=1, keepdims=True)
        top_b = jnp.max(jnp.where(left, -jnp.inf, top), axis=1, keepdims=True)
        factor = jnp.exp(top - jnp.where(left, top_a, top_b))
        total = factor * sum_ref[:, part]
        moment = factor * mom_ref[:, part]
        for k in range(2):
            mine = left if k == 0 else jnp.logical_not(left)
            den = jnp.sum(jnp.where(mine, total, 0.0), axis=1, keepdims=True)
            along_u = jnp.sum(jnp.where(mine, total * shift, 0.0), axis=1, keepdims=True)
            along_v = jnp.sum(jnp.where(mine, moment, 0.0), axis=1, keepdims=True)
            here = place == 2 * pair + k
            rows_out = jnp.where(here, along_u / den / 8.0, rows_out)
            cols_out = jnp.where(here, along_v / den / 8.0, cols_out)
    out_ref[0:PATCHES, :] = rows_out
    out_ref[PATCHES:, :] = cols_out


def measure(offsets, gaps, images, prior, low, high):
    sections = images.shape[0]
    stacked = sections + 2
    cols, rows, back_k, back_l = make_constants()
    smem = pl.BlockSpec(memory_space=pltpu.SMEM)
    vmem = pl.BlockSpec(memory_space=pltpu.VMEM)
    bf16 = jnp.bfloat16
    return pl.pallas_call(
        patch_kernel,
        out_shape=jax.ShapeDtypeStruct((2 * PATCHES, sections), jnp.float32),
        in_specs=[smem, smem] + [vmem] * 8,
        out_specs=vmem,
        scratch_shapes=[
            pltpu.VMEM((GR, GC * 128, 256), bf16),
            pltpu.VMEM((PATCHES, stacked * 64, 2 * WIN), bf16),
            pltpu.VMEM((PATCHES, 2 * WIN, 256), bf16),
            pltpu.VMEM((stacked * 64, 256), bf16),
            pltpu.VMEM((sections * 32, 512), bf16),
            pltpu.VMEM((128, sections * 64), bf16),
            pltpu.VMEM((PATCHES, sections * 64), jnp.float32),
            pltpu.VMEM((PATCHES, sections * 64), jnp.float32),
            pltpu.VMEM((PATCHES, sections * 64), jnp.float32),
        ],
        compiler_params=pltpu.CompilerParams(vmem_limit_bytes=48 * 1024 * 1024),
    )(offsets, gaps, images, prior, low, high, cols, rows, back_k, back_l)


def relaxed_step(extended):
    middle = extended[:, 1:-1]
    widened = jnp.pad(middle, ((0, 0), (0, 0), (1, 1), (0, 0)))
    beside = extended[:, :-2] + extended[:, 2:] + widened[:, :, :-2] + widened[:, :, 2:]
    return 0.5 * middle + 0.125 * beside


def local(images, offsets, gaps):
    sections = images.shape[0]
    rows_here = images.shape[1]
    prior = shifted(images[sections - 2 :], "gz", 1)
    top = jnp.concatenate([prior[:, :HALF], images[:, :HALF]], 0)
    bottom = jnp.concatenate([prior[:, rows_here - HALF :], images[:, rows_here - HALF :]], 0)
    low = shifted(bottom, "xy", 1)
    high = shifted(top, "xy", -1)
    measured = measure(offsets, gaps, images, prior, low, high)
    above = shifted(measured, "xy", 1).reshape(2, GR, GC, sections)
    below = shifted(measured, "xy", -1).reshape(2, GR, GC, sections)
    measured = measured.reshape(2, GR, GC, sections)
    wide = relaxed_step(jnp.concatenate([above, measured, below], 1))
    place = lax.axis_index("xy")
    row = place * GR + jnp.arange(-1, GR + 1)
    inside = (row >= 0) & (row < GR * lax.axis_size("xy"))
    wide = jnp.where(inside[None, :, None, None], wide, 0.0)
    smoothed = relaxed_step(wide).transpose(0, 3, 1, 2)
    running = jnp.cumsum(smoothed, axis=1)
    gathered = lax.all_gather(running[:, sections - 1], "gz")
    earlier = jnp.arange(gathered.shape[0]) < lax.axis_index("gz")
    earlier_sum = jnp.sum(jnp.where(earlier[:, None, None, None], gathered, 0.0), axis=0)
    return smoothed, running + earlier_sum[:, None]


def solution(mesh):
    in_specs = (P("gz", "xy", None), P("xy", None, None), P("gz"))
    out_specs = (P(None, "gz", "xy", None), P(None, "gz", "xy", None))
    return jax.shard_map(local, mesh=mesh, in_specs=in_specs, out_specs=out_specs, check_vma=False)
```

time: 135 us -> 58.7 us (0.43)
  local copies, waits for them, and re-layouts: 55.7 us -> 3.44 us
  other arithmetic: 20.9 us -> 0.29 us
  Pallas kernels: 0 us -> 11.6 us
  starting transfers between devices: 32.8 us -> 23.4 us
  matrix products: 6.97 us -> 0 us
  waiting for transfers between devices: 3.06 us -> 5.32 us
    gather x25 -> x0, local copies, waits for them, and re-layouts: 32.2 us -> none
    ppermute x6 -> x0, starting transfers between devices: 31.5 us -> none  [the longest x3 24.5 us: padded_2(): lax.ppermute(lax.slice_in_dim(block, 0, width, axis=dim), axis, backward)]
    ppermute x1 -> x5, starting transfers between devices: 1.29 us -> 23.4 us  [shifted(): lax.ppermute(value, axis, [(source, source + steps) for source in range(i...]
    pallas_call x0 -> x1, Pallas kernels: none -> 11.6 us  [measure(): pl.pallas_call(patch_kernel, out_shape=jax.ShapeDtypeStruct((2 * PATCHES,...]
    concatenate x3 -> x0, local copies, waits for them, and re-layouts: 8.78 us -> none  [the longest x2 7.48 us: correlate(): segment_two = jnp.concatenate([mixed_re, mixed_im], -1).astype(jnp.bfloat16)]
    another operation x5 -> x0, other arithmetic: 7.33 us -> none
    another operation x4 -> x0, local copies, waits for them, and re-layouts: 7.04 us -> none
    dot_general x4 -> x0, matrix products: 6.97 us -> none  [the longest x1 2.1 us: correlate(): jnp.einsum('kp,npq->nkq', col_pair, cross, preferred_element_type=jnp.flo...]
  transfers between devices with their start and end apart: 7 -> 5, of which waited for: 4 -> 4; matrix products, arithmetic and copies ran while one was open for 4% -> 2% of each run, Pallas kernels for 0% -> 0%
where the time goes in v1:
time: 58.7 us; the launch traced here: 58.4 us
  starting transfers between devices  23.4 us (40%)
  blocking collectives  13.5 us (23%)
  Pallas kernels  11.6 us (20%)
  waiting for transfers between devices  5.32 us (9%)
  local copies, waits for them, and re-layouts  3.44 us (6%)
  between operations  0.82 us (1%)
    ppermute x5, starting transfers between devices, shifted(): lax.ppermute(value, axis, [(source, source + steps) for source in range(i...  23.4 us
    all_gather x1, blocking collectives, local(): gathered = lax.all_gather(running[:, sections - 1], 'gz')  13.5 us
    pallas_call x1, Pallas kernels, measure(): pl.pallas_call(patch_kernel, out_shape=jax.ShapeDtypeStruct((2 * PATCHES,...  11.6 us
    ppermute x5, waiting for transfers between devices, shifted(): lax.ppermute(value, axis, [(source, source + steps) for source in range(i...  5.32 us
    unnamed x18, local copies, waits for them, and re-layouts  1.32 us
  transfers between devices with their start and end apart: 5, of which 4 were waited for; matrix products, arithmetic and copies ran while one was open for 2% of the time, Pallas kernels for 0%

profile of v1, /device:TPU:25, one launch (start us, length us, event | category | flops | bytes accessed | tf_op | source)
XLA Modules:
  0.0 58.4 jit_solution(12348006177151588293)
XLA Ops:
  0.6 0.9 %slice.46 = bf16[2,128,256]{2,1,0:T(8,128)(2,1)S(1)} slice(bf16[16,128,256]{2,1,0:T(8,128)(2,1)} %own_ref.1), slice={[14:16], [0:128], [0:256]} | slice | bytes 262144 | tf_op jit(solution)/shard_map/slice | solution.py:191
  1.5 0.0 copy-start
  1.6 1.4 %collective-permute-start = (bf16[2,128,256]{2,1,0:T(8,128)(2,1)S(1)}, bf16[2,128,256]{2,1,0:T(8,128)(2,1)S(1)}, u32[]{:S(2)}, u32[]{:S(2)}) collective-permute-start(bf16[2,128,256]{2,1,0:T(8,128)(2,1)S(1)} %slice.46), channel_id=1, source_target_pairs={{0,64},{64,128},{128,192},{1,65},{65,129},{129,193},{2,66},{66,130... | collective-permute-start | bytes 393224 | tf_op jit(solution)/shard_map/ppermute | solution.py:24
  3.0 1.1 %fusion.10 = (bf16[16,32,256]{2,1,0:T(8,128)(2,1)S(1)}, bf16[16,32,256]{2,1,0:T(8,128)(2,1)S(1)}) fusion(bf16[16,128,256]{2,1,0:T(8,128)(2,1)} %own_ref.1), kind=kLoop, calls=%fused_computation.24 | loop fusion | bytes 1048576 | tf_op jit(solution)/shard_map/slice | solution.py:192
  4.1 1.0 %collective-permute-done.prior_ref = bf16[2,128,256]{2,1,0:T(8,128)(2,1)S(1)} collective-permute-done((bf16[2,128,256]{2,1,0:T(8,128)(2,1)S(1)}, bf16[2,128,256]{2,1,0:T(8,128)(2,1)S(1)}, u32[]{:S(2)}, u32[]{:S(2)}) %collective-permute-start) | collective-permute-done | bytes 131104 | tf_op jit(solution)/shard_map/ppermute | solution.py:24
  5.2 3.3 %collective-permute-start.1 = (bf16[18,32,256]{2,1,0:T(8,128)(2,1)S(1)}, bf16[18,32,256]{2,1,0:T(8,128)(2,1)S(1)}, u32[]{:S(2)}, u32[]{:S(2)}) collective-permute-start(bf16[18,32,256]{2,1,0:T(8,128)(2,1)S(1)} %pad_maximum_fusion), channel_id=1, source_target_pairs={{0,1},{1,2},{2,3},{3,4},{4,5},{5,6},{6,7},{7,8},{8,9},{9,10},{10,1... | collective-permute-start | bytes 884744 | tf_op jit(solution)/shard_map/ppermute | solution.py:24
  8.4 0.0 copy-start.7
  8.4 0.0 copy-start.1
  8.4 0.0 copy-start.2
  8.5 0.0 copy-start.4
  8.5 8.8 %collective-permute-start.2 = (bf16[18,32,256]{2,1,0:T(8,128)(2,1)S(1)}, bf16[18,32,256]{2,1,0:T(8,128)(2,1)S(1)}, u32[]{:S(2)}, u32[]{:S(2)}) collective-permute-start(bf16[18,32,256]{2,1,0:T(8,128)(2,1)S(1)} %pad_maximum_fusion.1), channel_id=1, source_target_pairs={{1,0},{2,1},{3,2},{4,3},{5,4},{6,5},{7,6},{8,7},{9,8},{10,9},{11,1... | collective-permute-start | bytes 884744 | tf_op jit(solution)/shard_map/ppermute | solution.py:24
  17.3 0.0 copy-done.7
  17.3 0.1 copy.13.off_ref
  17.4 1.8 %collective-permute-done.1.low_ref = bf16[18,32,256]{2,1,0:T(8,128)(2,1)S(1)} collective-permute-done((bf16[18,32,256]{2,1,0:T(8,128)(2,1)S(1)}, bf16[18,32,256]{2,1,0:T(8,128)(2,1)S(1)}, u32[]{:S(2)}, u32[]{:S(2)}) %collective-permute-start.1) | collective-permute-done | bytes 294944 | tf_op jit(solution)/shard_map/ppermute | solution.py:24
  19.3 1.7 %collective-permute-done.2.high_ref = bf16[18,32,256]{2,1,0:T(8,128)(2,1)S(1)} collective-permute-done((bf16[18,32,256]{2,1,0:T(8,128)(2,1)S(1)}, bf16[18,32,256]{2,1,0:T(8,128)(2,1)S(1)}, u32[]{:S(2)}, u32[]{:S(2)}) %collective-permute-start.2) | collective-permute-done | bytes 294944 | tf_op jit(solution)/shard_map/ppermute | solution.py:24
  21.0 0.0 copy-done
  21.0 0.0 copy-done.3
  21.0 0.0 copy-done.1
  21.0 0.0 copy-done.2
  21.0 0.0 copy-done.4
  21.0 11.6 %shard_map.86 = f32[16,16]{1,0:T(8,128)S(1)} custom-call(s32[2,4,2]{2,1,0:T(4,128)S(1)} %copy.13.off_ref, s32[16]{0:T(128)S(1)} %copy-done.5, bf16[16,128,256]{2,1,0:T(8,128)(2,1)S(1)} %copy-done, bf16[2,128,256]{2,1,0:T(8,128)(2,1)S(1)} %collective-permute-done.prior_ref, bf16[18,32,256]{2,1,0:T(8,128)(2,1)S(1)} %collective-permute-done.1.low_ref, ...), custom_call_target="tpu_custom_call" | custom-call | tf_op jit(solution)/shard_map/pallas_call | solution.py:161
  32.6 1.9 %collective-permute-start.3 = (f32[16,16]{1,0:T(8,128)S(1)}, f32[16,16]{1,0:T(8,128)S(1)}, u32[]{:S(2)}, u32[]{:S(2)}) collective-permute-start(f32[16,16]{1,0:T(8,128)S(1)} %shard_map.86), channel_id=1, source_target_pairs={{0,1},{1,2},{2,3},{3,4},{4,5},{5,6},{6,7},{7,8},{8,9},{9,10},{10,1... | collective-permute-start | bytes 3080 | tf_op jit(solution)/shard_map/ppermute | solution.py:24
  34.5 8.0 %collective-permute-start.4 = (f32[16,16]{1,0:T(8,128)S(1)}, f32[16,16]{1,0:T(8,128)S(1)}, u32[]{:S(2)}, u32[]{:S(2)}) collective-permute-start(f32[16,16]{1,0:T(8,128)S(1)} %shard_map.86), channel_id=1, source_target_pairs={{1,0},{2,1},{3,2},{4,3},{5,4},{6,5},{7,6},{8,7},{9,8},{10,9},{11,1... | collective-permute-start | bytes 3080 | tf_op jit(solution)/shard_map/ppermute | solution.py:24
  42.6 0.0 collective-permute-done.3
  42.6 0.7 %collective-permute-done.4 = f32[16,16]{1,0:T(8,128)S(1)} collective-permute-done((f32[16,16]{1,0:T(8,128)S(1)}, f32[16,16]{1,0:T(8,128)S(1)}, u32[]{:S(2)}, u32[]{:S(2)}) %collective-permute-start.4) | collective-permute-done | bytes 1056 | tf_op jit(solution)/shard_map/ppermute | solution.py:24
  43.3 0.1 fusion.4
  43.4 0.0 copy-start.6
  43.4 0.1 copy.14
  43.6 0.5 copy-done.6
  44.1 13.5 %all-gather = f32[8,1,2,4]{3,2,1,0:T(2,128)S(1)} all-gather(f32[2,1,2,4]{3,2,1,0:T(2,128)S(1)} %slice.65), channel_id=2, replica_groups=mesh['gz'=4,'xy'=64] {'gz'}, dimensions={0}, use_global_device_ids=true | all-gather | bytes 320 | tf_op jit(solution)/shard_map/all_gather | solution.py:207
  57.6 0.1 select_reduce_fusion
  57.7 0.7 %copy.17 = f32[2,16,2,4]{1,3,2,0:T(4,128)} copy(f32[2,16,2,4]{3,2,1,0:T(2,128)S(1)} %broadcast_add_fusion) | data formatting | bytes 2048
  (16 shorter events, 0.2 us)
Async XLA Ops:
  1.5 19.4 %copy-start = (bf16[16,128,256]{2,1,0:T(8,128)(2,1)S(1)}, bf16[16,128,256]{2,1,0:T(8,128)(2,1)}, u32[]{:S(2)}) copy-start(bf16[16,128,256]{2,1,0:T(8,128)(2,1)} %own_ref.1) | copy-start | bytes 3145732
  1.6 3.6 %collective-permute-start = (bf16[2,128,256]{2,1,0:T(8,128)(2,1)S(1)}, bf16[2,128,256]{2,1,0:T(8,128)(2,1)S(1)}, u32[]{:S(2)}, u32[]{:S(2)}) collective-permute-start(bf16[2,128,256]{2,1,0:T(8,128)(2,1)S(1)} %slice.46), channel_id=1, source_target_pairs={{0,64},{64,128},{128,192},{1,65},{65,129},{129,193},{2,66},{66,130... | collective-permute-start | bytes 393224 | tf_op jit(solution)/shard_map/ppermute | solution.py:24
  5.1 15.8 %copy-start.3 = (f32[128,256]{1,0:T(8,128)S(1)}, f32[128,256]{1,0:T(8,128)}, u32[]{:S(2)}) copy-start(f32[128,256]{1,0:T(8,128)} %constant.38.clone.cols_ref) | copy-start | bytes 393220
  5.2 14.1 %collective-permute-start.1 = (bf16[18,32,256]{2,1,0:T(8,128)(2,1)S(1)}, bf16[18,32,256]{2,1,0:T(8,128)(2,1)S(1)}, u32[]{:S(2)}, u32[]{:S(2)}) collective-permute-start(bf16[18,32,256]{2,1,0:T(8,128)(2,1)S(1)} %pad_maximum_fusion), channel_id=1, source_target_pairs={{0,1},{1,2},{2,3},{3,4},{4,5},{5,6},{6,7},{7,8},{8,9},{9,10},{10,1... | collective-permute-start | bytes 884744 | tf_op jit(solution)/shard_map/ppermute | solution.py:24
  8.4 8.9 %copy-start.7 = (s32[2,4,2]{1,2,0:T(2,128)S(1)}, s32[2,4,2]{1,2,0:T(2,128)}, u32[]{:S(2)}) copy-start(s32[2,4,2]{1,2,0:T(2,128)} %param.8) | copy-start | bytes 196
  8.4 12.5 %copy-start.1 = (f32[2,128,256]{2,1,0:T(8,128)S(1)}, f32[2,128,256]{2,1,0:T(8,128)}, u32[]{:S(2)}) copy-start(f32[2,128,256]{2,1,0:T(8,128)} %constant.39.clone.rows_ref) | copy-start | bytes 786436
  8.4 12.5 %copy-start.2 = (bf16[512,256]{1,0:T(8,128)(2,1)S(1)}, bf16[512,256]{1,0:T(8,128)(2,1)}, u32[]{:S(2)}) copy-start(bf16[512,256]{1,0:T(8,128)(2,1)} %constant.40.clone.back_k_ref) | copy-start | bytes 786436
  8.5 12.5 %copy-start.4 = (bf16[64,128]{1,0:T(8,128)(2,1)S(1)}, bf16[64,128]{1,0:T(8,128)(2,1)}, u32[]{:S(2)}) copy-start(bf16[64,128]{1,0:T(8,128)(2,1)} %constant.41.clone.back_l_ref) | copy-start | bytes 49156
  8.5 12.4 %collective-permute-start.2 = (bf16[18,32,256]{2,1,0:T(8,128)(2,1)S(1)}, bf16[18,32,256]{2,1,0:T(8,128)(2,1)S(1)}, u32[]{:S(2)}, u32[]{:S(2)}) collective-permute-start(bf16[18,32,256]{2,1,0:T(8,128)(2,1)S(1)} %pad_maximum_fusion.1), channel_id=1, source_target_pairs={{1,0},{2,1},{3,2},{4,3},{5,4},{6,5},{7,6},{8,7},{9,8},{10,9},{11,1... | collective-permute-start | bytes 884744 | tf_op jit(solution)/shard_map/ppermute | solution.py:24
  17.4 3.6 %copy-start.5 = (s32[16]{0:T(128)S(1)}, s32[16]{0:T(128)}, u32[]{:S(2)}) copy-start(s32[16]{0:T(128)} %gap_ref.1) | copy-start | bytes 196
  32.6 10.0 %collective-permute-start.3 = (f32[16,16]{1,0:T(8,128)S(1)}, f32[16,16]{1,0:T(8,128)S(1)}, u32[]{:S(2)}, u32[]{:S(2)}) collective-permute-start(f32[16,16]{1,0:T(8,128)S(1)} %shard_map.86), channel_id=1, source_target_pairs={{0,1},{1,2},{2,3},{3,4},{4,5},{5,6},{6,7},{7,8},{8,9},{9,10},{10,1... | collective-permute-start | bytes 3080 | tf_op jit(solution)/shard_map/ppermute | solution.py:24
  34.5 8.8 %collective-permute-start.4 = (f32[16,16]{1,0:T(8,128)S(1)}, f32[16,16]{1,0:T(8,128)S(1)}, u32[]{:S(2)}, u32[]{:S(2)}) collective-permute-start(f32[16,16]{1,0:T(8,128)S(1)} %shard_map.86), channel_id=1, source_target_pairs={{1,0},{2,1},{3,2},{4,3},{5,4},{6,5},{7,6},{8,7},{9,8},{10,9},{11,1... | collective-permute-start | bytes 3080 | tf_op jit(solution)/shard_map/ppermute | solution.py:24
  43.4 0.6 %copy-start.6 = (f32[2,16,2,4]{1,3,2,0:T(4,128)}, f32[2,16,2,4]{1,3,2,0:T(4,128)S(1)}, u32[]{:S(2)}) copy-start(f32[2,16,2,4]{1,3,2,0:T(4,128)S(1)} %fusion.9) | copy-start | bytes 3076

commit v2 on v1

--- a/solution.py
+++ b/solution.py
@@ -35,16 +35,17 @@
 
 def make_constants():
     cos_t, sin_t = tables()
-    zero = np.zeros((P_SIZE, P_SIZE), np.float32)
-    cols = np.zeros((2 * P_SIZE, 256), np.float32)
-    cols[:P_SIZE, :P_SIZE] = cos_t
-    cols[P_SIZE:, :P_SIZE] = sin_t
+    half = P_SIZE // 2
+    cols = np.zeros((P_SIZE + 8, 256), np.float32)
+    cols[:half, :P_SIZE] = cos_t[:half]
+    cols[half:P_SIZE, :P_SIZE] = sin_t[:half]
+    cols[P_SIZE:, :P_SIZE] = cos_t[half]
     from_u = np.concatenate([cos_t, -sin_t, -sin_t, cos_t], 1)
     from_v = np.concatenate([-sin_t, -cos_t, -cos_t, -sin_t], 1)
     edge = np.zeros((P_SIZE, 256), np.float32)
     rows = np.stack([np.concatenate([t, edge], 0) for t in (from_u, from_v)])
-    to_re = np.concatenate([cos_t, cos_t, -sin_t, sin_t], 0)
-    to_im = np.concatenate([sin_t, sin_t, cos_t, -cos_t], 0)
+    to_re = np.concatenate([cos_t, -sin_t], 0)
+    to_im = np.concatenate([sin_t, cos_t], 0)
     blank = np.zeros_like(to_re)
     back_k = np.concatenate(
         [
@@ -53,21 +54,25 @@
         ],
         0,
     )
+    weight = np.where(np.arange(half) == 0, 1.0, 2.0).astype(np.float32)
+    one = np.concatenate([cos_t[:, :half] * weight, -sin_t[:, :half] * weight], 1)
+    one[:, half] = cos_t[:, half]
     scale = SHARPNESS / P_SIZE**4
-    back_l = np.concatenate([cos_t, -sin_t], 1) * np.float32(scale)
+    back_l = np.kron(np.eye(GC, dtype=np.float32), one * np.float32(scale))
     bf = ml_dtypes.bfloat16
     return cols, rows, back_k.astype(bf), back_l.astype(bf)
 
 
 def patch_kernel(
     off_ref, gap_ref, own_ref, prior_ref, low_ref, high_ref, cols_ref, rows_ref, back_k_ref, back_l_ref,
-    out_ref, m_ref, x_ref, w_ref, z_ref, ab_ref, g_ref, max_ref, sum_ref, mom_ref,
+    out_ref, m_ref, x_ref, w_ref, z_ref, n_ref, y_ref, g_ref, max_ref, sum_ref, mom_ref,
 ):
     sections = own_ref.shape[0]
     stacked = sections + 2
     f32 = jnp.float32
     bf16 = jnp.bfloat16
-    lane = lax.broadcasted_iota(jnp.int32, (2 * P_SIZE, 256), 1)
+    main = stacked * 32
+    lane = lax.broadcasted_iota(jnp.int32, cols_ref.shape, 1)
     for r in range(GR):
         for c in range(GC):
             i = r * GC + c
@@ -76,7 +81,9 @@
             turn = jnp.where(start < 0, start + 256, start)
             turned = pltpu.roll(cols_ref[...], turn, 1)
             inside = (lane >= start) & (lane < start + P_SIZE)
-            m_ref[r, c * 128 : (c + 1) * 128, :] = jnp.where(inside, turned, 0.0).astype(bf16)
+            turned = jnp.where(inside, turned, 0.0)
+            m_ref[r, c * 64 : (c + 1) * 64, :] = turned[:64].astype(bf16)
+            m_ref[r, 256 + c * 16 : 256 + (c + 1) * 16, :] = jnp.concatenate([turned[64:]] * 2, 0).astype(bf16)
             for half in range(2):
                 w_ref[i, half * WIN : (half + 1) * WIN, :] = pltpu.roll(rows_ref[half], row_at, 0).astype(bf16)
 
@@ -86,43 +93,91 @@
             return [low_ref[t], image[: WIN - HALF]]
         return [image[HALF:], high_ref[t]]
 
+    sub = lax.broadcasted_iota(jnp.int32, (8, WIN), 0)
     for r in range(GR):
+        nyquist = [[jnp.zeros((8, WIN), f32) for _ in range(3)] for _ in range(GC)]
         for pair in range(stacked // 2):
             both = jnp.concatenate(window(r, 2 * pair) + window(r, 2 * pair + 1), 0)
             first = lax.dot_general(m_ref[r], both, (((1,), (1,)), ((), ())), preferred_element_type=f32)
-            first = first.astype(bf16)
             for c in range(GC):
-                for half in range(2):
-                    for k in range(2):
-                        t = 2 * pair + k
-                        x_ref[r * GC + c, t * 64 : (t + 1) * 64, half * WIN : (half + 1) * WIN] = first[
-                            c * 128 + half * 64 : c * 128 + (half + 1) * 64, k * WIN : (k + 1) * WIN
-                        ]
-
-    signed = lax.broadcasted_iota(jnp.int32, (P_SIZE, sections * P_SIZE), 0)
+                for k in range(2):
+                    t = 2 * pair + k
+                    for half in range(2):
+                        x_ref[r * GC + c, t * 32 : (t + 1) * 32, half * WIN : (half + 1) * WIN] = first[
+                            c * 64 + half * 32 : c * 64 + (half + 1) * 32, k * WIN : (k + 1) * WIN
+                        ].astype(bf16)
+                    block, at = (2, t) if t < 2 else ((t - 2) // 8, (t - 2) % 8)
+                    row = first[256 + c * 16 : 264 + c * 16, k * WIN : (k + 1) * WIN]
+                    nyquist[c][block] = jnp.where(sub == at, row, nyquist[c][block])
+        for c in range(GC):
+            i = r * GC + c
+            x_ref[i, main : main + 16, :WIN] = jnp.concatenate(nyquist[c][:2], 0).astype(bf16)
+            x_ref[i, main + 16 :, :WIN] = jnp.concatenate([nyquist[c][2]] * 2, 0).astype(bf16)
+            x_ref[i, main:, WIN:] = jnp.zeros((32, WIN), bf16)
+
+    for i in range(PATCHES):
+        z_ref[i] = jnp.dot(x_ref[i], w_ref[i], preferred_element_type=f32).astype(bf16)
+
+    def crossed(partner_p, partner_q, own_p, own_q):
+        left = lax.broadcasted_iota(jnp.int32, partner_p.shape, 1) < 64
+        twice_re = jnp.where(left, partner_p, partner_q)
+        twice_im = jnp.where(left, partner_q, -partner_p)
+        return twice_re * own_p + twice_im * own_q
+
+    back = lax.broadcasted_iota(jnp.int32, (16, 128), 0)
+    gap_rows = jnp.ones((16, 128), jnp.int32)
+    for s in range(sections):
+        gap_rows = jnp.where(back == s, gap_ref[s], gap_rows)
+    even = back % 2 == 0
+    for i in range(PATCHES):
+        for s in range(sections):
+            at = pl.multiple_of((s + 2 - gap_ref[s]) * 32, 32)
+            row = i * 256 + (s // 2) * 32
+            y_ref[row : row + 32, (s % 2) * 128 : (s % 2 + 1) * 128] = crossed(
+                z_ref[i, pl.ds(at, 32), 0:128],
+                z_ref[i, pl.ds(at, 32), 128:256],
+                z_ref[i, (s + 2) * 32 : (s + 3) * 32, 0:128],
+                z_ref[i, (s + 2) * 32 : (s + 3) * 32, 128:256],
+            )
+        own = z_ref[i, main : main + 16, :].astype(f32)
+        n_ref[i, 8:24, :] = own
+        n_ref[i, 0:8, :] = pltpu.roll(z_ref[i, main + 16 : main + 32, :].astype(f32)[0:8], 6, 0)
+        one_up = n_ref[i, 7:23, :]
+        two_up = n_ref[i, 6:22, :]
+        partner_p = jnp.where(gap_rows == 1, one_up[:, :128], two_up[:, :128])
+        partner_q = jnp.where(gap_rows == 1, one_up[:, 128:], two_up[:, 128:])
+        line = crossed(partner_p, partner_q, own[:, :128], own[:, 128:])
+        row = PATCHES * 256 + i * 16
+        y_ref[row : row + 16, 0:128] = jnp.where(even, line, 0.0).astype(bf16)
+        y_ref[row : row + 16, 128:256] = jnp.where(even, 0.0, line).astype(bf16)
+
+    lines = jnp.dot(y_ref[PATCHES * 256 :, :], back_k_ref[:, :128], preferred_element_type=f32)
+    first_row = lax.broadcasted_iota(jnp.int32, (32, 128), 0) == 0
+    for i in range(PATCHES):
+        mixed = jnp.dot(y_ref[i * 256 : (i + 1) * 256, :], back_k_ref[...], preferred_element_type=f32)
+        at = (i % GC) * 64
+        for pair in range(sections // 2):
+            line = lines[i * 16 + 2 * pair : i * 16 + 2 * pair + 1] + lines[i * 16 + 2 * pair + 1 : i * 16 + 2 * pair + 2]
+            part = slice(pair * 128, (pair + 1) * 128)
+            g_ref[i // GC, at : at + 32, part] = mixed[pair * 32 : (pair + 1) * 32, 0:128].astype(bf16)
+            g_ref[i // GC, at + 32 : at + 64, part] = jnp.where(
+                first_row, line, mixed[pair * 32 : (pair + 1) * 32, 128:256]
+            ).astype(bf16)
+
+    signed = lax.broadcasted_iota(jnp.int32, (P_SIZE, 256), 0)
     signed = jnp.where(signed < HALF, signed, signed - P_SIZE).astype(f32)
-
-    def one_patch(i, carry):
-        z_ref[...] = jnp.dot(x_ref[i], w_ref[i], preferred_element_type=f32).astype(bf16)
-        for s in range(sections):
-            at = pl.multiple_of((s + 2 - gap_ref[s]) * 64, 64)
-            partner = z_ref[pl.ds(at, 64), 0:128]
-            row, col = (s // 2) * 64, (s % 2) * 256
-            ab_ref[row : row + 64, col : col + 128] = partner * z_ref[(s + 2) * 64 : (s + 3) * 64, 0:128]
-            ab_ref[row : row + 64, col + 128 : col + 256] = partner * z_ref[(s + 2) * 64 : (s + 3) * 64, 128:256]
-        mixed = jnp.dot(ab_ref[...], back_k_ref[...], preferred_element_type=f32).astype(bf16)
-        for pair in range(sections // 2):
-            g_ref[0:64, pair * 128 : (pair + 1) * 128] = mixed[pair * 64 : (pair + 1) * 64, 0:128]
-            g_ref[64:128, pair * 128 : (pair + 1) * 128] = mixed[pair * 64 : (pair + 1) * 64, 128:256]
-        scores = jnp.dot(back_l_ref[...], g_ref[...], preferred_element_type=f32)
-        top = jnp.max(scores, axis=0, keepdims=True)
-        weights = jnp.exp(scores - top)
-        max_ref[pl.ds(i, 1), :] = top
-        sum_ref[pl.ds(i, 1), :] = jnp.sum(weights, axis=0, keepdims=True)
-        mom_ref[pl.ds(i, 1), :] = jnp.sum(weights * signed, axis=0, keepdims=True)
-        return carry
-
-    lax.fori_loop(0, PATCHES, one_patch, 0)
+    for r in range(GR):
+        for block in range(sections * P_SIZE // 256):
+            part = slice(block * 256, (block + 1) * 256)
+            all_scores = jnp.dot(back_l_ref[...], g_ref[r, :, part], preferred_element_type=f32)
+            for c in range(GC):
+                i = r * GC + c
+                scores = all_scores[c * 64 : (c + 1) * 64]
+                top = jnp.max(scores, axis=0, keepdims=True)
+                weights = jnp.exp(scores - top)
+                max_ref[i : i + 1, part] = top
+                sum_ref[i : i + 1, part] = jnp.sum(weights, axis=0, keepdims=True)
+                mom_ref[i : i + 1, part] = jnp.sum(weights * signed, axis=0, keepdims=True)
 
     lane = lax.broadcasted_iota(jnp.int32, (PATCHES, 128), 1)
     left = lane < 64
@@ -153,26 +208,28 @@
 
 def measure(offsets, gaps, images, prior, low, high):
     sections = images.shape[0]
-    stacked = sections + 2
+    rows_x = (sections + 2) * 32 + 32
     cols, rows, back_k, back_l = make_constants()
     smem = pl.BlockSpec(memory_space=pltpu.SMEM)
     vmem = pl.BlockSpec(memory_space=pltpu.VMEM)
     bf16 = jnp.bfloat16
+    f32 = jnp.float32
     return pl.pallas_call(
         patch_kernel,
-        out_shape=jax.ShapeDtypeStruct((2 * PATCHES, sections), jnp.float32),
+        out_shape=jax.ShapeDtypeStruct((2 * PATCHES, sections), f32),
         in_specs=[smem, smem] + [vmem] * 8,
         out_specs=vmem,
         scratch_shapes=[
-            pltpu.VMEM((GR, GC * 128, 256), bf16),
-            pltpu.VMEM((PATCHES, stacked * 64, 2 * WIN), bf16),
+            pltpu.VMEM((GR, 256 + GC * 16, 256), bf16),
+            pltpu.VMEM((PATCHES, rows_x, 2 * WIN), bf16),
             pltpu.VMEM((PATCHES, 2 * WIN, 256), bf16),
-            pltpu.VMEM((stacked * 64, 256), bf16),
-            pltpu.VMEM((sections * 32, 512), bf16),
-            pltpu.VMEM((128, sections * 64), bf16),
-            pltpu.VMEM((PATCHES, sections * 64), jnp.float32),
-            pltpu.VMEM((PATCHES, sections * 64), jnp.float32),
-            pltpu.VMEM((PATCHES, sections * 64), jnp.float32),
+            pltpu.VMEM((PATCHES, rows_x, 256), bf16),
+            pltpu.VMEM((PATCHES, 24, 256), f32),
+            pltpu.VMEM((PATCHES * (sections * 16 + 16), 256), bf16),
+            pltpu.VMEM((GR, 256, sections * 64), bf16),
+            pltpu.VMEM((PATCHES, sections * 64), f32),
+            pltpu.VMEM((PATCHES, sections * 64), f32),
+            pltpu.VMEM((PATCHES, sections * 64), f32),
         ],
         compiler_params=pltpu.CompilerParams(vmem_limit_bytes=48 * 1024 * 1024),
     )(offsets, gaps, images, prior, low, high, cols, rows, back_k, back_l)
@@ -183,6 +240,15 @@
     widened = jnp.pad(middle, ((0, 0), (0, 0), (1, 1), (0, 0)))
     beside = extended[:, :-2] + extended[:, 2:] + widened[:, :, :-2] + widened[:, :, 2:]
     return 0.5 * middle + 0.125 * beside
+
+
+def earlier_groups(total):
+    place = lax.axis_index("gz")
+    count = lax.axis_size("gz")
+    other = lax.ppermute(total, "gz", [(i, i ^ 1) for i in range(count)])
+    pair = total + other
+    before = lax.ppermute(pair, "gz", [(i, i + 2) for i in range(count - 2)])
+    return before + jnp.where(place % 2 == 1, other, 0.0)
 
 
 def local(images, offsets, gaps):
@@ -204,9 +270,7 @@
     wide = jnp.where(inside[None, :, None, None], wide, 0.0)
     smoothed = relaxed_step(wide).transpose(0, 3, 1, 2)
     running = jnp.cumsum(smoothed, axis=1)
-    gathered = lax.all_gather(running[:, sections - 1], "gz")
-    earlier = jnp.arange(gathered.shape[0]) < lax.axis_index("gz")
-    earlier_sum = jnp.sum(jnp.where(earlier[:, None, None, None], gathered, 0.0), axis=0)
+    earlier_sum = earlier_groups(running[:, sections - 1])
     return smoothed, running + earlier_sum[:, None]
 
 

time: 58.7 us -> 52.2 us (0.89)
  the two profiles are of different devices: /device:TPU:25 before, /device:TPU:24 now
where the time goes in v2:
time: 52.2 us; the launch traced here: 51.9 us
  starting transfers between devices  26.2 us (50%)
  waiting for transfers between devices  17 us (33%)
  Pallas kernels  4.28 us (8%)
  local copies, waits for them, and re-layouts  3.44 us (7%)
  between operations  0.85 us (2%)
    ppermute x5, starting transfers between devices, shifted(): lax.ppermute(value, axis, [(source, source + steps) for source in range(i...  24.8 us
    ppermute x5, waiting for transfers between devices, shifted(): lax.ppermute(value, axis, [(source, source + steps) for source in range(i...  10.2 us
    ppermute x1, waiting for transfers between devices, earlier_groups(): before = lax.ppermute(pair, 'gz', [(i, i + 2) for i in range(count - 2)])  5.68 us
    pallas_call x1, Pallas kernels, measure(): pl.pallas_call(patch_kernel, out_shape=jax.ShapeDtypeStruct((2 * PATCHES,...  4.28 us
    unnamed x18, local copies, waits for them, and re-layouts  1.32 us
    ppermute x1, starting transfers between devices, earlier_groups(): before = lax.ppermute(pair, 'gz', [(i, i + 2) for i in range(count - 2)])  1.28 us
    ppermute x1, waiting for transfers between devices, earlier_groups(): other = lax.ppermute(total, 'gz', [(i, i ^ 1) for i in range(count)])  1.14 us
    slice x2, local copies, waits for them, and re-layouts, local(): top = jnp.concatenate([prior[:, :HALF], images[:, :HALF]], 0)  1.08 us
  transfers between devices with their start and end apart: 7, of which 6 were waited for; matrix products, arithmetic and copies ran while one was open for 2% of the time, Pallas kernels for 0%

profile of v2, /device:TPU:24, one launch (start us, length us, event | category | flops | bytes accessed | tf_op | source)
XLA Modules:
  0.0 51.9 jit_solution(107320393786094315)
XLA Ops:
  0.6 0.9 %slice.46 = bf16[2,128,256]{2,1,0:T(8,128)(2,1)S(1)} slice(bf16[16,128,256]{2,1,0:T(8,128)(2,1)} %own_ref.1), slice={[14:16], [0:128], [0:256]} | slice | bytes 262144 | tf_op jit(solution)/shard_map/slice | solution.py:257
  1.5 0.0 copy-start
  1.6 2.1 %collective-permute-start = (bf16[2,128,256]{2,1,0:T(8,128)(2,1)S(1)}, bf16[2,128,256]{2,1,0:T(8,128)(2,1)S(1)}, u32[]{:S(2)}, u32[]{:S(2)}) collective-permute-start(bf16[2,128,256]{2,1,0:T(8,128)(2,1)S(1)} %slice.46), channel_id=1, source_target_pairs={{0,64},{64,128},{128,192},{1,65},{65,129},{129,193},{2,66},{66,130... | collective-permute-start | bytes 393224 | tf_op jit(solution)/shard_map/ppermute | solution.py:24
  3.6 1.1 %fusion.11 = (bf16[16,32,256]{2,1,0:T(8,128)(2,1)S(1)}, bf16[16,32,256]{2,1,0:T(8,128)(2,1)S(1)}) fusion(bf16[16,128,256]{2,1,0:T(8,128)(2,1)} %own_ref.1), kind=kLoop, calls=%fused_computation.25 | loop fusion | bytes 1048576 | tf_op jit(solution)/shard_map/slice | solution.py:258
  4.7 4.8 %collective-permute-done.prior_ref = bf16[2,128,256]{2,1,0:T(8,128)(2,1)S(1)} collective-permute-done((bf16[2,128,256]{2,1,0:T(8,128)(2,1)S(1)}, bf16[2,128,256]{2,1,0:T(8,128)(2,1)S(1)}, u32[]{:S(2)}, u32[]{:S(2)}) %collective-permute-start) | collective-permute-done | bytes 131104 | tf_op jit(solution)/shard_map/ppermute | solution.py:24
  9.5 3.4 %collective-permute-start.1 = (bf16[18,32,256]{2,1,0:T(8,128)(2,1)S(1)}, bf16[18,32,256]{2,1,0:T(8,128)(2,1)S(1)}, u32[]{:S(2)}, u32[]{:S(2)}) collective-permute-start(bf16[18,32,256]{2,1,0:T(8,128)(2,1)S(1)} %pad_maximum_fusion), channel_id=1, source_target_pairs={{0,1},{1,2},{2,3},{3,4},{4,5},{5,6},{6,7},{7,8},{8,9},{9,10},{10,1... | collective-permute-start | bytes 884744 | tf_op jit(solution)/shard_map/ppermute | solution.py:24
  12.9 0.0 copy-start.1
  13.0 0.0 copy-start.2
  13.0 0.0 copy-start.3
  13.0 0.0 copy-start.4
  13.0 8.8 %collective-permute-start.2 = (bf16[18,32,256]{2,1,0:T(8,128)(2,1)S(1)}, bf16[18,32,256]{2,1,0:T(8,128)(2,1)S(1)}, u32[]{:S(2)}, u32[]{:S(2)}) collective-permute-start(bf16[18,32,256]{2,1,0:T(8,128)(2,1)S(1)} %pad_maximum_fusion.1), channel_id=1, source_target_pairs={{1,0},{2,1},{3,2},{4,3},{5,4},{6,5},{7,6},{8,7},{9,8},{10,9},{11,1... | collective-permute-start | bytes 884744 | tf_op jit(solution)/shard_map/ppermute | solution.py:24
  21.8 0.0 copy-done.7
  21.8 0.1 copy.9.off_ref
  21.9 2.4 %collective-permute-done.1.low_ref = bf16[18,32,256]{2,1,0:T(8,128)(2,1)S(1)} collective-permute-done((bf16[18,32,256]{2,1,0:T(8,128)(2,1)S(1)}, bf16[18,32,256]{2,1,0:T(8,128)(2,1)S(1)}, u32[]{:S(2)}, u32[]{:S(2)}) %collective-permute-start.1) | collective-permute-done | bytes 294944 | tf_op jit(solution)/shard_map/ppermute | solution.py:24
  24.4 1.7 %collective-permute-done.2.high_ref = bf16[18,32,256]{2,1,0:T(8,128)(2,1)S(1)} collective-permute-done((bf16[18,32,256]{2,1,0:T(8,128)(2,1)S(1)}, bf16[18,32,256]{2,1,0:T(8,128)(2,1)S(1)}, u32[]{:S(2)}, u32[]{:S(2)}) %collective-permute-start.2) | collective-permute-done | bytes 294944 | tf_op jit(solution)/shard_map/ppermute | solution.py:24
  26.0 0.0 copy-done
  26.1 0.0 copy-done.4
  26.1 0.0 copy-done.5
  26.1 4.3 %shard_map.86 = f32[16,16]{1,0:T(8,128)S(1)} custom-call(s32[2,4,2]{2,1,0:T(4,128)S(1)} %copy.9.off_ref, s32[16]{0:T(128)S(1)} %copy-done.5, bf16[16,128,256]{2,1,0:T(8,128)(2,1)S(1)} %copy-done, bf16[2,128,256]{2,1,0:T(8,128)(2,1)S(1)} %collective-permute-done.prior_ref, bf16[18,32,256]{2,1,0:T(8,128)(2,1)S(1)} %collective-permute-done.1.low_ref, ...), custom_call_target="tpu_custom_call" | custom-call | tf_op jit(solution)/shard_map/pallas_call | solution.py:217
  30.4 1.9 %collective-permute-start.3 = (f32[16,16]{1,0:T(8,128)S(1)}, f32[16,16]{1,0:T(8,128)S(1)}, u32[]{:S(2)}, u32[]{:S(2)}) collective-permute-start(f32[16,16]{1,0:T(8,128)S(1)} %shard_map.86), channel_id=1, source_target_pairs={{0,1},{1,2},{2,3},{3,4},{4,5},{5,6},{6,7},{7,8},{8,9},{9,10},{10,1... | collective-permute-start | bytes 3080 | tf_op jit(solution)/shard_map/ppermute | solution.py:24
  32.3 8.6 %collective-permute-start.4 = (f32[16,16]{1,0:T(8,128)S(1)}, f32[16,16]{1,0:T(8,128)S(1)}, u32[]{:S(2)}, u32[]{:S(2)}) collective-permute-start(f32[16,16]{1,0:T(8,128)S(1)} %shard_map.86), channel_id=1, source_target_pairs={{1,0},{2,1},{3,2},{4,3},{5,4},{6,5},{7,6},{8,7},{9,8},{10,9},{11,1... | collective-permute-start | bytes 3080 | tf_op jit(solution)/shard_map/ppermute | solution.py:24
  40.9 0.0 collective-permute-done.3
  41.0 1.3 %collective-permute-done.4 = f32[16,16]{1,0:T(8,128)S(1)} collective-permute-done((f32[16,16]{1,0:T(8,128)S(1)}, f32[16,16]{1,0:T(8,128)S(1)}, u32[]{:S(2)}, u32[]{:S(2)}) %collective-permute-start.4) | collective-permute-done | bytes 1056 | tf_op jit(solution)/shard_map/ppermute | solution.py:24
  42.3 0.1 fusion.4
  42.4 0.0 copy-start.6
  42.4 0.1 copy.10
  42.5 0.5 copy-done.6
  43.0 0.1 collective-permute-start.5
  43.1 1.1 %collective-permute-done.5 = f32[2,2,4]{2,1,0:T(2,128)S(1)} collective-permute-done((f32[2,2,4]{2,1,0:T(2,128)S(1)}, f32[2,2,4]{2,1,0:T(2,128)S(1)}, u32[]{:S(2)}, u32[]{:S(2)}) %collective-permute-start.5) | collective-permute-done | bytes 96 | tf_op jit(solution)/shard_map/ppermute | solution.py:248
  44.3 1.3 %collective-permute-start.6 = (f32[2,2,4]{2,1,0:T(2,128)S(1)}, f32[2,2,4]{2,1,0:T(2,128)S(1)}, u32[]{:S(2)}, u32[]{:S(2)}) collective-permute-start(f32[2,2,4]{2,1,0:T(2,128)S(1)} %fusion.10), channel_id=1, source_target_pairs={{0,128},{64,192},{1,129},{65,193},{2,130},{66,194},{3,131},{67,195... | collective-permute-start | bytes 200 | tf_op jit(solution)/shard_map/ppermute | solution.py:250
  45.5 5.7 %collective-permute-done.6 = f32[2,2,4]{2,1,0:T(2,128)S(1)} collective-permute-done((f32[2,2,4]{2,1,0:T(2,128)S(1)}, f32[2,2,4]{2,1,0:T(2,128)S(1)}, u32[]{:S(2)}, u32[]{:S(2)}) %collective-permute-start.6) | collective-permute-done | bytes 96 | tf_op jit(solution)/shard_map/ppermute | solution.py:250
  51.2 0.7 %copy.11 = f32[2,16,2,4]{1,3,2,0:T(4,128)} copy(f32[2,16,2,4]{3,2,1,0:T(2,128)S(1)} %broadcast_add_fusion) | data formatting | bytes 2048
  (17 shorter events, 0.2 us)
Async XLA Ops:
  1.5 24.5 %copy-start = (bf16[16,128,256]{2,1,0:T(8,128)(2,1)S(1)}, bf16[16,128,256]{2,1,0:T(8,128)(2,1)}, u32[]{:S(2)}) copy-start(bf16[16,128,256]{2,1,0:T(8,128)(2,1)} %own_ref.1) | copy-start | bytes 3145732
  1.6 7.9 %collective-permute-start = (bf16[2,128,256]{2,1,0:T(8,128)(2,1)S(1)}, bf16[2,128,256]{2,1,0:T(8,128)(2,1)S(1)}, u32[]{:S(2)}, u32[]{:S(2)}) collective-permute-start(bf16[2,128,256]{2,1,0:T(8,128)(2,1)S(1)} %slice.46), channel_id=1, source_target_pairs={{0,64},{64,128},{128,192},{1,65},{65,129},{129,193},{2,66},{66,130... | collective-permute-start | bytes 393224 | tf_op jit(solution)/shard_map/ppermute | solution.py:24
  9.5 12.3 %copy-start.7 = (s32[2,4,2]{1,2,0:T(2,128)S(1)}, s32[2,4,2]{1,2,0:T(2,128)}, u32[]{:S(2)}) copy-start(s32[2,4,2]{1,2,0:T(2,128)} %param.8) | copy-start | bytes 196
  9.5 14.8 %collective-permute-start.1 = (bf16[18,32,256]{2,1,0:T(8,128)(2,1)S(1)}, bf16[18,32,256]{2,1,0:T(8,128)(2,1)S(1)}, u32[]{:S(2)}, u32[]{:S(2)}) collective-permute-start(bf16[18,32,256]{2,1,0:T(8,128)(2,1)S(1)} %pad_maximum_fusion), channel_id=1, source_target_pairs={{0,1},{1,2},{2,3},{3,4},{4,5},{5,6},{6,7},{7,8},{8,9},{9,10},{10,1... | collective-permute-start | bytes 884744 | tf_op jit(solution)/shard_map/ppermute | solution.py:24
  12.9 13.1 %copy-start.1 = (f32[2,128,256]{2,1,0:T(8,128)S(1)}, f32[2,128,256]{2,1,0:T(8,128)}, u32[]{:S(2)}) copy-start(f32[2,128,256]{2,1,0:T(8,128)} %constant.50.clone.rows_ref) | copy-start | bytes 786436
  13.0 13.1 %copy-start.2 = (bf16[256,256]{1,0:T(8,128)(2,1)S(1)}, bf16[256,256]{1,0:T(8,128)(2,1)}, u32[]{:S(2)}) copy-start(bf16[256,256]{1,0:T(8,128)(2,1)} %constant.51.clone.back_k_ref) | copy-start | bytes 393220
  13.0 13.1 %copy-start.3 = (bf16[256,256]{1,0:T(8,128)(2,1)S(1)}, bf16[256,256]{1,0:T(8,128)(2,1)}, u32[]{:S(2)}) copy-start(bf16[256,256]{1,0:T(8,128)(2,1)} %constant.52.clone.back_l_ref) | copy-start | bytes 393220
  13.0 13.1 %copy-start.4 = (f32[72,256]{1,0:T(8,128)S(1)}, f32[72,256]{1,0:T(8,128)}, u32[]{:S(2)}) copy-start(f32[72,256]{1,0:T(8,128)} %constant.49.clone.cols_ref) | copy-start | bytes 221188
  13.0 13.0 %collective-permute-start.2 = (bf16[18,32,256]{2,1,0:T(8,128)(2,1)S(1)}, bf16[18,32,256]{2,1,0:T(8,128)(2,1)S(1)}, u32[]{:S(2)}, u32[]{:S(2)}) collective-permute-start(bf16[18,32,256]{2,1,0:T(8,128)(2,1)S(1)} %pad_maximum_fusion.1), channel_id=1, source_target_pairs={{1,0},{2,1},{3,2},{4,3},{5,4},{6,5},{7,6},{8,7},{9,8},{10,9},{11,1... | collective-permute-start | bytes 884744 | tf_op jit(solution)/shard_map/ppermute | solution.py:24
  21.9 4.1 %copy-start.5 = (s32[16]{0:T(128)S(1)}, s32[16]{0:T(128)}, u32[]{:S(2)}) copy-start(s32[16]{0:T(128)} %gap_ref.1) | copy-start | bytes 196
  30.4 10.6 %collective-permute-start.3 = (f32[16,16]{1,0:T(8,128)S(1)}, f32[16,16]{1,0:T(8,128)S(1)}, u32[]{:S(2)}, u32[]{:S(2)}) collective-permute-start(f32[16,16]{1,0:T(8,128)S(1)} %shard_map.86), channel_id=1, source_target_pairs={{0,1},{1,2},{2,3},{3,4},{4,5},{5,6},{6,7},{7,8},{8,9},{9,10},{10,1... | collective-permute-start | bytes 3080 | tf_op jit(solution)/shard_map/ppermute | solution.py:24
  32.3 10.0 %collective-permute-start.4 = (f32[16,16]{1,0:T(8,128)S(1)}, f32[16,16]{1,0:T(8,128)S(1)}, u32[]{:S(2)}, u32[]{:S(2)}) collective-permute-start(f32[16,16]{1,0:T(8,128)S(1)} %shard_map.86), channel_id=1, source_target_pairs={{1,0},{2,1},{3,2},{4,3},{5,4},{6,5},{7,6},{8,7},{9,8},{10,9},{11,1... | collective-permute-start | bytes 3080 | tf_op jit(solution)/shard_map/ppermute | solution.py:24
  42.4 0.6 %copy-start.6 = (f32[2,16,2,4]{1,3,2,0:T(4,128)}, f32[2,16,2,4]{1,3,2,0:T(4,128)S(1)}, u32[]{:S(2)}) copy-start(f32[2,16,2,4]{1,3,2,0:T(4,128)S(1)} %fusion.9) | copy-start | bytes 3076
  43.0 1.2 %collective-permute-start.5 = (f32[2,2,4]{2,1,0:T(2,128)S(1)}, f32[2,2,4]{2,1,0:T(2,128)S(1)}, u32[]{:S(2)}, u32[]{:S(2)}) collective-permute-start(f32[2,2,4]{2,1,0:T(2,128)S(1)} %slice_bitcast_fusion), channel_id=1, source_target_pairs={{0,64},{64,0},{128,192},{192,128},{1,65},{65,1},{129,193},{193,129... | collective-permute-start | bytes 200 | tf_op jit(solution)/shard_map/ppermute | solution.py:248
  44.3 7.0 %collective-permute-start.6 = (f32[2,2,4]{2,1,0:T(2,128)S(1)}, f32[2,2,4]{2,1,0:T(2,128)S(1)}, u32[]{:S(2)}, u32[]{:S(2)}) collective-permute-start(f32[2,2,4]{2,1,0:T(2,128)S(1)} %fusion.10), channel_id=1, source_target_pairs={{0,128},{64,192},{1,129},{65,193},{2,130},{66,194},{3,131},{67,195... | collective-permute-start | bytes 200 | tf_op jit(solution)/shard_map/ppermute | solution.py:250

commit v3 on v2

--- a/solution.py
+++ b/solution.py
@@ -18,10 +18,9 @@
 PATCHES = GR * GC
 
 
-def shifted(value, axis, steps):
+def ring(value, axis, steps):
     count = lax.axis_size(axis)
-    initial, last = (max(0, -steps), min(count, count - steps))
-    return lax.ppermute(value, axis, [(source, source + steps) for source in range(initial, last)])
+    return lax.ppermute(value, axis, [(source, (source + steps) % count) for source in range(count)])
 
 
 def tables():
@@ -63,17 +62,15 @@
     return cols, rows, back_k.astype(bf), back_l.astype(bf)
 
 
-def patch_kernel(
-    off_ref, gap_ref, own_ref, prior_ref, low_ref, high_ref, cols_ref, rows_ref, back_k_ref, back_l_ref,
-    out_ref, m_ref, x_ref, w_ref, z_ref, n_ref, y_ref, g_ref, max_ref, sum_ref, mom_ref,
-):
-    sections = own_ref.shape[0]
-    stacked = sections + 2
-    f32 = jnp.float32
+def table_kernel(off_ref, edge_ref, cols_ref, rows_ref, m_ref, w_ref):
     bf16 = jnp.bfloat16
-    main = stacked * 32
     lane = lax.broadcasted_iota(jnp.int32, cols_ref.shape, 1)
+    line = lax.broadcasted_iota(jnp.int32, (WIN, 256), 0)
     for r in range(GR):
+        if r == 0:
+            inside_image = line >= jnp.where(edge_ref[0] == 1, HALF, 0)
+        else:
+            inside_image = line < jnp.where(edge_ref[1] == 1, WIN - HALF, WIN)
         for c in range(GC):
             i = r * GC + c
             row_at = off_ref[r, c, 0]
@@ -85,13 +82,26 @@
             m_ref[r, c * 64 : (c + 1) * 64, :] = turned[:64].astype(bf16)
             m_ref[r, 256 + c * 16 : 256 + (c + 1) * 16, :] = jnp.concatenate([turned[64:]] * 2, 0).astype(bf16)
             for half in range(2):
-                w_ref[i, half * WIN : (half + 1) * WIN, :] = pltpu.roll(rows_ref[half], row_at, 0).astype(bf16)
+                turned = pltpu.roll(rows_ref[half], row_at, 0)
+                w_ref[i, half * WIN : (half + 1) * WIN, :] = jnp.where(inside_image, turned, 0.0).astype(bf16)
+
+
+def patch_kernel(
+    edge_ref, gap_ref, own_ref, prior_ref, low_ref, high_ref, plow_ref, phigh_ref, m_ref, w_ref, back_k_ref, back_l_ref,
+    out_ref, x_ref, z_ref, n_ref, y_ref, g_ref, max_ref, sum_ref, mom_ref,
+):
+    sections = own_ref.shape[0]
+    stacked = sections + 2
+    f32 = jnp.float32
+    bf16 = jnp.bfloat16
+    main = stacked * 32
+    has_prior = jnp.where(edge_ref[2] == 1, 0.0, 1.0)
 
     def window(r, t):
         image = prior_ref.at[t] if t < 2 else own_ref.at[t - 2]
         if r == 0:
-            return [low_ref[t], image[: WIN - HALF]]
-        return [image[HALF:], high_ref[t]]
+            return [plow_ref[t] if t < 2 else low_ref[t - 2], image[: WIN - HALF]]
+        return [image[HALF:], phigh_ref[t] if t < 2 else high_ref[t - 2]]
 
     sub = lax.broadcasted_iota(jnp.int32, (8, WIN), 0)
     for r in range(GR):
@@ -99,6 +109,8 @@
         for pair in range(stacked // 2):
             both = jnp.concatenate(window(r, 2 * pair) + window(r, 2 * pair + 1), 0)
             first = lax.dot_general(m_ref[r], both, (((1,), (1,)), ((), ())), preferred_element_type=f32)
+            if pair == 0:
+                first = first * has_prior
             for c in range(GC):
                 for k in range(2):
                     t = 2 * pair + k
@@ -206,10 +218,29 @@
     out_ref[PATCHES:, :] = cols_out
 
 
-def measure(offsets, gaps, images, prior, low, high):
+def make_tables(offsets, edges):
+    cols, rows, _, _ = make_constants()
+    smem = pl.BlockSpec(memory_space=pltpu.SMEM)
+    vmem = pl.BlockSpec(memory_space=pltpu.VMEM)
+    bf16 = jnp.bfloat16
+    return pl.pallas_call(
+        table_kernel,
+        out_shape=(
+            jax.ShapeDtypeStruct((GR, 256 + GC * 16, 256), bf16),
+            jax.ShapeDtypeStruct((PATCHES, 2 * WIN, 256), bf16),
+        ),
+        in_specs=[smem, smem, vmem, vmem],
+        out_specs=(vmem, vmem),
+        compiler_params=pltpu.CompilerParams(vmem_limit_bytes=16 * 1024 * 1024),
+        cost_estimate=pl.CostEstimate(flops=4_000_000, bytes_accessed=4_000_000, transcendentals=0),
+        name="make_tables",
+    )(offsets, edges, cols, rows)
+
+
+def measure(edges, gaps, images, prior, low, high, plow, phigh, m_table, w_table):
     sections = images.shape[0]
     rows_x = (sections + 2) * 32 + 32
-    cols, rows, back_k, back_l = make_constants()
+    _, _, back_k, back_l = make_constants()
     smem = pl.BlockSpec(memory_space=pltpu.SMEM)
     vmem = pl.BlockSpec(memory_space=pltpu.VMEM)
     bf16 = jnp.bfloat16
@@ -217,12 +248,10 @@
     return pl.pallas_call(
         patch_kernel,
         out_shape=jax.ShapeDtypeStruct((2 * PATCHES, sections), f32),
-        in_specs=[smem, smem] + [vmem] * 8,
+        in_specs=[smem, smem] + [vmem] * 10,
         out_specs=vmem,
         scratch_shapes=[
-            pltpu.VMEM((GR, 256 + GC * 16, 256), bf16),
             pltpu.VMEM((PATCHES, rows_x, 2 * WIN), bf16),
-            pltpu.VMEM((PATCHES, 2 * WIN, 256), bf16),
             pltpu.VMEM((PATCHES, rows_x, 256), bf16),
             pltpu.VMEM((PATCHES, 24, 256), f32),
             pltpu.VMEM((PATCHES * (sections * 16 + 16), 256), bf16),
@@ -231,8 +260,10 @@
             pltpu.VMEM((PATCHES, sections * 64), f32),
             pltpu.VMEM((PATCHES, sections * 64), f32),
         ],
-        compiler_params=pltpu.CompilerParams(vmem_limit_bytes=48 * 1024 * 1024),
-    )(offsets, gaps, images, prior, low, high, cols, rows, back_k, back_l)
+        compiler_params=pltpu.CompilerParams(vmem_limit_bytes=32 * 1024 * 1024),
+        cost_estimate=pl.CostEstimate(flops=2_000_000_000, bytes_accessed=6_000_000, transcendentals=600_000),
+        name="measure",
+    )(edges, gaps, images, prior, low, high, plow, phigh, m_table, w_table, back_k, back_l)
 
 
 def relaxed_step(extended):
@@ -247,26 +278,29 @@
     count = lax.axis_size("gz")
     other = lax.ppermute(total, "gz", [(i, i ^ 1) for i in range(count)])
     pair = total + other
-    before = lax.ppermute(pair, "gz", [(i, i + 2) for i in range(count - 2)])
-    return before + jnp.where(place % 2 == 1, other, 0.0)
+    across = lax.ppermute(pair, "gz", [(i, (i + 2) % count) for i in range(count)])
+    return jnp.where(place >= 2, across, 0.0) + jnp.where(place % 2 == 1, other, 0.0)
 
 
 def local(images, offsets, gaps):
     sections = images.shape[0]
     rows_here = images.shape[1]
-    prior = shifted(images[sections - 2 :], "gz", 1)
-    top = jnp.concatenate([prior[:, :HALF], images[:, :HALF]], 0)
-    bottom = jnp.concatenate([prior[:, rows_here - HALF :], images[:, rows_here - HALF :]], 0)
-    low = shifted(bottom, "xy", 1)
-    high = shifted(top, "xy", -1)
-    measured = measure(offsets, gaps, images, prior, low, high)
-    above = shifted(measured, "xy", 1).reshape(2, GR, GC, sections)
-    below = shifted(measured, "xy", -1).reshape(2, GR, GC, sections)
+    place = lax.axis_index("xy")
+    last = lax.axis_size("xy") - 1
+    edges = jnp.stack([place == 0, place == last, lax.axis_index("gz") == 0]).astype(jnp.int32)
+    m_table, w_table = make_tables(offsets, edges)
+    prior = ring(images[sections - 2 :], "gz", 1)
+    low = ring(images[:, rows_here - HALF :], "xy", 1)
+    high = ring(images[:, :HALF], "xy", -1)
+    plow = ring(prior[:, rows_here - HALF :], "xy", 1)
+    phigh = ring(prior[:, :HALF], "xy", -1)
+    measured = measure(edges, gaps, images, prior, low, high, plow, phigh, m_table, w_table)
+    above = jnp.where(place == 0, 0.0, ring(measured, "xy", 1)).reshape(2, GR, GC, sections)
+    below = jnp.where(place == last, 0.0, ring(measured, "xy", -1)).reshape(2, GR, GC, sections)
     measured = measured.reshape(2, GR, GC, sections)
     wide = relaxed_step(jnp.concatenate([above, measured, below], 1))
-    place = lax.axis_index("xy")
     row = place * GR + jnp.arange(-1, GR + 1)
-    inside = (row >= 0) & (row < GR * lax.axis_size("xy"))
+    inside = (row >= 0) & (row < GR * (last + 1))
     wide = jnp.where(inside[None, :, None, None], wide, 0.0)
     smoothed = relaxed_step(wide).transpose(0, 3, 1, 2)
     running = jnp.cumsum(smoothed, axis=1)

time: 52.2 us -> 47.2 us (0.904)
  the two profiles are of different devices: /device:TPU:24 before, /device:TPU:1 now
where the time goes in v3:
time: 47.2 us; the launch traced here: 47 us
  starting transfers between devices  26.7 us (57%)
  waiting for transfers between devices  8.75 us (19%)
  Pallas kernels  5.82 us (12%)
  local copies, waits for them, and re-layouts  4.76 us (10%)
  between operations  0.78 us (2%)
    ppermute x7, starting transfers between devices, ring(): lax.ppermute(value, axis, [(source, (source + steps) % count) for source...  22.6 us
    ppermute x7, waiting for transfers between devices, ring(): lax.ppermute(value, axis, [(source, (source + steps) % count) for source...  6.72 us
    pallas_call x1, Pallas kernels, measure(): pl.pallas_call(patch_kernel, out_shape=jax.ShapeDtypeStruct((2 * PATCHES,...  3.99 us
    ppermute x1, starting transfers between devices, earlier_groups(): lax.ppermute(pair, 'gz', [(i, (i + 2) % count) for i in range(count)])  2.73 us
    unnamed x18, local copies, waits for them, and re-layouts  2.53 us
    pallas_call x1, Pallas kernels, make_tables(): pl.pallas_call(table_kernel, out_shape=(jax.ShapeDtypeStruct((GR, 256 + G...  1.83 us
    ppermute x1, starting transfers between devices, earlier_groups(): other = lax.ppermute(total, 'gz', [(i, i ^ 1) for i in range(count)])  1.38 us
    ppermute x1, waiting for transfers between devices, earlier_groups(): lax.ppermute(pair, 'gz', [(i, (i + 2) % count) for i in range(count)])  1.21 us
  transfers between devices with their start and end apart: 9, of which 4 were waited for; matrix products, arithmetic and copies ran while one was open for 3% of the time, Pallas kernels for 4%

profile of v3, /device:TPU:1, one launch (start us, length us, event | category | flops | bytes accessed | tf_op | source)
XLA Modules:
  0.0 47.0 jit_solution(5344541513695446556)
XLA Ops:
  0.6 0.0 copy-start
  0.6 1.0 %slice.46 = bf16[2,128,256]{2,1,0:T(8,128)(2,1)S(1)} slice(bf16[16,128,256]{2,1,0:T(8,128)(2,1)} %own_ref.1), slice={[14:16], [0:128], [0:256]} | slice | bytes 262144 | tf_op jit(solution)/shard_map/slice | solution.py:292
  1.6 4.4 %collective-permute-start = (bf16[2,128,256]{2,1,0:T(8,128)(2,1)S(1)}, bf16[2,128,256]{2,1,0:T(8,128)(2,1)S(1)}, u32[]{:S(2)}, u32[]{:S(2)}) collective-permute-start(bf16[2,128,256]{2,1,0:T(8,128)(2,1)S(1)} %slice.46), channel_id=1, source_target_pairs={{0,64},{64,128},{128,192},{192,0},{1,65},{65,129},{129,193},{193,1... | collective-permute-start | bytes 393224 | tf_op jit(solution)/shard_map/ppermute | solution.py:23
  6.0 1.1 %fusion.11 = (bf16[16,32,256]{2,1,0:T(8,128)(2,1)S(1)}, bf16[16,32,256]{2,1,0:T(8,128)(2,1)S(1)}) fusion(bf16[16,128,256]{2,1,0:T(8,128)(2,1)} %own_ref.1), kind=kLoop, calls=%fused_computation.26 | loop fusion | bytes 1048576 | tf_op jit(solution)/shard_map/slice | solution.py:294
  7.1 1.3 %collective-permute-start.1 = (bf16[16,32,256]{2,1,0:T(8,128)(2,1)S(1)}, bf16[16,32,256]{2,1,0:T(8,128)(2,1)S(1)}, u32[]{:S(2)}, u32[]{:S(2)}) collective-permute-start(bf16[16,32,256]{2,1,0:T(8,128)(2,1)S(1)} %get-tuple-element.9), channel_id=1, source_target_pairs={{0,1},{1,2},{2,3},{3,4},{4,5},{5,6},{6,7},{7,8},{8,9},{9,10},{10,1... | collective-permute-start | bytes 786440 | tf_op jit(solution)/shard_map/ppermute | solution.py:23
  8.4 6.8 %collective-permute-start.2 = (bf16[16,32,256]{2,1,0:T(8,128)(2,1)S(1)}, bf16[16,32,256]{2,1,0:T(8,128)(2,1)S(1)}, u32[]{:S(2)}, u32[]{:S(2)}) collective-permute-start(bf16[16,32,256]{2,1,0:T(8,128)(2,1)S(1)} %get-tuple-element.8), channel_id=1, source_target_pairs={{0,63},{1,0},{2,1},{3,2},{4,3},{5,4},{6,5},{7,6},{8,7},{9,8},{10,9... | collective-permute-start | bytes 786440 | tf_op jit(solution)/shard_map/ppermute | solution.py:23
  15.2 0.0 collective-permute-done.prior_ref
  15.2 0.1 collective-permute-start.3
  15.3 5.7 %collective-permute-start.4 = (bf16[2,32,256]{2,1,0:T(8,128)(2,1)S(1)}, bf16[2,32,256]{2,1,0:T(8,128)(2,1)S(1)}, u32[]{:S(2)}, u32[]{:S(2)}) collective-permute-start(bf16[2,32,256]{2,1,0:T(8,128)(2,1)S(1)} %get-tuple-element.10), channel_id=1, source_target_pairs={{0,63},{1,0},{2,1},{3,2},{4,3},{5,4},{6,5},{7,6},{8,7},{9,8},{10,9... | collective-permute-start | bytes 98312 | tf_op jit(solution)/shard_map/ppermute | solution.py:23
  21.0 0.1 add_convert_fusion.edge_ref
  21.0 0.6 %copy-done.7 = s32[2,4,2]{1,2,0:T(2,128)S(1)} copy-done((s32[2,4,2]{1,2,0:T(2,128)S(1)}, s32[2,4,2]{1,2,0:T(2,128)}, u32[]{:S(2)}) %copy-start.7) | copy-done | bytes 88
  21.7 0.1 copy.9.off_ref
  21.8 0.0 copy-start.5
  21.8 1.8 %make_tables.1 = (bf16[2,320,256]{2,1,0:T(8,128)(2,1)S(1)}, bf16[8,256,256]{2,1,0:T(8,128)(2,1)S(1)}) custom-call(s32[2,4,2]{2,1,0:T(4,128)S(1)} %copy.9.off_ref, s32[3]{0:T(128)S(1)} %add_convert_fusion.edge_ref, f32[72,256]{1,0:T(8,128)S(1)} %copy-done.2, f32[2,128,256]{2,1,0:T(8,128)S(1)} %copy-done.1), custom_call_target="tpu_custom_call" | custom-call | flops 4000000 | bytes 4000000 | tf_op jit(solution)/shard_map/make_tables/pallas_call | solution.py:226
  23.6 0.0 collective-permute-done.4.phigh_ref
  23.6 0.0 collective-permute-done.1.low_ref
  23.6 0.0 copy-start.3
  23.7 0.6 %copy-done.3 = s32[16]{0:T(128)S(1)} copy-done((s32[16]{0:T(128)S(1)}, s32[16]{0:T(128)}, u32[]{:S(2)}) %copy-start.3) | copy-done | bytes 88
  24.3 4.0 %measure.1 = f32[16,16]{1,0:T(8,128)S(1)} custom-call(s32[3]{0:T(128)S(1)} %add_convert_fusion.edge_ref, s32[16]{0:T(128)S(1)} %copy-done.3, bf16[16,128,256]{2,1,0:T(8,128)(2,1)S(1)} %copy-done, bf16[2,128,256]{2,1,0:T(8,128)(2,1)S(1)} %collective-permute-done.prior_ref, bf16[16,32,256]{2,1,0:T(8,128)(2,1)S(1)} %collective-permute-done.1.low_ref, ...), custom_call_target="tpu_custom_call" | custom-call | flops 2000000000 | bytes 6000000 | tf_op jit(solution)/shard_map/measure/pallas_call | solution.py:248
  28.3 4.4 %collective-permute-start.6 = (f32[16,16]{1,0:T(8,128)S(1)}, f32[16,16]{1,0:T(8,128)S(1)}, u32[]{:S(2)}, u32[]{:S(2)}) collective-permute-start(f32[16,16]{1,0:T(8,128)S(1)} %measure.1), channel_id=1, source_target_pairs={{0,63},{1,0},{2,1},{3,2},{4,3},{5,4},{6,5},{7,6},{8,7},{9,8},{10,9... | collective-permute-start | bytes 3080 | tf_op jit(solution)/shard_map/ppermute | solution.py:23
  32.7 0.0 collective-permute-start.5
  32.7 0.8 %collective-permute-done.6 = f32[16,16]{1,0:T(8,128)S(1)} collective-permute-done((f32[16,16]{1,0:T(8,128)S(1)}, f32[16,16]{1,0:T(8,128)S(1)}, u32[]{:S(2)}, u32[]{:S(2)}) %collective-permute-start.6) | collective-permute-done | bytes 1056 | tf_op jit(solution)/shard_map/ppermute | solution.py:23
  33.5 5.9 %collective-permute-done.5 = f32[16,16]{1,0:T(8,128)S(1)} collective-permute-done((f32[16,16]{1,0:T(8,128)S(1)}, f32[16,16]{1,0:T(8,128)S(1)}, u32[]{:S(2)}, u32[]{:S(2)}) %collective-permute-start.5) | collective-permute-done | bytes 1056 | tf_op jit(solution)/shard_map/ppermute | solution.py:23
  39.4 0.1 fusion.4
  39.5 0.0 copy-start.6
  39.6 0.1 copy.10
  39.7 0.5 %copy-done.6 = f32[2,16,2,4]{1,3,2,0:T(4,128)} copy-done((f32[2,16,2,4]{1,3,2,0:T(4,128)}, f32[2,16,2,4]{1,3,2,0:T(4,128)S(1)}, u32[]{:S(2)}) %copy-start.6) | copy-done | bytes 1048
  40.2 1.4 %collective-permute-start.7 = (f32[2,2,4]{2,1,0:T(2,128)S(1)}, f32[2,2,4]{2,1,0:T(2,128)S(1)}, u32[]{:S(2)}, u32[]{:S(2)}) collective-permute-start(f32[2,2,4]{2,1,0:T(2,128)S(1)} %slice_bitcast_fusion), channel_id=1, source_target_pairs={{0,64},{64,0},{128,192},{192,128},{1,65},{65,1},{129,193},{193,129... | collective-permute-start | bytes 200 | tf_op jit(solution)/shard_map/ppermute | solution.py:279
  41.6 0.8 %collective-permute-done.7 = f32[2,2,4]{2,1,0:T(2,128)S(1)} collective-permute-done((f32[2,2,4]{2,1,0:T(2,128)S(1)}, f32[2,2,4]{2,1,0:T(2,128)S(1)}, u32[]{:S(2)}, u32[]{:S(2)}) %collective-permute-start.7) | collective-permute-done | bytes 96 | tf_op jit(solution)/shard_map/ppermute | solution.py:279
  42.4 2.7 %collective-permute-start.8 = (f32[2,2,4]{2,1,0:T(2,128)S(1)}, f32[2,2,4]{2,1,0:T(2,128)S(1)}, u32[]{:S(2)}, u32[]{:S(2)}) collective-permute-start(f32[2,2,4]{2,1,0:T(2,128)S(1)} %fusion.10), channel_id=1, source_target_pairs={{0,128},{64,192},{128,0},{192,64},{1,129},{65,193},{129,1},{193,65... | collective-permute-start | bytes 200 | tf_op jit(solution)/shard_map/ppermute | solution.py:281
  45.1 1.2 %collective-permute-done.8 = f32[2,2,4]{2,1,0:T(2,128)S(1)} collective-permute-done((f32[2,2,4]{2,1,0:T(2,128)S(1)}, f32[2,2,4]{2,1,0:T(2,128)S(1)}, u32[]{:S(2)}, u32[]{:S(2)}) %collective-permute-start.8) | collective-permute-done | bytes 96 | tf_op jit(solution)/shard_map/ppermute | solution.py:281
  46.3 0.7 %copy.11 = f32[2,16,2,4]{1,3,2,0:T(4,128)} copy(f32[2,16,2,4]{3,2,1,0:T(2,128)S(1)} %broadcast_add_fusion) | data formatting | bytes 2048
  (23 shorter events, 0.1 us)
Async XLA Ops:
  0.6 23.0 %copy-start = (bf16[16,128,256]{2,1,0:T(8,128)(2,1)S(1)}, bf16[16,128,256]{2,1,0:T(8,128)(2,1)}, u32[]{:S(2)}) copy-start(bf16[16,128,256]{2,1,0:T(8,128)(2,1)} %own_ref.1) | copy-start | bytes 3145732
  1.6 13.6 %collective-permute-start = (bf16[2,128,256]{2,1,0:T(8,128)(2,1)S(1)}, bf16[2,128,256]{2,1,0:T(8,128)(2,1)S(1)}, u32[]{:S(2)}, u32[]{:S(2)}) collective-permute-start(bf16[2,128,256]{2,1,0:T(8,128)(2,1)S(1)} %slice.46), channel_id=1, source_target_pairs={{0,64},{64,128},{128,192},{192,0},{1,65},{65,129},{129,193},{193,1... | collective-permute-start | bytes 393224 | tf_op jit(solution)/shard_map/ppermute | solution.py:23
  6.0 15.7 %copy-start.1 = (f32[2,128,256]{2,1,0:T(8,128)S(1)}, f32[2,128,256]{2,1,0:T(8,128)}, u32[]{:S(2)}) copy-start(f32[2,128,256]{2,1,0:T(8,128)} %constant.52.clone.rows_ref) | copy-start | bytes 786436
  7.1 16.5 %collective-permute-start.1 = (bf16[16,32,256]{2,1,0:T(8,128)(2,1)S(1)}, bf16[16,32,256]{2,1,0:T(8,128)(2,1)S(1)}, u32[]{:S(2)}, u32[]{:S(2)}) collective-permute-start(bf16[16,32,256]{2,1,0:T(8,128)(2,1)S(1)} %get-tuple-element.9), channel_id=1, source_target_pairs={{0,1},{1,2},{2,3},{3,4},{4,5},{5,6},{6,7},{7,8},{8,9},{9,10},{10,1... | collective-permute-start | bytes 786440 | tf_op jit(solution)/shard_map/ppermute | solution.py:23
  8.4 15.2 %collective-permute-start.2 = (bf16[16,32,256]{2,1,0:T(8,128)(2,1)S(1)}, bf16[16,32,256]{2,1,0:T(8,128)(2,1)S(1)}, u32[]{:S(2)}, u32[]{:S(2)}) collective-permute-start(bf16[16,32,256]{2,1,0:T(8,128)(2,1)S(1)} %get-tuple-element.8), channel_id=1, source_target_pairs={{0,63},{1,0},{2,1},{3,2},{4,3},{5,4},{6,5},{7,6},{8,7},{9,8},{10,9... | collective-permute-start | bytes 786440 | tf_op jit(solution)/shard_map/ppermute | solution.py:23
  15.2 6.6 %copy-start.2 = (f32[72,256]{1,0:T(8,128)S(1)}, f32[72,256]{1,0:T(8,128)}, u32[]{:S(2)}) copy-start(f32[72,256]{1,0:T(8,128)} %constant.51.clone.cols_ref) | copy-start | bytes 221188
  15.2 8.4 %collective-permute-start.3 = (bf16[2,32,256]{2,1,0:T(8,128)(2,1)S(1)}, bf16[2,32,256]{2,1,0:T(8,128)(2,1)S(1)}, u32[]{:S(2)}, u32[]{:S(2)}) collective-permute-start(bf16[2,32,256]{2,1,0:T(8,128)(2,1)S(1)} %get-tuple-element.11), channel_id=1, source_target_pairs={{0,1},{1,2},{2,3},{3,4},{4,5},{5,6},{6,7},{7,8},{8,9},{9,10},{10,1... | collective-permute-start | bytes 98312 | tf_op jit(solution)/shard_map/ppermute | solution.py:23
  15.3 8.3 %collective-permute-start.4 = (bf16[2,32,256]{2,1,0:T(8,128)(2,1)S(1)}, bf16[2,32,256]{2,1,0:T(8,128)(2,1)S(1)}, u32[]{:S(2)}, u32[]{:S(2)}) collective-permute-start(bf16[2,32,256]{2,1,0:T(8,128)(2,1)S(1)} %get-tuple-element.10), channel_id=1, source_target_pairs={{0,63},{1,0},{2,1},{3,2},{4,3},{5,4},{6,5},{7,6},{8,7},{9,8},{10,9... | collective-permute-start | bytes 98312 | tf_op jit(solution)/shard_map/ppermute | solution.py:23
  21.0 0.7 %copy-start.7 = (s32[2,4,2]{1,2,0:T(2,128)S(1)}, s32[2,4,2]{1,2,0:T(2,128)}, u32[]{:S(2)}) copy-start(s32[2,4,2]{1,2,0:T(2,128)} %param.8) | copy-start | bytes 196
  21.8 1.9 %copy-start.4 = (bf16[256,256]{1,0:T(8,128)(2,1)S(1)}, bf16[256,256]{1,0:T(8,128)(2,1)}, u32[]{:S(2)}) copy-start(bf16[256,256]{1,0:T(8,128)(2,1)} %constant.53.clone.back_k_ref) | copy-start | bytes 393220
  21.8 1.9 %copy-start.5 = (bf16[256,256]{1,0:T(8,128)(2,1)S(1)}, bf16[256,256]{1,0:T(8,128)(2,1)}, u32[]{:S(2)}) copy-start(bf16[256,256]{1,0:T(8,128)(2,1)} %constant.54.clone.back_l_ref) | copy-start | bytes 393220
  23.6 0.7 %copy-start.3 = (s32[16]{0:T(128)S(1)}, s32[16]{0:T(128)}, u32[]{:S(2)}) copy-start(s32[16]{0:T(128)} %gap_ref.1) | copy-start | bytes 196
  28.3 5.2 %collective-permute-start.6 = (f32[16,16]{1,0:T(8,128)S(1)}, f32[16,16]{1,0:T(8,128)S(1)}, u32[]{:S(2)}, u32[]{:S(2)}) collective-permute-start(f32[16,16]{1,0:T(8,128)S(1)} %measure.1), channel_id=1, source_target_pairs={{0,63},{1,0},{2,1},{3,2},{4,3},{5,4},{6,5},{7,6},{8,7},{9,8},{10,9... | collective-permute-start | bytes 3080 | tf_op jit(solution)/shard_map/ppermute | solution.py:23
  32.7 6.7 %collective-permute-start.5 = (f32[16,16]{1,0:T(8,128)S(1)}, f32[16,16]{1,0:T(8,128)S(1)}, u32[]{:S(2)}, u32[]{:S(2)}) collective-permute-start(f32[16,16]{1,0:T(8,128)S(1)} %measure.1), channel_id=1, source_target_pairs={{0,1},{1,2},{2,3},{3,4},{4,5},{5,6},{6,7},{7,8},{8,9},{9,10},{10,1... | collective-permute-start | bytes 3080 | tf_op jit(solution)/shard_map/ppermute | solution.py:23
  39.5 0.6 %copy-start.6 = (f32[2,16,2,4]{1,3,2,0:T(4,128)}, f32[2,16,2,4]{1,3,2,0:T(4,128)S(1)}, u32[]{:S(2)}) copy-start(f32[2,16,2,4]{1,3,2,0:T(4,128)S(1)} %fusion.9) | copy-start | bytes 3076
  40.2 2.2 %collective-permute-start.7 = (f32[2,2,4]{2,1,0:T(2,128)S(1)}, f32[2,2,4]{2,1,0:T(2,128)S(1)}, u32[]{:S(2)}, u32[]{:S(2)}) collective-permute-start(f32[2,2,4]{2,1,0:T(2,128)S(1)} %slice_bitcast_fusion), channel_id=1, source_target_pairs={{0,64},{64,0},{128,192},{192,128},{1,65},{65,1},{129,193},{193,129... | collective-permute-start | bytes 200 | tf_op jit(solution)/shard_map/ppermute | solution.py:279
  42.4 3.9 %collective-permute-start.8 = (f32[2,2,4]{2,1,0:T(2,128)S(1)}, f32[2,2,4]{2,1,0:T(2,128)S(1)}, u32[]{:S(2)}, u32[]{:S(2)}) collective-permute-start(f32[2,2,4]{2,1,0:T(2,128)S(1)} %fusion.10), channel_id=1, source_target_pairs={{0,128},{64,192},{128,0},{192,64},{1,129},{65,193},{129,1},{193,65... | collective-permute-start | bytes 200 | tf_op jit(solution)/shard_map/ppermute | solution.py:281

commit v4 on v3

--- a/solution.py
+++ b/solution.py
@@ -21,6 +21,16 @@
 def ring(value, axis, steps):
     count = lax.axis_size(axis)
     return lax.ppermute(value, axis, [(source, (source + steps) % count) for source in range(count)])
+
+
+def swap_near(value):
+    count = lax.axis_size("xy")
+    return lax.ppermute(value, "xy", [(i, i ^ 1) for i in range(count)])
+
+
+def swap_far(value):
+    count = lax.axis_size("xy")
+    return lax.ppermute(value, "xy", [(i, (i + 1 if i % 2 else i - 1) % count) for i in range(count)])
 
 
 def tables():
@@ -87,7 +97,7 @@
 
 
 def patch_kernel(
-    edge_ref, gap_ref, own_ref, prior_ref, low_ref, high_ref, plow_ref, phigh_ref, m_ref, w_ref, back_k_ref, back_l_ref,
+    edge_ref, gap_ref, own_ref, prior_ref, far_ref, near_ref, pfar_ref, pnear_ref, m_ref, w_ref, back_k_ref, back_l_ref,
     out_ref, x_ref, z_ref, n_ref, y_ref, g_ref, max_ref, sum_ref, mom_ref,
 ):
     sections = own_ref.shape[0]
@@ -97,11 +107,15 @@
     main = stacked * 32
     has_prior = jnp.where(edge_ref[2] == 1, 0.0, 1.0)
 
+    odd = edge_ref[3] == 1
+
     def window(r, t):
         image = prior_ref.at[t] if t < 2 else own_ref.at[t - 2]
+        near = pnear_ref[t] if t < 2 else near_ref[t - 2]
+        far = pfar_ref[t] if t < 2 else far_ref[t - 2]
         if r == 0:
-            return [plow_ref[t] if t < 2 else low_ref[t - 2], image[: WIN - HALF]]
-        return [image[HALF:], phigh_ref[t] if t < 2 else high_ref[t - 2]]
+            return [jnp.where(odd, near, far), image[: WIN - HALF]]
+        return [image[HALF:], jnp.where(odd, far, near)]
 
     sub = lax.broadcasted_iota(jnp.int32, (8, WIN), 0)
     for r in range(GR):
@@ -237,7 +251,7 @@
     )(offsets, edges, cols, rows)
 
 
-def measure(edges, gaps, images, prior, low, high, plow, phigh, m_table, w_table):
+def measure(edges, gaps, images, prior, far, near, pfar, pnear, m_table, w_table):
     sections = images.shape[0]
     rows_x = (sections + 2) * 32 + 32
     _, _, back_k, back_l = make_constants()
@@ -263,7 +277,7 @@
         compiler_params=pltpu.CompilerParams(vmem_limit_bytes=32 * 1024 * 1024),
         cost_estimate=pl.CostEstimate(flops=2_000_000_000, bytes_accessed=6_000_000, transcendentals=600_000),
         name="measure",
-    )(edges, gaps, images, prior, low, high, plow, phigh, m_table, w_table, back_k, back_l)
+    )(edges, gaps, images, prior, far, near, pfar, pnear, m_table, w_table, back_k, back_l)
 
 
 def relaxed_step(extended):
@@ -282,30 +296,41 @@
     return jnp.where(place >= 2, across, 0.0) + jnp.where(place % 2 == 1, other, 0.0)
 
 
+def exchange_edges(value, odd):
+    rows = value.shape[1]
+    top, bottom = value[:, :HALF], value[:, rows - HALF :]
+    far = swap_far(jnp.where(odd, bottom, top))
+    near = swap_near(jnp.where(odd, top, bottom))
+    return near, far
+
+
 def local(images, offsets, gaps):
     sections = images.shape[0]
-    rows_here = images.shape[1]
     place = lax.axis_index("xy")
     last = lax.axis_size("xy") - 1
-    edges = jnp.stack([place == 0, place == last, lax.axis_index("gz") == 0]).astype(jnp.int32)
+    odd = place % 2 == 1
+    even = jnp.logical_not(odd)
+    edges = jnp.stack([place == 0, place == last, lax.axis_index("gz") == 0, odd]).astype(jnp.int32)
     m_table, w_table = make_tables(offsets, edges)
     prior = ring(images[sections - 2 :], "gz", 1)
-    low = ring(images[:, rows_here - HALF :], "xy", 1)
-    high = ring(images[:, :HALF], "xy", -1)
-    plow = ring(prior[:, rows_here - HALF :], "xy", 1)
-    phigh = ring(prior[:, :HALF], "xy", -1)
-    measured = measure(edges, gaps, images, prior, low, high, plow, phigh, m_table, w_table)
-    above = jnp.where(place == 0, 0.0, ring(measured, "xy", 1)).reshape(2, GR, GC, sections)
-    below = jnp.where(place == last, 0.0, ring(measured, "xy", -1)).reshape(2, GR, GC, sections)
+    near, far = exchange_edges(images, odd)
+    pnear, pfar = exchange_edges(prior, odd)
+    measured = measure(edges, gaps, images, prior, far, near, pfar, pnear, m_table, w_table)
+    far = swap_far(measured)
+    near = swap_near(measured)
+    above = jnp.where(place == 0, 0.0, jnp.where(even, far, near)).reshape(2, GR, GC, sections)
+    below = jnp.where(place == last, 0.0, jnp.where(even, near, far)).reshape(2, GR, GC, sections)
     measured = measured.reshape(2, GR, GC, sections)
     wide = relaxed_step(jnp.concatenate([above, measured, below], 1))
     row = place * GR + jnp.arange(-1, GR + 1)
     inside = (row >= 0) & (row < GR * (last + 1))
     wide = jnp.where(inside[None, :, None, None], wide, 0.0)
-    smoothed = relaxed_step(wide).transpose(0, 3, 1, 2)
-    running = jnp.cumsum(smoothed, axis=1)
-    earlier_sum = earlier_groups(running[:, sections - 1])
-    return smoothed, running + earlier_sum[:, None]
+    smoothed = relaxed_step(wide)
+    earlier_sum = earlier_groups(jnp.sum(smoothed, axis=3))
+    triangle = jnp.triu(jnp.ones((sections, sections), jnp.float32))
+    running = jnp.dot(smoothed.reshape(2 * PATCHES, sections), triangle, precision=lax.Precision.HIGHEST)
+    composed = running.reshape(smoothed.shape) + earlier_sum[..., None]
+    return smoothed.transpose(0, 3, 1, 2), composed.transpose(0, 3, 1, 2)
 
 
 def solution(mesh):

time: 47.2 us -> 41.7 us (0.88)
  starting transfers between devices: 26.7 us -> 22.4 us
  local copies, waits for them, and re-layouts: 4.76 us -> 2.36 us
  other arithmetic: 0.24 us -> 1.41 us
  waiting for transfers between devices: 8.75 us -> 7.88 us
  matrix products: 0 us -> 0.83 us
    ppermute x7 -> x1, starting transfers between devices: 22.6 us -> 4.38 us  [ring(): lax.ppermute(value, axis, [(source, (source + steps) % count) for source...]
    ppermute x0 -> x6, starting transfers between devices: none -> 13.6 us  [the longest x3 12.9 us: swap_far(): lax.ppermute(value, 'xy', [(i, (i + 1 if i % 2 else i - 1) % count) for i...]
    ppermute x7 -> x1, waiting for transfers between devices: 6.72 us -> 0.01 us  [ring(): lax.ppermute(value, axis, [(source, (source + steps) % count) for source...]
    ppermute x0 -> x6, waiting for transfers between devices: none -> 6.08 us  [the longest x3 5.55 us: swap_far(): lax.ppermute(value, 'xy', [(i, (i + 1 if i % 2 else i - 1) % count) for i...]
    unnamed x18 -> x17, local copies, waits for them, and re-layouts: 2.53 us -> 1.35 us
    select_n x2 -> x3, other arithmetic: 0.01 us -> 1.13 us  [the longest x2 1.12 us: exchange_edges(): near = swap_near(jnp.where(odd, top, bottom))]
    slice x2 -> x0, local copies, waits for them, and re-layouts: 1.11 us -> none  [the longest x1 1.11 us: local(): high = ring(images[:, :HALF], 'xy', -1)]
    dot_general x0 -> x1, matrix products: none -> 0.83 us  [local(): jnp.dot(smoothed.reshape(2 * PATCHES, sections), triangle, precision=lax....]
  transfers between devices with their start and end apart: 9 -> 9, of which waited for: 4 -> 5; matrix products, arithmetic and copies ran while one was open for 3% -> 3% of each run, Pallas kernels for 4% -> 4%
where the time goes in v4:
time: 41.7 us; the launch traced here: 41.5 us
  starting transfers between devices  22.4 us (54%)
  waiting for transfers between devices  7.88 us (19%)
  Pallas kernels  5.83 us (14%)
  local copies, waits for them, and re-layouts  2.36 us (6%)
  other arithmetic  1.41 us (3%)
  matrix products  0.83 us (2%)
  between operations  0.74 us (2%)
    ppermute x3, starting transfers between devices, swap_far(): lax.ppermute(value, 'xy', [(i, (i + 1 if i % 2 else i - 1) % count) for i...  12.9 us
    ppermute x3, waiting for transfers between devices, swap_far(): lax.ppermute(value, 'xy', [(i, (i + 1 if i % 2 else i - 1) % count) for i...  5.55 us
    ppermute x1, starting transfers between devices, ring(): lax.ppermute(value, axis, [(source, (source + steps) % count) for source...  4.38 us
    pallas_call x1, Pallas kernels, measure(): pl.pallas_call(patch_kernel, out_shape=jax.ShapeDtypeStruct((2 * PATCHES,...  4 us
    ppermute x1, starting transfers between devices, earlier_groups(): lax.ppermute(pair, 'gz', [(i, (i + 2) % count) for i in range(count)])  3.36 us
    pallas_call x1, Pallas kernels, make_tables(): pl.pallas_call(table_kernel, out_shape=(jax.ShapeDtypeStruct((GR, 256 + G...  1.83 us
    unnamed x17, local copies, waits for them, and re-layouts  1.35 us
    select_n x2, other arithmetic, exchange_edges(): near = swap_near(jnp.where(odd, top, bottom))  1.12 us
  transfers between devices with their start and end apart: 9, of which 5 were waited for; matrix products, arithmetic and copies ran while one was open for 3% of the time, Pallas kernels for 4%

profile of v4, /device:TPU:1, one launch (start us, length us, event | category | flops | bytes accessed | tf_op | source)
XLA Modules:
  0.0 41.5 jit_solution(8438039977069519915)
XLA Ops:
  0.6 0.0 copy-start
  0.6 1.0 %slice.43 = bf16[2,128,256]{2,1,0:T(8,128)(2,1)S(1)} slice(bf16[16,128,256]{2,1,0:T(8,128)(2,1)} %own_ref.1), slice={[14:16], [0:128], [0:256]} | slice | bytes 262144 | tf_op jit(solution)/shard_map/slice | solution.py:315
  1.6 4.4 %collective-permute-start = (bf16[2,128,256]{2,1,0:T(8,128)(2,1)S(1)}, bf16[2,128,256]{2,1,0:T(8,128)(2,1)S(1)}, u32[]{:S(2)}, u32[]{:S(2)}) collective-permute-start(bf16[2,128,256]{2,1,0:T(8,128)(2,1)S(1)} %slice.43), channel_id=1, source_target_pairs={{0,64},{64,128},{128,192},{192,0},{1,65},{65,129},{129,193},{193,1... | collective-permute-start | bytes 393224 | tf_op jit(solution)/shard_map/ppermute | solution.py:23
  6.0 1.1 %broadcast_select_fusion = (bf16[16,32,256]{2,1,0:T(8,128)(2,1)S(1)}, bf16[16,32,256]{2,1,0:T(8,128)(2,1)S(1)}) fusion(pred[]{:T(512)} %eq.21, bf16[16,128,256]{2,1,0:T(8,128)(2,1)} %own_ref.1), kind=kLoop, calls=%fused_computation | loop fusion | flops 262144 | bytes 1048577 | tf_op jit(solution)/shard_map/jit(_where)/select_n | solution.py:303
  7.1 8.0 %collective-permute-start.1 = (bf16[16,32,256]{2,1,0:T(8,128)(2,1)S(1)}, bf16[16,32,256]{2,1,0:T(8,128)(2,1)S(1)}, u32[]{:S(2)}, u32[]{:S(2)}) collective-permute-start(bf16[16,32,256]{2,1,0:T(8,128)(2,1)S(1)} %get-tuple-element.9), channel_id=1, source_target_pairs={{0,63},{1,2},{2,1},{3,4},{4,3},{5,6},{6,5},{7,8},{8,7},{9,10},{10,... | collective-permute-start | bytes 786440 | tf_op jit(solution)/shard_map/ppermute | solution.py:33
  15.1 0.0 collective-permute-start.2
  15.1 0.0 collective-permute-done.prior_ref
  15.1 0.9 %collective-permute-start.3 = (bf16[2,32,256]{2,1,0:T(8,128)(2,1)S(1)}, bf16[2,32,256]{2,1,0:T(8,128)(2,1)S(1)}, u32[]{:S(2)}, u32[]{:S(2)}) collective-permute-start(bf16[2,32,256]{2,1,0:T(8,128)(2,1)S(1)} %get-tuple-element.11), channel_id=1, source_target_pairs={{0,63},{1,2},{2,1},{3,4},{4,3},{5,6},{6,5},{7,8},{8,7},{9,10},{10,... | collective-permute-start | bytes 98312 | tf_op jit(solution)/shard_map/ppermute | solution.py:33
  16.0 0.8 %collective-permute-start.4 = (bf16[2,32,256]{2,1,0:T(8,128)(2,1)S(1)}, bf16[2,32,256]{2,1,0:T(8,128)(2,1)S(1)}, u32[]{:S(2)}, u32[]{:S(2)}) collective-permute-start(bf16[2,32,256]{2,1,0:T(8,128)(2,1)S(1)} %get-tuple-element.10), channel_id=1, source_target_pairs={{0,1},{1,0},{2,3},{3,2},{4,5},{5,4},{6,7},{7,6},{8,9},{9,8},{10,11... | collective-permute-start | bytes 98312 | tf_op jit(solution)/shard_map/ppermute | solution.py:28
  16.8 0.1 add_convert_fusion.edge_ref
  16.9 0.6 %copy-done.7 = s32[2,4,2]{1,2,0:T(2,128)S(1)} copy-done((s32[2,4,2]{1,2,0:T(2,128)S(1)}, s32[2,4,2]{1,2,0:T(2,128)}, u32[]{:S(2)}) %copy-start.7) | copy-done | bytes 88
  17.5 0.1 copy.9.off_ref
  17.6 0.0 copy-done.1
  17.6 0.0 copy-start.5
  17.6 1.8 %make_tables.1 = (bf16[2,320,256]{2,1,0:T(8,128)(2,1)S(1)}, bf16[8,256,256]{2,1,0:T(8,128)(2,1)S(1)}) custom-call(s32[2,4,2]{2,1,0:T(4,128)S(1)} %copy.9.off_ref, s32[4]{0:T(128)S(1)} %add_convert_fusion.edge_ref, f32[72,256]{1,0:T(8,128)S(1)} %copy-done.2, f32[2,128,256]{2,1,0:T(8,128)S(1)} %copy-done.1), custom_call_target="tpu_custom_call" | custom-call | flops 4000000 | bytes 4000000 | tf_op jit(solution)/shard_map/make_tables/pallas_call | solution.py:240
  19.4 2.8 %collective-permute-done.3.pfar_ref = bf16[2,32,256]{2,1,0:T(8,128)(2,1)S(1)} collective-permute-done((bf16[2,32,256]{2,1,0:T(8,128)(2,1)S(1)}, bf16[2,32,256]{2,1,0:T(8,128)(2,1)S(1)}, u32[]{:S(2)}, u32[]{:S(2)}) %collective-permute-start.3) | collective-permute-done | bytes 32800 | tf_op jit(solution)/shard_map/ppermute | solution.py:33
  22.2 0.5 %collective-permute-done.4.pnear_ref = bf16[2,32,256]{2,1,0:T(8,128)(2,1)S(1)} collective-permute-done((bf16[2,32,256]{2,1,0:T(8,128)(2,1)S(1)}, bf16[2,32,256]{2,1,0:T(8,128)(2,1)S(1)}, u32[]{:S(2)}, u32[]{:S(2)}) %collective-permute-start.4) | collective-permute-done | bytes 32800 | tf_op jit(solution)/shard_map/ppermute | solution.py:28
  22.7 0.0 collective-permute-done.1.far_ref
  22.7 0.0 collective-permute-done.2.near_ref
  22.8 0.6 %copy-done.3 = s32[16]{0:T(128)S(1)} copy-done((s32[16]{0:T(128)S(1)}, s32[16]{0:T(128)}, u32[]{:S(2)}) %copy-start.3) | copy-done | bytes 88
  23.4 4.0 %measure.1 = f32[16,16]{1,0:T(8,128)S(1)} custom-call(s32[4]{0:T(128)S(1)} %add_convert_fusion.edge_ref, s32[16]{0:T(128)S(1)} %copy-done.3, bf16[16,128,256]{2,1,0:T(8,128)(2,1)S(1)} %copy-done, bf16[2,128,256]{2,1,0:T(8,128)(2,1)S(1)} %collective-permute-done.prior_ref, bf16[16,32,256]{2,1,0:T(8,128)(2,1)S(1)} %collective-permute-done.1.far_ref, ...), custom_call_target="tpu_custom_call" | custom-call | flops 2000000000 | bytes 6000000 | tf_op jit(solution)/shard_map/measure/pallas_call | solution.py:262
  27.4 4.0 %collective-permute-start.5 = (f32[16,16]{1,0:T(8,128)S(1)}, f32[16,16]{1,0:T(8,128)S(1)}, u32[]{:S(2)}, u32[]{:S(2)}) collective-permute-start(f32[16,16]{1,0:T(8,128)S(1)} %measure.1), channel_id=1, source_target_pairs={{0,63},{1,2},{2,1},{3,4},{4,3},{5,6},{6,5},{7,8},{8,7},{9,10},{10,... | collective-permute-start | bytes 3080 | tf_op jit(solution)/shard_map/ppermute | solution.py:33
  31.4 0.0 collective-permute-start.6
  31.5 2.8 %collective-permute-done.5 = f32[16,16]{1,0:T(8,128)S(1)} collective-permute-done((f32[16,16]{1,0:T(8,128)S(1)}, f32[16,16]{1,0:T(8,128)S(1)}, u32[]{:S(2)}, u32[]{:S(2)}) %collective-permute-start.5) | collective-permute-done | bytes 1056 | tf_op jit(solution)/shard_map/ppermute | solution.py:33
  34.2 0.0 collective-permute-done.6
  34.2 0.1 fusion.4
  34.3 0.1 fusion.23
  34.4 1.1 %collective-permute-start.7 = (f32[2,2,4]{2,1,0:T(2,128)S(1)}, f32[2,2,4]{2,1,0:T(2,128)S(1)}, u32[]{:S(2)}, u32[]{:S(2)}) collective-permute-start(f32[2,2,4]{2,1,0:T(2,128)S(1)} %get-tuple-element.6), channel_id=1, source_target_pairs={{0,64},{64,0},{128,192},{192,128},{1,65},{65,1},{129,193},{193,129... | collective-permute-start | bytes 200 | tf_op jit(solution)/shard_map/ppermute | solution.py:293
  35.5 0.8 %collective-permute-done.7 = f32[2,2,4]{2,1,0:T(2,128)S(1)} collective-permute-done((f32[2,2,4]{2,1,0:T(2,128)S(1)}, f32[2,2,4]{2,1,0:T(2,128)S(1)}, u32[]{:S(2)}, u32[]{:S(2)}) %collective-permute-start.7) | collective-permute-done | bytes 96 | tf_op jit(solution)/shard_map/ppermute | solution.py:293
  36.3 3.4 %collective-permute-start.8 = (f32[2,2,4]{2,1,0:T(2,128)S(1)}, f32[2,2,4]{2,1,0:T(2,128)S(1)}, u32[]{:S(2)}, u32[]{:S(2)}) collective-permute-start(f32[2,2,4]{2,1,0:T(2,128)S(1)} %add.93), channel_id=1, source_target_pairs={{0,128},{64,192},{128,0},{192,64},{1,129},{65,193},{129,1},{193,65... | collective-permute-start | bytes 200 | tf_op jit(solution)/shard_map/ppermute | solution.py:295
  39.7 1.0 %collective-permute-done.8 = f32[2,2,4]{2,1,0:T(2,128)S(1)} collective-permute-done((f32[2,2,4]{2,1,0:T(2,128)S(1)}, f32[2,2,4]{2,1,0:T(2,128)S(1)}, u32[]{:S(2)}, u32[]{:S(2)}) %collective-permute-start.8) | collective-permute-done | bytes 96 | tf_op jit(solution)/shard_map/ppermute | solution.py:295
  40.7 0.8 %fusion.14 = f32[2,16,2,4]{1,3,2,0:T(4,128)} fusion(f32[2,2,4,16]{3,2,1,0:T(4,128)S(1)} %get-tuple-element.7, f32[2,2,4]{2,1,0:T(2,128)S(1)} %select_add_fusion, s32[16]{0:T(128)S(1)} %iota_add_fusion), kind=kOutput, calls=%fused_computation.24 | convolution fusion | flops 49920 | bytes 2176 | tf_op jit(solution)/shard_map/dot_general | solution.py:331
  (19 shorter events, 0.1 us)
Async XLA Ops:
  0.6 22.1 %copy-start = (bf16[16,128,256]{2,1,0:T(8,128)(2,1)S(1)}, bf16[16,128,256]{2,1,0:T(8,128)(2,1)}, u32[]{:S(2)}) copy-start(bf16[16,128,256]{2,1,0:T(8,128)(2,1)} %own_ref.1) | copy-start | bytes 3145732
  1.6 13.5 %collective-permute-start = (bf16[2,128,256]{2,1,0:T(8,128)(2,1)S(1)}, bf16[2,128,256]{2,1,0:T(8,128)(2,1)S(1)}, u32[]{:S(2)}, u32[]{:S(2)}) collective-permute-start(bf16[2,128,256]{2,1,0:T(8,128)(2,1)S(1)} %slice.43), channel_id=1, source_target_pairs={{0,64},{64,128},{128,192},{192,0},{1,65},{65,129},{129,193},{193,1... | collective-permute-start | bytes 393224 | tf_op jit(solution)/shard_map/ppermute | solution.py:23
  6.0 11.5 %copy-start.1 = (f32[2,128,256]{2,1,0:T(8,128)S(1)}, f32[2,128,256]{2,1,0:T(8,128)}, u32[]{:S(2)}) copy-start(f32[2,128,256]{2,1,0:T(8,128)} %constant.59.clone.rows_ref) | copy-start | bytes 786436
  7.1 15.6 %collective-permute-start.1 = (bf16[16,32,256]{2,1,0:T(8,128)(2,1)S(1)}, bf16[16,32,256]{2,1,0:T(8,128)(2,1)S(1)}, u32[]{:S(2)}, u32[]{:S(2)}) collective-permute-start(bf16[16,32,256]{2,1,0:T(8,128)(2,1)S(1)} %get-tuple-element.9), channel_id=1, source_target_pairs={{0,63},{1,2},{2,1},{3,4},{4,3},{5,6},{6,5},{7,8},{8,7},{9,10},{10,... | collective-permute-start | bytes 786440 | tf_op jit(solution)/shard_map/ppermute | solution.py:33
  15.1 7.6 %collective-permute-start.2 = (bf16[16,32,256]{2,1,0:T(8,128)(2,1)S(1)}, bf16[16,32,256]{2,1,0:T(8,128)(2,1)S(1)}, u32[]{:S(2)}, u32[]{:S(2)}) collective-permute-start(bf16[16,32,256]{2,1,0:T(8,128)(2,1)S(1)} %get-tuple-element.8), channel_id=1, source_target_pairs={{0,1},{1,0},{2,3},{3,2},{4,5},{5,4},{6,7},{7,6},{8,9},{9,8},{10,11... | collective-permute-start | bytes 786440 | tf_op jit(solution)/shard_map/ppermute | solution.py:28
  15.1 2.5 %copy-start.2 = (f32[72,256]{1,0:T(8,128)S(1)}, f32[72,256]{1,0:T(8,128)}, u32[]{:S(2)}) copy-start(f32[72,256]{1,0:T(8,128)} %constant.58.clone.cols_ref) | copy-start | bytes 221188
  15.1 7.1 %collective-permute-start.3 = (bf16[2,32,256]{2,1,0:T(8,128)(2,1)S(1)}, bf16[2,32,256]{2,1,0:T(8,128)(2,1)S(1)}, u32[]{:S(2)}, u32[]{:S(2)}) collective-permute-start(bf16[2,32,256]{2,1,0:T(8,128)(2,1)S(1)} %get-tuple-element.11), channel_id=1, source_target_pairs={{0,63},{1,2},{2,1},{3,4},{4,3},{5,6},{6,5},{7,8},{8,7},{9,10},{10,... | collective-permute-start | bytes 98312 | tf_op jit(solution)/shard_map/ppermute | solution.py:33
  16.0 6.7 %collective-permute-start.4 = (bf16[2,32,256]{2,1,0:T(8,128)(2,1)S(1)}, bf16[2,32,256]{2,1,0:T(8,128)(2,1)S(1)}, u32[]{:S(2)}, u32[]{:S(2)}) collective-permute-start(bf16[2,32,256]{2,1,0:T(8,128)(2,1)S(1)} %get-tuple-element.10), channel_id=1, source_target_pairs={{0,1},{1,0},{2,3},{3,2},{4,5},{5,4},{6,7},{7,6},{8,9},{9,8},{10,11... | collective-permute-start | bytes 98312 | tf_op jit(solution)/shard_map/ppermute | solution.py:28
  16.8 0.7 %copy-start.7 = (s32[2,4,2]{1,2,0:T(2,128)S(1)}, s32[2,4,2]{1,2,0:T(2,128)}, u32[]{:S(2)}) copy-start(s32[2,4,2]{1,2,0:T(2,128)} %param.8) | copy-start | bytes 196
  17.6 5.2 %copy-start.4 = (bf16[256,256]{1,0:T(8,128)(2,1)S(1)}, bf16[256,256]{1,0:T(8,128)(2,1)}, u32[]{:S(2)}) copy-start(bf16[256,256]{1,0:T(8,128)(2,1)} %constant.60.clone.back_k_ref) | copy-start | bytes 393220
  17.6 5.2 %copy-start.5 = (bf16[256,256]{1,0:T(8,128)(2,1)S(1)}, bf16[256,256]{1,0:T(8,128)(2,1)}, u32[]{:S(2)}) copy-start(bf16[256,256]{1,0:T(8,128)(2,1)} %constant.61.clone.back_l_ref) | copy-start | bytes 393220
  22.7 0.7 %copy-start.3 = (s32[16]{0:T(128)S(1)}, s32[16]{0:T(128)}, u32[]{:S(2)}) copy-start(s32[16]{0:T(128)} %gap_ref.1) | copy-start | bytes 196
  27.4 6.8 %collective-permute-start.5 = (f32[16,16]{1,0:T(8,128)S(1)}, f32[16,16]{1,0:T(8,128)S(1)}, u32[]{:S(2)}, u32[]{:S(2)}) collective-permute-start(f32[16,16]{1,0:T(8,128)S(1)} %measure.1), channel_id=1, source_target_pairs={{0,63},{1,2},{2,1},{3,4},{4,3},{5,6},{6,5},{7,8},{8,7},{9,10},{10,... | collective-permute-start | bytes 3080 | tf_op jit(solution)/shard_map/ppermute | solution.py:33
  31.4 2.8 %collective-permute-start.6 = (f32[16,16]{1,0:T(8,128)S(1)}, f32[16,16]{1,0:T(8,128)S(1)}, u32[]{:S(2)}, u32[]{:S(2)}) collective-permute-start(f32[16,16]{1,0:T(8,128)S(1)} %measure.1), channel_id=1, source_target_pairs={{0,1},{1,0},{2,3},{3,2},{4,5},{5,4},{6,7},{7,6},{8,9},{9,8},{10,11... | collective-permute-start | bytes 3080 | tf_op jit(solution)/shard_map/ppermute | solution.py:28
  34.4 6.2 %copy-start.6 = (f32[2,2,4,16]{3,2,1,0:T(4,128)}, f32[2,2,4,16]{3,2,1,0:T(4,128)S(1)}, u32[]{:S(2)}) copy-start(f32[2,2,4,16]{3,2,1,0:T(4,128)S(1)} %get-tuple-element.7) | copy-start | bytes 3076
  34.4 1.9 %collective-permute-start.7 = (f32[2,2,4]{2,1,0:T(2,128)S(1)}, f32[2,2,4]{2,1,0:T(2,128)S(1)}, u32[]{:S(2)}, u32[]{:S(2)}) collective-permute-start(f32[2,2,4]{2,1,0:T(2,128)S(1)} %get-tuple-element.6), channel_id=1, source_target_pairs={{0,64},{64,0},{128,192},{192,128},{1,65},{65,1},{129,193},{193,129... | collective-permute-start | bytes 200 | tf_op jit(solution)/shard_map/ppermute | solution.py:293
  36.3 4.3 %collective-permute-start.8 = (f32[2,2,4]{2,1,0:T(2,128)S(1)}, f32[2,2,4]{2,1,0:T(2,128)S(1)}, u32[]{:S(2)}, u32[]{:S(2)}) collective-permute-start(f32[2,2,4]{2,1,0:T(2,128)S(1)} %add.93), channel_id=1, source_target_pairs={{0,128},{64,192},{128,0},{192,64},{1,129},{65,193},{129,1},{193,65... | collective-permute-start | bytes 200 | tf_op jit(solution)/shard_map/ppermute | solution.py:295

commit v5 on v4

v5 whole, which is shorter than its diff:
```python
import math

import jax
import jax.numpy as jnp
import ml_dtypes
import numpy as np
from jax import lax
from jax.experimental import pallas as pl
from jax.experimental.pallas import tpu as pltpu
from jax.sharding import PartitionSpec as P

P_SIZE = 64
HALF = 32
SHARPNESS = 16.0
WIN = 128
GR = 2
GC = 4
PATCHES = GR * GC
AT_TOP, AT_BOTTOM, FIRST_GROUP, ODD, GAPS, OFFSETS = 0, 1, 2, 3, 4, 20


def ring(value, axis, steps):
    count = lax.axis_size(axis)
    return lax.ppermute(value, axis, [(source, (source + steps) % count) for source in range(count)])


def swap_near(value):
    count = lax.axis_size("xy")
    return lax.ppermute(value, "xy", [(i, i ^ 1) for i in range(count)])


def swap_far(value):
    count = lax.axis_size("xy")
    return lax.ppermute(value, "xy", [(i, (i + 1 if i % 2 else i - 1) % count) for i in range(count)])


def tables():
    indices = np.arange(P_SIZE)
    angles = (indices[:, None] * indices[None, :] % P_SIZE) * (2.0 * math.pi / P_SIZE)
    cos_t = np.cos(angles).astype(np.float32).astype(ml_dtypes.bfloat16).astype(np.float32)
    sin_t = np.sin(angles).astype(np.float32).astype(ml_dtypes.bfloat16).astype(np.float32)
    sin_t = np.where(np.abs(sin_t) < 1e-6, np.float32(0), sin_t)
    return cos_t, sin_t


def make_constants():
    cos_t, sin_t = tables()
    half = P_SIZE // 2
    cols = np.zeros((P_SIZE + 8, 256), np.float32)
    cols[:half, :P_SIZE] = cos_t[:half]
    cols[half:P_SIZE, :P_SIZE] = sin_t[:half]
    cols[P_SIZE:, :P_SIZE] = cos_t[half]
    from_u = np.concatenate([cos_t, -sin_t, -sin_t, cos_t], 1)
    from_v = np.concatenate([-sin_t, -cos_t, -cos_t, -sin_t], 1)
    edge = np.zeros((P_SIZE, 256), np.float32)
    rows = np.stack([np.concatenate([t, edge], 0) for t in (from_u, from_v)])
    to_re = np.concatenate([cos_t, -sin_t], 0)
    to_im = np.concatenate([sin_t, cos_t], 0)
    blank = np.zeros_like(to_re)
    back_k = np.concatenate(
        [
            np.concatenate([to_re, blank, to_im, blank], 1),
            np.concatenate([blank, to_re, blank, to_im], 1),
        ],
        0,
    )
    weight = np.where(np.arange(half) == 0, 1.0, 2.0).astype(np.float32)
    one = np.concatenate([cos_t[:, :half] * weight, -sin_t[:, :half] * weight], 1)
    one[:, half] = cos_t[:, half]
    scale = SHARPNESS / P_SIZE**4
    back_l = np.kron(np.eye(GC, dtype=np.float32), one * np.float32(scale))
    bf = ml_dtypes.bfloat16
    return cols, rows, back_k.astype(bf), back_l.astype(bf)


def table_kernel(scalar_ref, cols_ref, rows_ref, m_ref, w_ref):
    bf16 = jnp.bfloat16
    lane = lax.broadcasted_iota(jnp.int32, cols_ref.shape, 1)
    line = lax.broadcasted_iota(jnp.int32, (WIN, 256), 0)
    for r in range(GR):
        if r == 0:
            inside_image = line >= jnp.where(scalar_ref[AT_TOP] == 1, HALF, 0)
        else:
            inside_image = line < jnp.where(scalar_ref[AT_BOTTOM] == 1, WIN - HALF, WIN)
        for c in range(GC):
            i = r * GC + c
            row_at = scalar_ref[OFFSETS + 2 * i]
            start = c * P_SIZE - HALF + scalar_ref[OFFSETS + 2 * i + 1]
            turn = jnp.where(start < 0, start + 256, start)
            turned = pltpu.roll(cols_ref[...], turn, 1)
            inside = (lane >= start) & (lane < start + P_SIZE)
            turned = jnp.where(inside, turned, 0.0)
            m_ref[r, c * 64 : (c + 1) * 64, :] = turned[:64].astype(bf16)
            m_ref[r, 256 + c * 16 : 256 + (c + 1) * 16, :] = jnp.concatenate([turned[64:]] * 2, 0).astype(bf16)
            for half in range(2):
                turned = pltpu.roll(rows_ref[half], row_at, 0)
                w_ref[i, half * WIN : (half + 1) * WIN, :] = jnp.where(inside_image, turned, 0.0).astype(bf16)


def transform_pair(r, pair, both, m_ref, x_ref, nyquist, scale=None):
    f32 = jnp.float32
    sub = lax.broadcasted_iota(jnp.int32, (8, WIN), 0)
    first = lax.dot_general(m_ref[r], both, (((1,), (1,)), ((), ())), preferred_element_type=f32)
    if scale is not None:
        first = first * scale
    for c in range(GC):
        for k in range(2):
            t = 2 * pair + k
            for half in range(2):
                x_ref[r * GC + c, t * 32 : (t + 1) * 32, half * WIN : (half + 1) * WIN] = first[
                    c * 64 + half * 32 : c * 64 + (half + 1) * 32, k * WIN : (k + 1) * WIN
                ].astype(jnp.bfloat16)
            row = first[256 + c * 16 : 264 + c * 16, k * WIN : (k + 1) * WIN]
            nyquist[c][t // 8] = jnp.where(sub == t % 8, row, nyquist[c][t // 8])


def store_nyquist(r, main, x_ref, nyquist):
    bf16 = jnp.bfloat16
    for c in range(GC):
        i = r * GC + c
        x_ref[i, main : main + 16, :WIN] = jnp.concatenate(nyquist[c], 0).astype(bf16)
        x_ref[i, main : main + 16, WIN:] = jnp.zeros((16, WIN), bf16)


def crossed(partner_p, partner_q, own_p, own_q):
    left = lax.broadcasted_iota(jnp.int32, partner_p.shape, 1) < 64
    twice_re = jnp.where(left, partner_p, partner_q)
    twice_im = jnp.where(left, partner_q, -partner_p)
    return twice_re * own_p + twice_im * own_q


def gap_column(scalar_ref):
    row = lax.broadcasted_iota(jnp.int32, (16, 128), 0)
    gaps = jnp.ones((16, 128), jnp.int32)
    for s in range(16):
        gaps = jnp.where(row == s, scalar_ref[GAPS + s], gaps)
    return gaps


def cross_nyquist(i, own, prior, gaps, n_ref, y_ref, row):
    even = lax.broadcasted_iota(jnp.int32, (16, 128), 0) % 2 == 0
    n_ref[i, 8:24, :] = own
    n_ref[i, 0:8, :] = prior
    one_up = n_ref[i, 7:23, :]
    two_up = n_ref[i, 6:22, :]
    partner_p = jnp.where(gaps == 1, one_up[:, :128], two_up[:, :128])
    partner_q = jnp.where(gaps == 1, one_up[:, 128:], two_up[:, 128:])
    line = crossed(partner_p, partner_q, own[:, :128], own[:, 128:])
    y_ref[row : row + 16, 0:128] = jnp.where(even, line, 0.0).astype(jnp.bfloat16)
    y_ref[row : row + 16, 128:256] = jnp.where(even, 0.0, line).astype(jnp.bfloat16)


def correlate_pairs(pairs, first, y_ref, g_ref, back_k_ref, back_l_ref, max_ref, sum_ref, mom_ref):
    f32 = jnp.float32
    bf16 = jnp.bfloat16
    lines = jnp.dot(y_ref[PATCHES * pairs * 32 :, :], back_k_ref[:, :128], preferred_element_type=f32)
    first_row = lax.broadcasted_iota(jnp.int32, (32, 128), 0) == 0
    for i in range(PATCHES):
        mixed = jnp.dot(y_ref[i * pairs * 32 : (i + 1) * pairs * 32, :], back_k_ref[...], preferred_element_type=f32)
        at = (i % GC) * 64
        for pair in range(pairs):
            row = i * 16 + first + 2 * pair
            line = lines[row : row + 1] + lines[row + 1 : row + 2]
            part = slice(pair * 128, (pair + 1) * 128)
            g_ref[i // GC, at : at + 32, part] = mixed[pair * 32 : (pair + 1) * 32, 0:128].astype(bf16)
            g_ref[i // GC, at + 32 : at + 64, part] = jnp.where(
                first_row, line, mixed[pair * 32 : (pair + 1) * 32, 128:256]
            ).astype(bf16)
    for r in range(GR):
        for lane_at in range(0, pairs * 128, 256):
            part = slice(lane_at, min(lane_at + 256, pairs * 128))
            all_scores = jnp.dot(back_l_ref[...], g_ref[r, :, part], preferred_element_type=f32)
            signed = lax.broadcasted_iota(jnp.int32, (P_SIZE, all_scores.shape[1]), 0)
            signed = jnp.where(signed < HALF, signed, signed - P_SIZE).astype(f32)
            for c in range(GC):
                i = r * GC + c
                scores = all_scores[c * 64 : (c + 1) * 64]
                top = jnp.max(scores, axis=0, keepdims=True)
                weights = jnp.exp(scores - top)
                max_ref[i : i + 1, part] = top
                sum_ref[i : i + 1, part] = jnp.sum(weights, axis=0, keepdims=True)
                mom_ref[i : i + 1, part] = jnp.sum(weights * signed, axis=0, keepdims=True)


def merge_pairs(pairs, first, rows_out, cols_out, max_ref, sum_ref, mom_ref):
    f32 = jnp.float32
    lane = lax.broadcasted_iota(jnp.int32, (PATCHES, 128), 1)
    left = lane < 64
    shift = lane % 64
    shift = jnp.where(shift < HALF, shift, shift - P_SIZE).astype(f32)
    place = lax.broadcasted_iota(jnp.int32, rows_out.shape, 1)
    for pair in range(pairs):
        part = slice(pair * 128, (pair + 1) * 128)
        top = max_ref[:, part]
        top_a = jnp.max(jnp.where(left, top, -jnp.inf), axis=1, keepdims=True)
        top_b = jnp.max(jnp.where(left, -jnp.inf, top), axis=1, keepdims=True)
        factor = jnp.exp(top - jnp.where(left, top_a, top_b))
        total = factor * sum_ref[:, part]
        moment = factor * mom_ref[:, part]
        for k in range(2):
            mine = left if k == 0 else jnp.logical_not(left)
            den = jnp.sum(jnp.where(mine, total, 0.0), axis=1, keepdims=True)
            along_u = jnp.sum(jnp.where(mine, total * shift, 0.0), axis=1, keepdims=True)
            along_v = jnp.sum(jnp.where(mine, moment, 0.0), axis=1, keepdims=True)
            here = place == first + 2 * pair + k
            rows_out = jnp.where(here, along_u / den / 8.0, rows_out)
            cols_out = jnp.where(here, along_v / den / 8.0, cols_out)
    return rows_out, cols_out


def own_kernel(
    scalar_ref, own_ref, far_ref, near_ref, m_ref, w_ref, back_k_ref, back_l_ref,
    out_ref, head_ref, x_ref, z_ref, n_ref, y_ref, g_ref, max_ref, sum_ref, mom_ref,
):
    sections = own_ref.shape[0]
    pairs = sections // 2 - 1
    f32 = jnp.float32
    main = sections * 32
    odd = scalar_ref[ODD] == 1

    def window(r, t):
        if r == 0:
            return [jnp.where(odd, near_ref[t], far_ref[t]), own_ref[t, : WIN - HALF]]
        return [own_ref[t, HALF:], jnp.where(odd, far_ref[t], near_ref[t])]

    for r in range(GR):
        nyquist = [[jnp.zeros((8, WIN), f32) for _ in range(2)] for _ in range(GC)]
        for pair in range(sections // 2):
            both = jnp.concatenate(window(r, 2 * pair) + window(r, 2 * pair + 1), 0)
            transform_pair(r, pair, both, m_ref, x_ref, nyquist)
        store_nyquist(r, main, x_ref, nyquist)

    for i in range(PATCHES):
        spectrum = jnp.dot(x_ref[i], w_ref[i], preferred_element_type=f32).astype(jnp.bfloat16)
        z_ref[i] = spectrum
        head_ref[i, 0:64, :] = spectrum[0:64]
        head_ref[i, 64:80, :] = spectrum[main : main + 16]

    gaps = gap_column(scalar_ref)
    for i in range(PATCHES):
        for s in range(2, sections):
            at = pl.multiple_of((s - scalar_ref[GAPS + s]) * 32, 32)
            row = (i * pairs + s // 2 - 1) * 32
            y_ref[row : row + 32, (s % 2) * 128 : (s % 2 + 1) * 128] = crossed(
                z_ref[i, pl.ds(at, 32), 0:128],
                z_ref[i, pl.ds(at, 32), 128:256],
                z_ref[i, s * 32 : (s + 1) * 32, 0:128],
                z_ref[i, s * 32 : (s + 1) * 32, 128:256],
            )
        own = z_ref[i, main : main + 16, :].astype(f32)
        cross_nyquist(i, own, jnp.zeros((8, 256), f32), gaps, n_ref, y_ref, PATCHES * pairs * 32 + i * 16)

    correlate_pairs(pairs, 2, y_ref, g_ref, back_k_ref, back_l_ref, max_ref, sum_ref, mom_ref)
    zeros = jnp.zeros((PATCHES, sections), f32)
    rows_out, cols_out = merge_pairs(pairs, 2, zeros, zeros, max_ref, sum_ref, mom_ref)
    out_ref[0:PATCHES, :] = rows_out
    out_ref[PATCHES:, :] = cols_out


def head_kernel(
    scalar_ref, prior_ref, head_ref, part_ref, m_ref, w_ref, back_k_ref, back_l_ref,
    out_ref, x_ref, z_ref, n_ref, y_ref, g_ref, max_ref, sum_ref, mom_ref,
):
    f32 = jnp.float32
    has_prior = jnp.where(scalar_ref[FIRST_GROUP] == 1, 0.0, 1.0)
    for r in range(GR):
        nyquist = [[jnp.zeros((8, WIN), f32) for _ in range(2)] for _ in range(GC)]
        at = 0 if r == 0 else HALF
        both = jnp.concatenate([prior_ref[0, at : at + WIN], prior_ref[1, at : at + WIN]], 0)
        transform_pair(r, 0, both, m_ref, x_ref, nyquist, has_prior)
        store_nyquist(r, 64, x_ref, nyquist)

    gaps = gap_column(scalar_ref)
    for i in range(PATCHES):
        spectrum = jnp.dot(x_ref[i], w_ref[i], preferred_element_type=f32)
        z_ref[i, 0:64, :] = spectrum[0:64].astype(jnp.bfloat16)
        z_ref[i, 64:128, :] = head_ref[i, 0:64, :]
        for s in range(2):
            at = pl.multiple_of((s + 2 - scalar_ref[GAPS + s]) * 32, 32)
            y_ref[i * 32 : (i + 1) * 32, s * 128 : (s + 1) * 128] = crossed(
                z_ref[i, pl.ds(at, 32), 0:128],
                z_ref[i, pl.ds(at, 32), 128:256],
                head_ref[i, s * 32 : (s + 1) * 32, 0:128],
                head_ref[i, s * 32 : (s + 1) * 32, 128:256],
            )
        prior = pltpu.roll(spectrum[64:72].astype(jnp.bfloat16).astype(f32), 6, 0)
        cross_nyquist(i, head_ref[i, 64:80, :].astype(f32), prior, gaps, n_ref, y_ref, PATCHES * 32 + i * 16)

    correlate_pairs(1, 0, y_ref, g_ref, back_k_ref, back_l_ref, max_ref, sum_ref, mom_ref)
    rows_out, cols_out = merge_pairs(1, 0, part_ref[0:PATCHES, :], part_ref[PATCHES:, :], max_ref, sum_ref, mom_ref)
    out_ref[0:PATCHES, :] = rows_out
    out_ref[PATCHES:, :] = cols_out


def call(kernel, name, out_shape, scratch, operands, flops, limit):
    smem = pl.BlockSpec(memory_space=pltpu.SMEM)
    vmem = pl.BlockSpec(memory_space=pltpu.VMEM)
    return pl.pallas_call(
        kernel,
        out_shape=out_shape,
        in_specs=[smem] + [vmem] * (len(operands) - 1),
        out_specs=tuple(vmem for _ in out_shape),
        scratch_shapes=scratch,
        compiler_params=pltpu.CompilerParams(vmem_limit_bytes=limit * 1024 * 1024),
        cost_estimate=pl.CostEstimate(flops=flops, bytes_accessed=4_000_000, transcendentals=0),
        name=name,
    )(*operands)


def work_buffers(sections, rows_x, rows_z, pairs):
    bf16 = jnp.bfloat16
    return [
        pltpu.VMEM((PATCHES, rows_x, 2 * WIN), bf16),
        pltpu.VMEM((PATCHES, rows_z, 256), bf16),
        pltpu.VMEM((PATCHES, 24, 256), jnp.float32),
        pltpu.VMEM((PATCHES * (pairs * 32 + 16), 256), bf16),
        pltpu.VMEM((GR, 256, pairs * 128), bf16),
    ] + [pltpu.VMEM((PATCHES, pairs * 128), jnp.float32)] * 3


def make_tables(scalars):
    cols, rows, _, _ = make_constants()
    bf16 = jnp.bfloat16
    shapes = (
        jax.ShapeDtypeStruct((GR, 256 + GC * 16, 256), bf16),
        jax.ShapeDtypeStruct((PATCHES, 2 * WIN, 256), bf16),
    )
    return call(table_kernel, "make_tables", shapes, [], (scalars, cols, rows), 4_000_000, 16)


def measure_own(scalars, images, far, near, m_table, w_table):
    sections = images.shape[0]
    _, _, back_k, back_l = make_constants()
    rows_x = sections * 32 + 16
    shapes = (
        jax.ShapeDtypeStruct((2 * PATCHES, sections), jnp.float32),
        jax.ShapeDtypeStruct((PATCHES, 80, 256), jnp.bfloat16),
    )
    scratch = work_buffers(sections, rows_x, rows_x, sections // 2 - 1)
    operands = (scalars, images, far, near, m_table, w_table, back_k, back_l)
    return call(own_kernel, "measure_own", shapes, scratch, operands, 3_000_000_000, 32)


def measure_head(scalars, prior, head, part, m_table, w_table):
    _, _, back_k, back_l = make_constants()
    shapes = (jax.ShapeDtypeStruct(part.shape, jnp.float32),)
    scratch = work_buffers(part.shape[1], 80, 128, 1)
    operands = (scalars, prior, head, part, m_table, w_table, back_k, back_l)
    return call(head_kernel, "measure_head", shapes, scratch, operands, 500_000_000, 16)[0]


def relaxed_step(extended):
    middle = extended[:, 1:-1]
    widened = jnp.pad(middle, ((0, 0), (0, 0), (1, 1), (0, 0)))
    beside = extended[:, :-2] + extended[:, 2:] + widened[:, :, :-2] + widened[:, :, 2:]
    return 0.5 * middle + 0.125 * beside


def earlier_groups(total):
    place = lax.axis_index("gz")
    count = lax.axis_size("gz")
    other = lax.ppermute(total, "gz", [(i, i ^ 1) for i in range(count)])
    pair = total + other
    across = lax.ppermute(pair, "gz", [(i, (i + 2) % count) for i in range(count)])
    return jnp.where(place >= 2, across, 0.0) + jnp.where(place % 2 == 1, other, 0.0)


def local(images, offsets, gaps):
    sections = images.shape[0]
    rows = images.shape[1]
    place = lax.axis_index("xy")
    last = lax.axis_size("xy") - 1
    odd = place % 2 == 1
    even = jnp.logical_not(odd)
    flags = jnp.stack([place == 0, place == last, lax.axis_index("gz") == 0, odd]).astype(jnp.int32)
    scalars = jnp.concatenate([flags, gaps, offsets.reshape(-1)])
    m_table, w_table = make_tables(scalars)
    top, bottom = images[:, :HALF], images[:, rows - HALF :]
    far = swap_far(jnp.where(odd, bottom, top))
    near = swap_near(jnp.where(odd, top, bottom))
    tail = slice(sections - 2, sections)
    low = jnp.where(even, far[tail], near[tail])
    high = jnp.where(even, near[tail], far[tail])
    kept = HALF + 16
    windows = jnp.concatenate([low, images[tail, :kept], images[tail, rows - kept :], high], axis=1)
    prior = ring(windows, "gz", 1)
    part, head = measure_own(scalars, images, far, near, m_table, w_table)
    measured = measure_head(scalars, prior, head, part, m_table, w_table)
    near = swap_near(measured)
    far = swap_far(measured)
    above = jnp.where(place == 0, 0.0, jnp.where(odd, near, far)).reshape(2, GR, GC, sections)
    below = jnp.where(place == last, 0.0, jnp.where(odd, far, near)).reshape(2, GR, GC, sections)
    measured = measured.reshape(2, GR, GC, sections)
    wide = relaxed_step(jnp.concatenate([above, measured, below], 1))
    row = place * GR + jnp.arange(-1, GR + 1)
    inside = (row >= 0) & (row < GR * (last + 1))
    wide = jnp.where(inside[None, :, None, None], wide, 0.0)
    smoothed = relaxed_step(wide)
    earlier_sum = earlier_groups(jnp.sum(smoothed, axis=3))
    triangle = jnp.triu(jnp.ones((sections, sections), jnp.float32))
    running = jnp.dot(smoothed.reshape(2 * PATCHES, sections), triangle, precision=lax.Precision.HIGHEST)
    running = lax.optimization_barrier(running)
    composed = running.reshape(smoothed.shape) + earlier_sum[..., None]
    return smoothed.transpose(0, 3, 1, 2), composed.transpose(0, 3, 1, 2)


def solution(mesh):
    in_specs = (P("gz", "xy", None), P("xy", None, None), P("gz"))
    out_specs = (P(None, "gz", "xy", None), P(None, "gz", "xy", None))
    return jax.shard_map(local, mesh=mesh, in_specs=in_specs, out_specs=out_specs, check_vma=False)
```

time: 41.7 us -> 42.4 us (1.017)
  Pallas kernels: 5.83 us -> 7.15 us
  other arithmetic: 1.41 us -> 2.22 us
  matrix products: 0.83 us -> 0.19 us
  local copies, waits for them, and re-layouts: 2.36 us -> 1.86 us
    pallas_call x2 -> x3, Pallas kernels: 5.83 us -> 7.15 us  [call(): pl.pallas_call(kernel, out_shape=out_shape, in_specs=[smem] + [vmem] * (l...]
    slice x1, local copies, waits for them, and re-layouts: 1 us -> 0.01 us  [local(): images[tail, :kept]]
    ppermute x1, starting transfers between devices: 3.36 us -> 2.62 us  [earlier_groups(): lax.ppermute(pair, 'gz', [(i, (i + 2) % count) for i in range(count)])]
    ppermute x3 -> x2, starting transfers between devices: 0.77 us -> 0.07 us  [swap_near(): return lax.ppermute(value, 'xy', [(i, i ^ 1) for i in range(count)])]
    transpose x0 -> x1, other arithmetic: none -> 0.67 us  [local(): return (smoothed.transpose(0, 3, 1, 2), composed.transpose(0, 3, 1, 2))]
    dot_general x1, matrix products: 0.83 us -> 0.19 us  [local(): jnp.dot(smoothed.reshape(2 * PATCHES, sections), triangle, precision=lax....]
    ppermute x3 -> x2, starting transfers between devices: 12.9 us -> 13.4 us  [swap_far(): lax.ppermute(value, 'xy', [(i, (i + 1 if i % 2 else i - 1) % count) for i...]
    unnamed x17 -> x15, local copies, waits for them, and re-layouts: 1.35 us -> 1.76 us
  transfers between devices with their start and end apart: 9 -> 7, of which waited for: 5 -> 5; matrix products, arithmetic and copies ran while one was open for 3% -> 3% of each run, Pallas kernels for 4% -> 13%
where the time goes in v5:
time: 42.4 us; the launch traced here: 42.3 us
  starting transfers between devices  22 us (52%)
  waiting for transfers between devices  8.12 us (19%)
  Pallas kernels  7.15 us (17%)
  other arithmetic  2.22 us (5%)
  local copies, waits for them, and re-layouts  1.86 us (4%)
  between operations  0.76 us (2%)
    ppermute x2, starting transfers between devices, swap_far(): lax.ppermute(value, 'xy', [(i, (i + 1 if i % 2 else i - 1) % count) for i...  13.4 us
    pallas_call x3, Pallas kernels, call(): pl.pallas_call(kernel, out_shape=out_shape, in_specs=[smem] + [vmem] * (l...  7.15 us
    ppermute x2, waiting for transfers between devices, swap_far(): lax.ppermute(value, 'xy', [(i, (i + 1 if i % 2 else i - 1) % count) for i...  5.35 us
    ppermute x1, starting transfers between devices, ring(): lax.ppermute(value, axis, [(source, (source + steps) % count) for source...  4.45 us
    ppermute x1, starting transfers between devices, earlier_groups(): lax.ppermute(pair, 'gz', [(i, (i + 2) % count) for i in range(count)])  2.62 us
    unnamed x15, local copies, waits for them, and re-layouts  1.76 us
    ppermute x1, starting transfers between devices, earlier_groups(): other = lax.ppermute(total, 'gz', [(i, i ^ 1) for i in range(count)])  1.42 us
    ppermute x1, waiting for transfers between devices, earlier_groups(): lax.ppermute(pair, 'gz', [(i, (i + 2) % count) for i in range(count)])  1.32 us
  transfers between devices with their start and end apart: 7, of which 5 were waited for; matrix products, arithmetic and copies ran while one was open for 3% of the time, Pallas kernels for 13%

profile of v5, /device:TPU:1, one launch (start us, length us, event | category | flops | bytes accessed | tf_op | source)
XLA Modules:
  0.0 42.3 jit_solution(13097565004434099542)
XLA Ops:
  0.7 0.0 copy-start.4
  0.7 1.2 %broadcast_select_fusion.1 = (bf16[16,32,256]{2,1,0:T(8,128)(2,1)S(1)}, bf16[16,32,256]{2,1,0:T(8,128)(2,1)S(1)}) fusion(pred[]{:T(512)} %eq.21, bf16[16,128,256]{2,1,0:T(8,128)(2,1)} %own_ref.1), kind=kLoop, calls=%fused_computation.1 | loop fusion | flops 262144 | bytes 1048577 | tf_op jit(solution)/shard_map/jit(_where)/select_n | solution.py:379
  1.8 9.7 %collective-permute-start = (bf16[16,32,256]{2,1,0:T(8,128)(2,1)S(1)}, bf16[16,32,256]{2,1,0:T(8,128)(2,1)S(1)}, u32[]{:S(2)}, u32[]{:S(2)}) collective-permute-start(bf16[16,32,256]{2,1,0:T(8,128)(2,1)S(1)} %get-tuple-element.14), channel_id=1, source_target_pairs={{0,63},{1,2},{2,1},{3,4},{4,3},{5,6},{6,5},{7,8},{8,7},{9,10},{10,... | collective-permute-start | bytes 786440 | tf_op jit(solution)/shard_map/ppermute | solution.py:34
  11.5 0.0 collective-permute-start.1
  11.5 0.8 %copy.12 = s32[2,4,2]{2,1,0:T(4,128)S(1)} copy(s32[2,4,2]{1,2,0:T(2,128)} %param.10) | data formatting | bytes 128 | tf_op args[1]
  12.3 0.1 reshape.31
  12.4 0.1 add_convert_fusion
  12.5 0.1 pad_add_fusion.scalar_ref
  12.6 0.0 copy-done.4
  12.6 1.0 %copy-done.1 = f32[2,128,256]{2,1,0:T(8,128)S(1)} copy-done((f32[2,128,256]{2,1,0:T(8,128)S(1)}, f32[2,128,256]{2,1,0:T(8,128)}, u32[]{:S(2)}) %copy-start.1) | copy-done | bytes 262168
  13.5 1.8 %make_tables.1 = (bf16[2,320,256]{2,1,0:T(8,128)(2,1)S(1)}, bf16[8,256,256]{2,1,0:T(8,128)(2,1)S(1)}) custom-call(s32[36]{0:T(128)S(1)} %pad_add_fusion.scalar_ref, f32[72,256]{1,0:T(8,128)S(1)} %copy-done.4, f32[2,128,256]{2,1,0:T(8,128)S(1)} %copy-done.1), custom_call_target="tpu_custom_call" | custom-call | flops 4000000 | bytes 4000000 | tf_op jit(solution)/shard_map/make_tables/pallas_call | solution.py:298
  15.3 2.3 %collective-permute-done.far_ref = bf16[16,32,256]{2,1,0:T(8,128)(2,1)S(1)} collective-permute-done((bf16[16,32,256]{2,1,0:T(8,128)(2,1)S(1)}, bf16[16,32,256]{2,1,0:T(8,128)(2,1)S(1)}, u32[]{:S(2)}, u32[]{:S(2)}) %collective-permute-start) | collective-permute-done | bytes 262176 | tf_op jit(solution)/shard_map/ppermute | solution.py:34
  17.6 0.8 %collective-permute-done.1.near_ref = bf16[16,32,256]{2,1,0:T(8,128)(2,1)S(1)} collective-permute-done((bf16[16,32,256]{2,1,0:T(8,128)(2,1)S(1)}, bf16[16,32,256]{2,1,0:T(8,128)(2,1)S(1)}, u32[]{:S(2)}, u32[]{:S(2)}) %collective-permute-start.1) | collective-permute-done | bytes 262176 | tf_op jit(solution)/shard_map/ppermute | solution.py:29
  18.4 0.0 copy-start.2
  18.4 0.0 copy-start.3
  18.5 4.4 %collective-permute-start.2 = (bf16[2,160,256]{2,1,0:T(8,128)(2,1)S(1)}, bf16[2,160,256]{2,1,0:T(8,128)(2,1)S(1)}, u32[]{:S(2)}, u32[]{:S(2)}) collective-permute-start(bf16[2,160,256]{2,1,0:T(8,128)(2,1)S(1)} %pad_maximum_fusion), channel_id=1, source_target_pairs={{0,64},{64,128},{128,192},{192,0},{1,65},{65,129},{129,193},{193,1... | collective-permute-start | bytes 491528 | tf_op jit(solution)/shard_map/ppermute | solution.py:24
  22.9 0.0 copy-done.3
  22.9 3.6 %measure_own.1 = (f32[16,16]{1,0:T(8,128)S(1)}, bf16[8,80,256]{2,1,0:T(8,128)(2,1)S(1)}) custom-call(s32[36]{0:T(128)S(1)} %pad_add_fusion.scalar_ref, bf16[16,128,256]{2,1,0:T(8,128)(2,1)S(1)} %copy-done, bf16[16,32,256]{2,1,0:T(8,128)(2,1)S(1)} %collective-permute-done.far_ref, bf16[16,32,256]{2,1,0:T(8,128)(2,1)S(1)} %collective-permute-done.1.near_ref, ...), custom_call_target="tpu_custom_call" | custom-call | flops 3000000000 | bytes 4000000 | tf_op jit(solution)/shard_map/measure_own/pallas_call | solution.py:298
  26.6 0.0 collective-permute-done.2.prior_ref
  26.6 1.7 %measure_head.1 = f32[16,16]{1,0:T(8,128)S(1)} custom-call(s32[36]{0:T(128)S(1)} %pad_add_fusion.scalar_ref, bf16[2,160,256]{2,1,0:T(8,128)(2,1)S(1)} %collective-permute-done.2.prior_ref, bf16[8,80,256]{2,1,0:T(8,128)(2,1)S(1)} %get-tuple-element.8.head_ref, f32[16,16]{1,0:T(8,128)S(1)} %get-tuple-element.9.part_ref, ...), custom_call_target="tpu_custom_call" | custom-call | flops 500000000 | bytes 4000000 | tf_op jit(solution)/shard_map/measure_head/pallas_call | solution.py:298
  28.3 0.1 collective-permute-start.3
  28.4 3.7 %collective-permute-start.4 = (f32[16,16]{1,0:T(8,128)S(1)}, f32[16,16]{1,0:T(8,128)S(1)}, u32[]{:S(2)}, u32[]{:S(2)}) collective-permute-start(f32[16,16]{1,0:T(8,128)S(1)} %measure_head.1), channel_id=1, source_target_pairs={{0,63},{1,2},{2,1},{3,4},{4,3},{5,6},{6,5},{7,8},{8,7},{9,10},{10,... | collective-permute-start | bytes 3080 | tf_op jit(solution)/shard_map/ppermute | solution.py:34
  32.1 0.0 collective-permute-done.3
  32.1 3.1 %collective-permute-done.4 = f32[16,16]{1,0:T(8,128)S(1)} collective-permute-done((f32[16,16]{1,0:T(8,128)S(1)}, f32[16,16]{1,0:T(8,128)S(1)}, u32[]{:S(2)}, u32[]{:S(2)}) %collective-permute-start.4) | collective-permute-done | bytes 1056 | tf_op jit(solution)/shard_map/ppermute | solution.py:34
  35.2 0.1 fusion.4
  35.3 0.1 fusion.16
  35.4 1.4 %collective-permute-start.5 = (f32[2,2,4]{2,1,0:T(2,128)S(1)}, f32[2,2,4]{2,1,0:T(2,128)S(1)}, u32[]{:S(2)}, u32[]{:S(2)}) collective-permute-start(f32[2,2,4]{2,1,0:T(2,128)S(1)} %get-tuple-element.10), channel_id=1, source_target_pairs={{0,64},{64,0},{128,192},{192,128},{1,65},{65,1},{129,193},{193,129... | collective-permute-start | bytes 200 | tf_op jit(solution)/shard_map/ppermute | solution.py:362
  36.8 0.2 fusion.9
  37.0 0.6 %collective-permute-done.5 = f32[2,2,4]{2,1,0:T(2,128)S(1)} collective-permute-done((f32[2,2,4]{2,1,0:T(2,128)S(1)}, f32[2,2,4]{2,1,0:T(2,128)S(1)}, u32[]{:S(2)}, u32[]{:S(2)}) %collective-permute-start.5) | collective-permute-done | bytes 96 | tf_op jit(solution)/shard_map/ppermute | solution.py:362
  37.6 2.6 %collective-permute-start.6 = (f32[2,2,4]{2,1,0:T(2,128)S(1)}, f32[2,2,4]{2,1,0:T(2,128)S(1)}, u32[]{:S(2)}, u32[]{:S(2)}) collective-permute-start(f32[2,2,4]{2,1,0:T(2,128)S(1)} %add.89), channel_id=1, source_target_pairs={{0,128},{64,192},{128,0},{192,64},{1,129},{65,193},{129,1},{193,65... | collective-permute-start | bytes 200 | tf_op jit(solution)/shard_map/ppermute | solution.py:364
  40.3 1.3 %collective-permute-done.6 = f32[2,2,4]{2,1,0:T(2,128)S(1)} collective-permute-done((f32[2,2,4]{2,1,0:T(2,128)S(1)}, f32[2,2,4]{2,1,0:T(2,128)S(1)}, u32[]{:S(2)}, u32[]{:S(2)}) %collective-permute-start.6) | collective-permute-done | bytes 96 | tf_op jit(solution)/shard_map/ppermute | solution.py:364
  41.6 0.7 %add_bitcast_fusion = f32[2,16,2,4]{1,3,2,0:T(4,128)} fusion(f32[2,2,4,16]{3,2,1,0:T(4,128)S(1)} %bitcast.21, f32[2,2,4]{2,1,0:T(2,128)S(1)} %select_add_fusion), kind=kLoop, calls=%fused_computation.22 | loop fusion | flops 256 | bytes 2112 | tf_op jit(solution)/shard_map/transpose | solution.py:404
  (18 shorter events, 0.1 us)
Async XLA Ops:
  0.6 14.7 %copy-start = (bf16[16,128,256]{2,1,0:T(8,128)(2,1)S(1)}, bf16[16,128,256]{2,1,0:T(8,128)(2,1)}, u32[]{:S(2)}) copy-start(bf16[16,128,256]{2,1,0:T(8,128)(2,1)} %own_ref.1) | copy-start | bytes 3145732
  0.6 11.8 %copy-start.6 = (s32[16]{0:T(128)S(1)}, s32[16]{0:T(128)}, u32[]{:S(2)}) copy-start(s32[16]{0:T(128)} %param.11) | copy-start | bytes 196
  0.7 11.9 %copy-start.4 = (f32[72,256]{1,0:T(8,128)S(1)}, f32[72,256]{1,0:T(8,128)}, u32[]{:S(2)}) copy-start(f32[72,256]{1,0:T(8,128)} %constant.58.clone.cols_ref) | copy-start | bytes 221188
  1.8 15.7 %collective-permute-start = (bf16[16,32,256]{2,1,0:T(8,128)(2,1)S(1)}, bf16[16,32,256]{2,1,0:T(8,128)(2,1)S(1)}, u32[]{:S(2)}, u32[]{:S(2)}) collective-permute-start(bf16[16,32,256]{2,1,0:T(8,128)(2,1)S(1)} %get-tuple-element.14), channel_id=1, source_target_pairs={{0,63},{1,2},{2,1},{3,4},{4,3},{5,6},{6,5},{7,8},{8,7},{9,10},{10,... | collective-permute-start | bytes 786440 | tf_op jit(solution)/shard_map/ppermute | solution.py:34
  11.5 6.9 %collective-permute-start.1 = (bf16[16,32,256]{2,1,0:T(8,128)(2,1)S(1)}, bf16[16,32,256]{2,1,0:T(8,128)(2,1)S(1)}, u32[]{:S(2)}, u32[]{:S(2)}) collective-permute-start(bf16[16,32,256]{2,1,0:T(8,128)(2,1)S(1)} %get-tuple-element.15), channel_id=1, source_target_pairs={{0,1},{1,0},{2,3},{3,2},{4,5},{5,4},{6,7},{7,6},{8,9},{9,8},{10,11... | collective-permute-start | bytes 786440 | tf_op jit(solution)/shard_map/ppermute | solution.py:29
  12.6 1.0 %copy-start.1 = (f32[2,128,256]{2,1,0:T(8,128)S(1)}, f32[2,128,256]{2,1,0:T(8,128)}, u32[]{:S(2)}) copy-start(f32[2,128,256]{2,1,0:T(8,128)} %constant.59.clone.rows_ref) | copy-start | bytes 786436
  18.4 4.5 %copy-start.2 = (bf16[256,256]{1,0:T(8,128)(2,1)S(1)}, bf16[256,256]{1,0:T(8,128)(2,1)}, u32[]{:S(2)}) copy-start(bf16[256,256]{1,0:T(8,128)(2,1)} %constant.60.clone.back_k_ref) | copy-start | bytes 393220
  18.4 4.5 %copy-start.3 = (bf16[256,256]{1,0:T(8,128)(2,1)S(1)}, bf16[256,256]{1,0:T(8,128)(2,1)}, u32[]{:S(2)}) copy-start(bf16[256,256]{1,0:T(8,128)(2,1)} %constant.61.clone.back_l_ref) | copy-start | bytes 393220
  18.5 8.1 %collective-permute-start.2 = (bf16[2,160,256]{2,1,0:T(8,128)(2,1)S(1)}, bf16[2,160,256]{2,1,0:T(8,128)(2,1)S(1)}, u32[]{:S(2)}, u32[]{:S(2)}) collective-permute-start(bf16[2,160,256]{2,1,0:T(8,128)(2,1)S(1)} %pad_maximum_fusion), channel_id=1, source_target_pairs={{0,64},{64,128},{128,192},{192,0},{1,65},{65,129},{129,193},{193,1... | collective-permute-start | bytes 491528 | tf_op jit(solution)/shard_map/ppermute | solution.py:24
  28.3 3.8 %collective-permute-start.3 = (f32[16,16]{1,0:T(8,128)S(1)}, f32[16,16]{1,0:T(8,128)S(1)}, u32[]{:S(2)}, u32[]{:S(2)}) collective-permute-start(f32[16,16]{1,0:T(8,128)S(1)} %measure_head.1), channel_id=1, source_target_pairs={{0,1},{1,0},{2,3},{3,2},{4,5},{5,4},{6,7},{7,6},{8,9},{9,8},{10,11... | collective-permute-start | bytes 3080 | tf_op jit(solution)/shard_map/ppermute | solution.py:29
  28.4 6.8 %collective-permute-start.4 = (f32[16,16]{1,0:T(8,128)S(1)}, f32[16,16]{1,0:T(8,128)S(1)}, u32[]{:S(2)}, u32[]{:S(2)}) collective-permute-start(f32[16,16]{1,0:T(8,128)S(1)} %measure_head.1), channel_id=1, source_target_pairs={{0,63},{1,2},{2,1},{3,4},{4,3},{5,6},{6,5},{7,8},{8,7},{9,10},{10,... | collective-permute-start | bytes 3080 | tf_op jit(solution)/shard_map/ppermute | solution.py:34
  35.4 1.6 %copy-start.5 = (f32[2,2,4,16]{3,2,1,0:T(4,128)}, f32[2,2,4,16]{3,2,1,0:T(4,128)S(1)}, u32[]{:S(2)}) copy-start(f32[2,2,4,16]{3,2,1,0:T(4,128)S(1)} %get-tuple-element.11) | copy-start | bytes 3076
  35.4 2.2 %collective-permute-start.5 = (f32[2,2,4]{2,1,0:T(2,128)S(1)}, f32[2,2,4]{2,1,0:T(2,128)S(1)}, u32[]{:S(2)}, u32[]{:S(2)}) collective-permute-start(f32[2,2,4]{2,1,0:T(2,128)S(1)} %get-tuple-element.10), channel_id=1, source_target_pairs={{0,64},{64,0},{128,192},{192,128},{1,65},{65,1},{129,193},{193,129... | collective-permute-start | bytes 200 | tf_op jit(solution)/shard_map/ppermute | solution.py:362
  37.6 3.9 %collective-permute-start.6 = (f32[2,2,4]{2,1,0:T(2,128)S(1)}, f32[2,2,4]{2,1,0:T(2,128)S(1)}, u32[]{:S(2)}, u32[]{:S(2)}) collective-permute-start(f32[2,2,4]{2,1,0:T(2,128)S(1)} %add.89), channel_id=1, source_target_pairs={{0,128},{64,192},{128,0},{192,64},{1,129},{65,193},{129,1},{193,65... | collective-permute-start | bytes 200 | tf_op jit(solution)/shard_map/ppermute | solution.py:364

commit v6 on v5

v6 whole, which is shorter than its diff:
```python
from functools import partial
import math

import jax
import jax.numpy as jnp
import ml_dtypes
import numpy as np
from jax import lax
from jax.experimental import pallas as pl
from jax.experimental.pallas import tpu as pltpu
from jax.sharding import PartitionSpec as P

P_SIZE = 64
HALF = 32
SHARPNESS = 16.0
WIN = 128
GR = 2
GC = 4
PATCHES = GR * GC
AT_TOP, AT_BOTTOM, FIRST_GROUP, ODD, GAPS, OFFSETS = 0, 1, 2, 3, 4, 20


def ring(value, axis, steps):
    count = lax.axis_size(axis)
    return lax.ppermute(value, axis, [(source, (source + steps) % count) for source in range(count)])


def swap_near(value):
    count = lax.axis_size("xy")
    return lax.ppermute(value, "xy", [(i, i ^ 1) for i in range(count)])


def swap_far(value):
    count = lax.axis_size("xy")
    return lax.ppermute(value, "xy", [(i, (i + 1 if i % 2 else i - 1) % count) for i in range(count)])


def tables():
    indices = np.arange(P_SIZE)
    angles = (indices[:, None] * indices[None, :] % P_SIZE) * (2.0 * math.pi / P_SIZE)
    cos_t = np.cos(angles).astype(np.float32).astype(ml_dtypes.bfloat16).astype(np.float32)
    sin_t = np.sin(angles).astype(np.float32).astype(ml_dtypes.bfloat16).astype(np.float32)
    sin_t = np.where(np.abs(sin_t) < 1e-6, np.float32(0), sin_t)
    return cos_t, sin_t


def make_constants():
    cos_t, sin_t = tables()
    half = P_SIZE // 2
    cols = np.zeros((P_SIZE + 8, 256), np.float32)
    cols[:half, :P_SIZE] = cos_t[:half]
    cols[half:P_SIZE, :P_SIZE] = sin_t[:half]
    cols[P_SIZE:, :P_SIZE] = cos_t[half]
    rows = np.zeros((WIN, 2 * P_SIZE), np.float32)
    rows[:P_SIZE] = np.concatenate([cos_t, -sin_t], 1)
    to_re = np.concatenate([cos_t, -sin_t], 0)
    to_im = np.concatenate([sin_t, cos_t], 0)
    blank = np.zeros_like(to_re)
    back_k = np.concatenate(
        [
            np.concatenate([to_re, blank, to_im, blank], 1),
            np.concatenate([blank, to_re, blank, to_im], 1),
        ],
        0,
    )
    weight = np.where(np.arange(half) == 0, 1.0, 2.0).astype(np.float32)
    one = np.concatenate([cos_t[:, :half] * weight, -sin_t[:, :half] * weight], 1)
    one[:, half] = cos_t[:, half]
    scale = SHARPNESS / P_SIZE**4
    back_l = np.kron(np.eye(GC, dtype=np.float32), one * np.float32(scale))
    bf = ml_dtypes.bfloat16
    return cols, rows, back_k.astype(bf), back_l.astype(bf)


def table_kernel(scalar_ref, cols_ref, rows_ref, m_ref, w_ref):
    bf16 = jnp.bfloat16
    lane = lax.broadcasted_iota(jnp.int32, cols_ref.shape, 1)
    line = lax.broadcasted_iota(jnp.int32, (WIN, 128), 0)
    sign = jnp.where(lax.broadcasted_iota(jnp.int32, (WIN, 128), 1) < P_SIZE, 1.0, -1.0)
    for r in range(GR):
        inside_image = line >= jnp.where(scalar_ref[AT_TOP if r == 0 else AT_BOTTOM] == 1, HALF, 0)
        for c in range(GC):
            i = r * GC + c
            row_at = scalar_ref[OFFSETS + 2 * i] + r * HALF
            start = c * P_SIZE - HALF + scalar_ref[OFFSETS + 2 * i + 1]
            turn = jnp.where(start < 0, start + 256, start)
            turned = pltpu.roll(cols_ref[...], turn, 1)
            inside = (lane >= start) & (lane < start + P_SIZE)
            turned = jnp.where(inside, turned, 0.0)
            m_ref[r, c * 64 : (c + 1) * 64, :] = turned[:64].astype(bf16)
            m_ref[r, 256 + c * 16 : 256 + (c + 1) * 16, :] = jnp.concatenate([turned[64:]] * 2, 0).astype(bf16)
            straight = jnp.where(inside_image, pltpu.roll(rows_ref[...], row_at, 0), 0.0)
            crossed_over = pltpu.roll(straight, P_SIZE, 1)
            w_ref[i, 0:WIN, 0:128] = straight.astype(bf16)
            w_ref[i, 0:WIN, 128:256] = crossed_over.astype(bf16)
            w_ref[i, WIN:, 0:128] = (crossed_over * sign).astype(bf16)
            w_ref[i, WIN:, 128:256] = (straight * -sign).astype(bf16)


def crossed(partner_p, partner_q, own_p, own_q):
    left = lax.broadcasted_iota(jnp.int32, partner_p.shape, 1) < 64
    twice_re = jnp.where(left, partner_p, partner_q)
    twice_im = jnp.where(left, partner_q, -partner_p)
    return twice_re * own_p + twice_im * own_q


def gap_column(scalar_ref):
    row = lax.broadcasted_iota(jnp.int32, (16, 128), 0)
    gaps = jnp.ones((16, 128), jnp.int32)
    for s in range(16):
        gaps = jnp.where(row == s, scalar_ref[GAPS + s], gaps)
    return gaps


def cross_nyquist(i, own, prior, gaps, n_ref, y_ref, row):
    even = lax.broadcasted_iota(jnp.int32, (16, 128), 0) % 2 == 0
    n_ref[i, 8:24, :] = own
    n_ref[i, 0:8, :] = prior
    one_up = n_ref[i, 7:23, :]
    two_up = n_ref[i, 6:22, :]
    partner_p = jnp.where(gaps == 1, one_up[:, :128], two_up[:, :128])
    partner_q = jnp.where(gaps == 1, one_up[:, 128:], two_up[:, 128:])
    line = crossed(partner_p, partner_q, own[:, :128], own[:, 128:])
    y_ref[row : row + 16, 0:128] = jnp.where(even, line, 0.0).astype(jnp.bfloat16)
    y_ref[row : row + 16, 128:256] = jnp.where(even, 0.0, line).astype(jnp.bfloat16)


def row_kernel(
    is_far, scalar_ref, own_ref, halo_ref, prior_ref, phalo_ref, m_ref, w_ref, back_k_ref, back_l_ref, *rest
):
    if is_far:
        part_ref, *rest = rest
    out_ref, x_ref, z_ref, n_ref, y_ref, g_ref, max_ref, sum_ref, mom_ref = rest
    sections = own_ref.shape[0]
    stacked = sections + 2
    pairs = sections // 2
    f32 = jnp.float32
    bf16 = jnp.bfloat16
    main = stacked * 32
    r = scalar_ref[ODD] if is_far else 1 - scalar_ref[ODD]
    own_at = pl.multiple_of(r * HALF, HALF)
    has_prior = jnp.where(scalar_ref[FIRST_GROUP] == 1, 0.0, 1.0)

    def window(t):
        if t < 2:
            return [phalo_ref[t], prior_ref[t, pl.ds(own_at, WIN - HALF), :]]
        return [halo_ref[t - 2], own_ref[t - 2, pl.ds(own_at, WIN - HALF), :]]

    sub = lax.broadcasted_iota(jnp.int32, (8, WIN), 0)
    nyquist = [[jnp.zeros((8, WIN), f32) for _ in range(3)] for _ in range(GC)]
    for pair in range(stacked // 2):
        both = jnp.concatenate(window(2 * pair) + window(2 * pair + 1), 0)
        first = lax.dot_general(m_ref[r], both, (((1,), (1,)), ((), ())), preferred_element_type=f32)
        if pair == 0:
            first = first * has_prior
        for c in range(GC):
            for k in range(2):
                t = 2 * pair + k
                for half in range(2):
                    x_ref[c, t * 32 : (t + 1) * 32, half * WIN : (half + 1) * WIN] = first[
                        c * 64 + half * 32 : c * 64 + (half + 1) * 32, k * WIN : (k + 1) * WIN
                    ].astype(bf16)
                block, at = (2, t) if t < 2 else ((t - 2) // 8, (t - 2) % 8)
                line = first[256 + c * 16 : 264 + c * 16, k * WIN : (k + 1) * WIN]
                nyquist[c][block] = jnp.where(sub == at, line, nyquist[c][block])
    for c in range(GC):
        x_ref[c, main : main + 16, :WIN] = jnp.concatenate(nyquist[c][:2], 0).astype(bf16)
        x_ref[c, main + 16 :, :WIN] = jnp.concatenate([nyquist[c][2]] * 2, 0).astype(bf16)
        x_ref[c, main:, WIN:] = jnp.zeros((32, WIN), bf16)

    for c in range(GC):
        z_ref[c] = jnp.dot(x_ref[c], w_ref[r * GC + c], preferred_element_type=f32).astype(bf16)

    gaps = gap_column(scalar_ref)
    for c in range(GC):
        for s in range(sections):
            at = pl.multiple_of((s + 2 - scalar_ref[GAPS + s]) * 32, 32)
            row = (c * pairs + s // 2) * 32
            y_ref[row : row + 32, (s % 2) * 128 : (s % 2 + 1) * 128] = crossed(
                z_ref[c, pl.ds(at, 32), 0:128],
                z_ref[c, pl.ds(at, 32), 128:256],
                z_ref[c, (s + 2) * 32 : (s + 3) * 32, 0:128],
                z_ref[c, (s + 2) * 32 : (s + 3) * 32, 128:256],
            )
        own = z_ref[c, main : main + 16, :].astype(f32)
        prior = pltpu.roll(z_ref[c, main + 16 : main + 32, :].astype(f32)[0:8], 6, 0)
        cross_nyquist(c, own, prior, gaps, n_ref, y_ref, GC * pairs * 32 + c * 16)

    lines = jnp.dot(y_ref[GC * pairs * 32 :, :], back_k_ref[:, :128], preferred_element_type=f32)
    first_row = lax.broadcasted_iota(jnp.int32, (32, 128), 0) == 0
    for c in range(GC):
        mixed = jnp.dot(y_ref[c * pairs * 32 : (c + 1) * pairs * 32, :], back_k_ref[...], preferred_element_type=f32)
        for pair in range(pairs):
            row = c * 16 + 2 * pair
            line = lines[row : row + 1] + lines[row + 1 : row + 2]
            part = slice(pair * 128, (pair + 1) * 128)
            g_ref[c * 64 : c * 64 + 32, part] = mixed[pair * 32 : (pair + 1) * 32, 0:128].astype(bf16)
            g_ref[c * 64 + 32 : c * 64 + 64, part] = jnp.where(
                first_row, line, mixed[pair * 32 : (pair + 1) * 32, 128:256]
            ).astype(bf16)

    signed = lax.broadcasted_iota(jnp.int32, (P_SIZE, 256), 0)
    signed = jnp.where(signed < HALF, signed, signed - P_SIZE).astype(f32)
    for lane_at in range(0, pairs * 128, 256):
        part = slice(lane_at, lane_at + 256)
        all_scores = jnp.dot(back_l_ref[...], g_ref[:, part], preferred_element_type=f32)
        for c in range(GC):
            scores = all_scores[c * 64 : (c + 1) * 64]
            top = jnp.max(scores, axis=0, keepdims=True)
            weights = jnp.exp(scores - top)
            max_ref[c : c + 1, part] = top
            sum_ref[c : c + 1, part] = jnp.sum(weights, axis=0, keepdims=True)
            mom_ref[c : c + 1, part] = jnp.sum(weights * signed, axis=0, keepdims=True)

    lane = lax.broadcasted_iota(jnp.int32, (GC, 128), 1)
    left = lane < 64
    shift = lane % 64
    shift = jnp.where(shift < HALF, shift, shift - P_SIZE).astype(f32)
    place = lax.broadcasted_iota(jnp.int32, (GC, sections), 1)
    rows_out = jnp.zeros((GC, sections), f32)
    cols_out = jnp.zeros((GC, sections), f32)
    for pair in range(pairs):
        part = slice(pair * 128, (pair + 1) * 128)
        top = max_ref[:, part]
        top_a = jnp.max(jnp.where(left, top, -jnp.inf), axis=1, keepdims=True)
        top_b = jnp.max(jnp.where(left, -jnp.inf, top), axis=1, keepdims=True)
        factor = jnp.exp(top - jnp.where(left, top_a, top_b))
        total = factor * sum_ref[:, part]
        moment = factor * mom_ref[:, part]
        for k in range(2):
            mine = left if k == 0 else jnp.logical_not(left)
            den = jnp.sum(jnp.where(mine, total, 0.0), axis=1, keepdims=True)
            along_u = jnp.sum(jnp.where(mine, total * shift, 0.0), axis=1, keepdims=True)
            along_v = jnp.sum(jnp.where(mine, moment, 0.0), axis=1, keepdims=True)
            here = place == 2 * pair + k
            rows_out = jnp.where(here, along_u / den / 8.0, rows_out)
            cols_out = jnp.where(here, along_v / den / 8.0, cols_out)
    if not is_far:
        out_ref[0:GC, :] = rows_out
        out_ref[GC:, :] = cols_out
        return
    for component, mine in enumerate((rows_out, cols_out)):
        other = part_ref[component * GC : (component + 1) * GC, :]
        at = component * PATCHES
        out_ref[at : at + GC, :] = jnp.where(r == 0, mine, other)
        out_ref[at + GC : at + PATCHES, :] = jnp.where(r == 0, other, mine)


def call(kernel, name, out_shape, scratch, operands, flops, limit):
    smem = pl.BlockSpec(memory_space=pltpu.SMEM)
    vmem = pl.BlockSpec(memory_space=pltpu.VMEM)
    in_specs = [smem] + [vmem] * (len(operands) - 1)
    return pl.pallas_call(
        kernel,
        out_shape=out_shape,
        in_specs=in_specs,
        out_specs=tuple(vmem for _ in out_shape),
        scratch_shapes=scratch,
        compiler_params=pltpu.CompilerParams(vmem_limit_bytes=limit * 1024 * 1024),
        cost_estimate=pl.CostEstimate(flops=flops, bytes_accessed=0, transcendentals=0),
        name=name,
    )(*operands)


def make_tables(scalars):
    cols, rows, _, _ = make_constants()
    bf16 = jnp.bfloat16
    shapes = (
        jax.ShapeDtypeStruct((GR, 256 + GC * 16, 256), bf16),
        jax.ShapeDtypeStruct((PATCHES, 2 * WIN, 256), bf16),
    )
    return call(table_kernel, "make_tables", shapes, [], (scalars, cols, rows), 0, 16)


def measure_row(scalars, images, halo, prior, phalo, m_table, w_table, part=None):
    sections = images.shape[0]
    rows_x = (sections + 2) * 32 + 32
    _, _, back_k, back_l = make_constants()
    bf16 = jnp.bfloat16
    f32 = jnp.float32
    is_far = part is not None
    shapes = (jax.ShapeDtypeStruct((2 * (PATCHES if is_far else GC), sections), f32),)
    scratch = [
        pltpu.VMEM((GC, rows_x, 2 * WIN), bf16),
        pltpu.VMEM((GC, rows_x, 256), bf16),
        pltpu.VMEM((GC, 24, 256), f32),
        pltpu.VMEM((GC * (sections * 16 + 16), 256), bf16),
        pltpu.VMEM((256, sections * 64), bf16),
    ] + [pltpu.VMEM((GC, sections * 64), f32)] * 3
    operands = (scalars, images, halo, prior, phalo, m_table, w_table, back_k, back_l)
    operands = operands + ((part,) if is_far else ())
    name = "measure_far" if is_far else "measure_near"
    return call(partial(row_kernel, is_far), name, shapes, scratch, operands, 0, 24)[0]


def relaxed_step(extended):
    middle = extended[:, 1:-1]
    widened = jnp.pad(middle, ((0, 0), (0, 0), (1, 1), (0, 0)))
    beside = extended[:, :-2] + extended[:, 2:] + widened[:, :, :-2] + widened[:, :, 2:]
    return 0.5 * middle + 0.125 * beside


def earlier_groups(total):
    place = lax.axis_index("gz")
    count = lax.axis_size("gz")
    other = lax.ppermute(total, "gz", [(i, i ^ 1) for i in range(count)])
    pair = total + other
    across = lax.ppermute(pair, "gz", [(i, (i + 2) % count) for i in range(count)])
    return jnp.where(place >= 2, across, 0.0) + jnp.where(place % 2 == 1, other, 0.0)


def edge_rows(value, odd):
    top, bottom = value[:, :HALF], value[:, value.shape[1] - HALF :]
    return jnp.where(odd, bottom, top), jnp.where(odd, top, bottom)


def local(images, offsets, gaps):
    sections = images.shape[0]
    place = lax.axis_index("xy")
    last = lax.axis_size("xy") - 1
    odd = place % 2 == 1
    flags = jnp.stack([place == 0, place == last, lax.axis_index("gz") == 0, odd]).astype(jnp.int32)
    scalars = jnp.concatenate([flags, gaps, offsets.reshape(-1)])
    prior = ring(images[sections - 2 :], "gz", 1)
    far, near = edge_rows(images, odd)
    far, near = swap_far(far), swap_near(near)
    m_table, w_table, prior = lax.optimization_barrier((*make_tables(scalars), prior))
    pfar, pnear = edge_rows(prior, odd)
    pfar, pnear = swap_far(pfar), swap_near(pnear)
    part = measure_row(scalars, images, near, prior, pnear, m_table, w_table)
    measured = measure_row(scalars, images, far, prior, pfar, m_table, w_table, part)
    near = swap_near(measured)
    far = swap_far(measured)
    above = jnp.where(place == 0, 0.0, jnp.where(odd, near, far)).reshape(2, GR, GC, sections)
    below = jnp.where(place == last, 0.0, jnp.where(odd, far, near)).reshape(2, GR, GC, sections)
    measured = measured.reshape(2, GR, GC, sections)
    wide = relaxed_step(jnp.concatenate([above, measured, below], 1))
    row = place * GR + jnp.arange(-1, GR + 1)
    inside = (row >= 0) & (row < GR * (last + 1))
    wide = jnp.where(inside[None, :, None, None], wide, 0.0)
    smoothed = relaxed_step(wide)
    earlier_sum = earlier_groups(jnp.sum(smoothed, axis=3))
    triangle = jnp.triu(jnp.ones((sections, sections), jnp.float32))
    running = jnp.dot(smoothed.reshape(2 * PATCHES, sections), triangle, precision=lax.Precision.HIGHEST)
    running = lax.optimization_barrier(running)
    composed = running.reshape(smoothed.shape) + earlier_sum[..., None]
    return smoothed.transpose(0, 3, 1, 2), composed.transpose(0, 3, 1, 2)


def solution(mesh):
    in_specs = (P("gz", "xy", None), P("xy", None, None), P("gz"))
    out_specs = (P(None, "gz", "xy", None), P(None, "gz", "xy", None))
    return jax.shard_map(local, mesh=mesh, in_specs=in_specs, out_specs=out_specs, check_vma=False)
```

time: 42.4 us -> 42.8 us (level)
  starting transfers between devices: 22 us -> 19.9 us
  waiting for transfers between devices: 8.12 us -> 9.76 us
  local copies, waits for them, and re-layouts: 1.86 us -> 3.04 us
  Pallas kernels: 7.15 us -> 6.02 us
  other arithmetic: 2.22 us -> 2.95 us
    ppermute x2 -> x3, starting transfers between devices: 13.4 us -> 10.5 us  [swap_far(): lax.ppermute(value, 'xy', [(i, (i + 1 if i % 2 else i - 1) % count) for i...]
    slice x1, local copies, waits for them, and re-layouts: 0.01 us -> 1.65 us  [local(): prior = ring(images[sections - 2:], 'gz', 1)]
    ppermute x2 -> x3, starting transfers between devices: 0.07 us -> 1.31 us  [swap_near(): return lax.ppermute(value, 'xy', [(i, i ^ 1) for i in range(count)])]
    pallas_call x3, Pallas kernels: 7.15 us -> 6.02 us  [call(): pl.pallas_call(kernel, out_shape=out_shape, in_specs=in_specs, out_specs=...]
    ppermute x2 -> x3, waiting for transfers between devices: 0.83 us -> 1.85 us  [swap_near(): return lax.ppermute(value, 'xy', [(i, i ^ 1) for i in range(count)])]
    ppermute x2 -> x3, waiting for transfers between devices: 5.35 us -> 6.14 us  [swap_far(): lax.ppermute(value, 'xy', [(i, (i + 1 if i % 2 else i - 1) % count) for i...]
    select_n x2, other arithmetic: 1.17 us -> 1.92 us  [edge_rows(): return (jnp.where(odd, bottom, top), jnp.where(odd, top, bottom))]
    unnamed x15 -> x17, local copies, waits for them, and re-layouts: 1.76 us -> 1.3 us
  transfers between devices with their start and end apart: 7 -> 9, of which waited for: 5 -> 5; matrix products, arithmetic and copies ran while one was open for 3% -> 6% of each run, Pallas kernels for 13% -> 8%
where the time goes in v6:
time: 42.8 us; the launch traced here: 42.6 us
  starting transfers between devices  19.9 us (46%)
  waiting for transfers between devices  9.76 us (23%)
  Pallas kernels  6.02 us (14%)
  local copies, waits for them, and re-layouts  3.04 us (7%)
  other arithmetic  2.95 us (7%)
  between operations  0.75 us (2%)
    ppermute x3, starting transfers between devices, swap_far(): lax.ppermute(value, 'xy', [(i, (i + 1 if i % 2 else i - 1) % count) for i...  10.5 us
    ppermute x3, waiting for transfers between devices, swap_far(): lax.ppermute(value, 'xy', [(i, (i + 1 if i % 2 else i - 1) % count) for i...  6.14 us
    pallas_call x3, Pallas kernels, call(): pl.pallas_call(kernel, out_shape=out_shape, in_specs=in_specs, out_specs=...  6.02 us
    ppermute x1, starting transfers between devices, ring(): lax.ppermute(value, axis, [(source, (source + steps) % count) for source...  4.3 us
    ppermute x1, starting transfers between devices, earlier_groups(): lax.ppermute(pair, 'gz', [(i, (i + 2) % count) for i in range(count)])  2.79 us
    select_n x2, other arithmetic, edge_rows(): return (jnp.where(odd, bottom, top), jnp.where(odd, top, bottom))  1.92 us
    ppermute x3, waiting for transfers between devices, swap_near(): return lax.ppermute(value, 'xy', [(i, i ^ 1) for i in range(count)])  1.85 us
    slice x1, local copies, waits for them, and re-layouts, local(): prior = ring(images[sections - 2:], 'gz', 1)  1.65 us
  transfers between devices with their start and end apart: 9, of which 5 were waited for; matrix products, arithmetic and copies ran while one was open for 6% of the time, Pallas kernels for 8%

profile of v6, /device:TPU:1, one launch (start us, length us, event | category | flops | bytes accessed | tf_op | source)
XLA Modules:
  0.0 42.6 jit_solution(17825039300182157560)
XLA Ops:
  0.6 0.0 copy-start
  0.6 1.6 %slice.45 = bf16[2,128,256]{2,1,0:T(8,128)(2,1)} slice(bf16[16,128,256]{2,1,0:T(8,128)(2,1)} %own_ref.3), slice={[14:16], [0:128], [0:256]} | slice | bytes 262144 | tf_op jit(solution)/shard_map/slice | solution.py:324
  2.3 4.3 %collective-permute-start.1 = (bf16[2,128,256]{2,1,0:T(8,128)(2,1)}, bf16[2,128,256]{2,1,0:T(8,128)(2,1)S(1)}, u32[]{:S(2)}, u32[]{:S(2)}) collective-permute-start(bf16[2,128,256]{2,1,0:T(8,128)(2,1)} %slice.45), channel_id=1, source_target_pairs={{0,64},{64,128},{128,192},{192,0},{1,65},{65,129},{129,193},{193,1... | collective-permute-start | bytes 393224 | tf_op jit(solution)/shard_map/ppermute | solution.py:25
  6.6 1.9 %broadcast_select_fusion = (bf16[16,32,256]{2,1,0:T(8,128)(2,1)}, bf16[16,32,256]{2,1,0:T(8,128)(2,1)}) fusion(pred[]{:T(512)} %eq.21, bf16[16,128,256]{2,1,0:T(8,128)(2,1)} %own_ref.3), kind=kLoop, calls=%fused_computation | loop fusion | flops 262144 | bytes 1048577 | tf_op jit(solution)/shard_map/jit(_where)/select_n | solution.py:314
  8.5 1.2 %collective-permute-start.3 = (bf16[16,32,256]{2,1,0:T(8,128)(2,1)}, bf16[16,32,256]{2,1,0:T(8,128)(2,1)S(1)}, u32[]{:S(2)}, u32[]{:S(2)}) collective-permute-start(bf16[16,32,256]{2,1,0:T(8,128)(2,1)} %get-tuple-element.14), channel_id=1, source_target_pairs={{0,1},{1,0},{2,3},{3,2},{4,5},{5,4},{6,7},{7,6},{8,9},{9,8},{10,11... | collective-permute-start | bytes 786440 | tf_op jit(solution)/shard_map/ppermute | solution.py:30
  9.7 7.2 %collective-permute-start = (bf16[16,32,256]{2,1,0:T(8,128)(2,1)}, bf16[16,32,256]{2,1,0:T(8,128)(2,1)S(1)}, u32[]{:S(2)}, u32[]{:S(2)}) collective-permute-start(bf16[16,32,256]{2,1,0:T(8,128)(2,1)} %get-tuple-element.15), channel_id=1, source_target_pairs={{0,63},{1,2},{2,1},{3,4},{4,3},{5,6},{6,5},{7,8},{8,7},{9,10},{10,... | collective-permute-start | bytes 786440 | tf_op jit(solution)/shard_map/ppermute | solution.py:35
  16.9 0.1 add_convert_fusion
  17.0 0.6 %copy-done.6 = s32[2,4,2]{1,2,0:T(2,128)S(1)} copy-done((s32[2,4,2]{1,2,0:T(2,128)S(1)}, s32[2,4,2]{1,2,0:T(2,128)}, u32[]{:S(2)}) %copy-start.6) | copy-done | bytes 88
  17.6 0.1 copy.12
  17.7 0.1 reshape.31
  17.8 0.6 %copy-done.7 = s32[16]{0:T(128)S(1)} copy-done((s32[16]{0:T(128)S(1)}, s32[16]{0:T(128)}, u32[]{:S(2)}) %copy-start.7) | copy-done | bytes 88
  18.4 0.1 pad_add_fusion.scalar_ref
  18.5 0.0 copy-start.2
  18.5 1.0 %make_tables.1 = (bf16[2,320,256]{2,1,0:T(8,128)(2,1)S(1)}, bf16[8,256,256]{2,1,0:T(8,128)(2,1)S(1)}) custom-call(s32[36]{0:T(128)S(1)} %pad_add_fusion.scalar_ref, f32[72,256]{1,0:T(8,128)S(1)} %copy-done.3, f32[128,128]{1,0:T(8,128)S(1)} %copy-done.4), custom_call_target="tpu_custom_call" | custom-call | tf_op jit(solution)/shard_map/make_tables/pallas_call | solution.py:253
  19.4 0.0 collective-permute-done.1.prior_ref
  19.5 0.1 collective-permute-start.4
  19.6 0.9 %collective-permute-start.2 = (bf16[2,32,256]{2,1,0:T(8,128)(2,1)S(1)}, bf16[2,32,256]{2,1,0:T(8,128)(2,1)S(1)}, u32[]{:S(2)}, u32[]{:S(2)}) collective-permute-start(bf16[2,32,256]{2,1,0:T(8,128)(2,1)S(1)} %get-tuple-element.17), channel_id=1, source_target_pairs={{0,63},{1,2},{2,1},{3,4},{4,3},{5,6},{6,5},{7,8},{8,7},{9,10},{10,... | collective-permute-start | bytes 98312 | tf_op jit(solution)/shard_map/ppermute | solution.py:35
  20.5 1.8 %collective-permute-done.4.phalo_ref = bf16[2,32,256]{2,1,0:T(8,128)(2,1)S(1)} collective-permute-done((bf16[2,32,256]{2,1,0:T(8,128)(2,1)S(1)}, bf16[2,32,256]{2,1,0:T(8,128)(2,1)S(1)}, u32[]{:S(2)}, u32[]{:S(2)}) %collective-permute-start.4) | collective-permute-done | bytes 32800 | tf_op jit(solution)/shard_map/ppermute | solution.py:30
  22.3 0.0 collective-permute-done.3.halo_ref
  22.3 2.5 %measure_near.1.rest_0_ = f32[8,16]{1,0:T(8,128)S(1)} custom-call(s32[36]{0:T(128)S(1)} %pad_add_fusion.scalar_ref, bf16[16,128,256]{2,1,0:T(8,128)(2,1)S(1)} %copy-done, bf16[16,32,256]{2,1,0:T(8,128)(2,1)S(1)} %collective-permute-done.3.halo_ref, bf16[2,128,256]{2,1,0:T(8,128)(2,1)S(1)} %collective-permute-done.1.prior_ref, ...), custom_call_target="tpu_custom_call" | custom-call | tf_op jit(solution)/shard_map/measure_near/pallas_call | solution.py:253
  24.9 1.8 %collective-permute-done.2.phalo_ref = bf16[2,32,256]{2,1,0:T(8,128)(2,1)S(1)} collective-permute-done((bf16[2,32,256]{2,1,0:T(8,128)(2,1)S(1)}, bf16[2,32,256]{2,1,0:T(8,128)(2,1)S(1)}, u32[]{:S(2)}, u32[]{:S(2)}) %collective-permute-start.2) | collective-permute-done | bytes 32800 | tf_op jit(solution)/shard_map/ppermute | solution.py:35
  26.6 2.5 %measure_far.1 = f32[16,16]{1,0:T(8,128)S(1)} custom-call(s32[36]{0:T(128)S(1)} %pad_add_fusion.scalar_ref, bf16[16,128,256]{2,1,0:T(8,128)(2,1)S(1)} %copy-done, bf16[16,32,256]{2,1,0:T(8,128)(2,1)S(1)} %collective-permute-done.halo_ref, bf16[2,128,256]{2,1,0:T(8,128)(2,1)S(1)} %collective-permute-done.1.prior_ref, ...), custom_call_target="tpu_custom_call" | custom-call | tf_op jit(solution)/shard_map/measure_far/pallas_call | solution.py:253
  29.2 2.4 %collective-permute-start.6 = (f32[16,16]{1,0:T(8,128)S(1)}, f32[16,16]{1,0:T(8,128)S(1)}, u32[]{:S(2)}, u32[]{:S(2)}) collective-permute-start(f32[16,16]{1,0:T(8,128)S(1)} %measure_far.1), channel_id=1, source_target_pairs={{0,63},{1,2},{2,1},{3,4},{4,3},{5,6},{6,5},{7,8},{8,7},{9,10},{10,... | collective-permute-start | bytes 3080 | tf_op jit(solution)/shard_map/ppermute | solution.py:35
  31.6 4.4 %collective-permute-done.6 = f32[16,16]{1,0:T(8,128)S(1)} collective-permute-done((f32[16,16]{1,0:T(8,128)S(1)}, f32[16,16]{1,0:T(8,128)S(1)}, u32[]{:S(2)}, u32[]{:S(2)}) %collective-permute-start.6) | collective-permute-done | bytes 1056 | tf_op jit(solution)/shard_map/ppermute | solution.py:35
  36.0 0.1 fusion.4
  36.1 0.1 fusion.16
  36.2 1.0 %collective-permute-start.7 = (f32[2,2,4]{2,1,0:T(2,128)S(1)}, f32[2,2,4]{2,1,0:T(2,128)S(1)}, u32[]{:S(2)}, u32[]{:S(2)}) collective-permute-start(f32[2,2,4]{2,1,0:T(2,128)S(1)} %get-tuple-element.12), channel_id=1, source_target_pairs={{0,64},{64,0},{128,192},{192,128},{1,65},{65,1},{129,193},{193,129... | collective-permute-start | bytes 200 | tf_op jit(solution)/shard_map/ppermute | solution.py:306
  37.2 0.2 fusion.9
  37.4 0.6 %collective-permute-done.7 = f32[2,2,4]{2,1,0:T(2,128)S(1)} collective-permute-done((f32[2,2,4]{2,1,0:T(2,128)S(1)}, f32[2,2,4]{2,1,0:T(2,128)S(1)}, u32[]{:S(2)}, u32[]{:S(2)}) %collective-permute-start.7) | collective-permute-done | bytes 96 | tf_op jit(solution)/shard_map/ppermute | solution.py:306
  38.0 2.8 %collective-permute-start.8 = (f32[2,2,4]{2,1,0:T(2,128)S(1)}, f32[2,2,4]{2,1,0:T(2,128)S(1)}, u32[]{:S(2)}, u32[]{:S(2)}) collective-permute-start(f32[2,2,4]{2,1,0:T(2,128)S(1)} %add.89), channel_id=1, source_target_pairs={{0,128},{64,192},{128,0},{192,64},{1,129},{65,193},{129,1},{193,65... | collective-permute-start | bytes 200 | tf_op jit(solution)/shard_map/ppermute | solution.py:308
  40.8 1.1 %collective-permute-done.8 = f32[2,2,4]{2,1,0:T(2,128)S(1)} collective-permute-done((f32[2,2,4]{2,1,0:T(2,128)S(1)}, f32[2,2,4]{2,1,0:T(2,128)S(1)}, u32[]{:S(2)}, u32[]{:S(2)}) %collective-permute-start.8) | collective-permute-done | bytes 96 | tf_op jit(solution)/shard_map/ppermute | solution.py:308
  41.9 0.7 %add_bitcast_fusion = f32[2,16,2,4]{1,3,2,0:T(4,128)} fusion(f32[2,2,4,16]{3,2,1,0:T(4,128)S(1)} %bitcast.21, f32[2,2,4]{2,1,0:T(2,128)S(1)} %select_add_fusion), kind=kLoop, calls=%fused_computation.21 | loop fusion | flops 256 | bytes 2112 | tf_op jit(solution)/shard_map/transpose | solution.py:347
  (23 shorter events, 0.1 us)
Async XLA Ops:
  0.6 21.7 %copy-start = (bf16[16,128,256]{2,1,0:T(8,128)(2,1)S(1)}, bf16[16,128,256]{2,1,0:T(8,128)(2,1)}, u32[]{:S(2)}) copy-start(bf16[16,128,256]{2,1,0:T(8,128)(2,1)} %own_ref.3) | copy-start | bytes 3145732
  2.3 17.1 %collective-permute-start.1 = (bf16[2,128,256]{2,1,0:T(8,128)(2,1)}, bf16[2,128,256]{2,1,0:T(8,128)(2,1)S(1)}, u32[]{:S(2)}, u32[]{:S(2)}) collective-permute-start(bf16[2,128,256]{2,1,0:T(8,128)(2,1)} %slice.45), channel_id=1, source_target_pairs={{0,64},{64,128},{128,192},{192,0},{1,65},{65,129},{129,193},{193,1... | collective-permute-start | bytes 393224 | tf_op jit(solution)/shard_map/ppermute | solution.py:25
  6.6 11.9 %copy-start.3 = (f32[72,256]{1,0:T(8,128)S(1)}, f32[72,256]{1,0:T(8,128)}, u32[]{:S(2)}) copy-start(f32[72,256]{1,0:T(8,128)} %constant.58.clone.cols_ref) | copy-start | bytes 221188
  6.6 11.9 %copy-start.4 = (f32[128,128]{1,0:T(8,128)S(1)}, f32[128,128]{1,0:T(8,128)}, u32[]{:S(2)}) copy-start(f32[128,128]{1,0:T(8,128)} %constant.59.clone.rows_ref) | copy-start | bytes 196612
  8.5 13.8 %collective-permute-start.3 = (bf16[16,32,256]{2,1,0:T(8,128)(2,1)}, bf16[16,32,256]{2,1,0:T(8,128)(2,1)S(1)}, u32[]{:S(2)}, u32[]{:S(2)}) collective-permute-start(bf16[16,32,256]{2,1,0:T(8,128)(2,1)} %get-tuple-element.14), channel_id=1, source_target_pairs={{0,1},{1,0},{2,3},{3,2},{4,5},{5,4},{6,7},{7,6},{8,9},{9,8},{10,11... | collective-permute-start | bytes 786440 | tf_op jit(solution)/shard_map/ppermute | solution.py:30
  9.7 16.9 %collective-permute-start = (bf16[16,32,256]{2,1,0:T(8,128)(2,1)}, bf16[16,32,256]{2,1,0:T(8,128)(2,1)S(1)}, u32[]{:S(2)}, u32[]{:S(2)}) collective-permute-start(bf16[16,32,256]{2,1,0:T(8,128)(2,1)} %get-tuple-element.15), channel_id=1, source_target_pairs={{0,63},{1,2},{2,1},{3,4},{4,3},{5,6},{6,5},{7,8},{8,7},{9,10},{10,... | collective-permute-start | bytes 786440 | tf_op jit(solution)/shard_map/ppermute | solution.py:35
  16.9 0.7 %copy-start.6 = (s32[2,4,2]{1,2,0:T(2,128)S(1)}, s32[2,4,2]{1,2,0:T(2,128)}, u32[]{:S(2)}) copy-start(s32[2,4,2]{1,2,0:T(2,128)} %param.10) | copy-start | bytes 196
  17.7 0.7 %copy-start.7 = (s32[16]{0:T(128)S(1)}, s32[16]{0:T(128)}, u32[]{:S(2)}) copy-start(s32[16]{0:T(128)} %param.11) | copy-start | bytes 196
  18.5 3.9 %copy-start.1 = (bf16[256,256]{1,0:T(8,128)(2,1)S(1)}, bf16[256,256]{1,0:T(8,128)(2,1)}, u32[]{:S(2)}) copy-start(bf16[256,256]{1,0:T(8,128)(2,1)} %constant.61.clone.back_l_ref) | copy-start | bytes 393220
  18.5 3.9 %copy-start.2 = (bf16[256,256]{1,0:T(8,128)(2,1)S(1)}, bf16[256,256]{1,0:T(8,128)(2,1)}, u32[]{:S(2)}) copy-start(bf16[256,256]{1,0:T(8,128)(2,1)} %constant.60.clone.back_k_ref) | copy-start | bytes 393220
  19.5 2.9 %collective-permute-start.4 = (bf16[2,32,256]{2,1,0:T(8,128)(2,1)S(1)}, bf16[2,32,256]{2,1,0:T(8,128)(2,1)S(1)}, u32[]{:S(2)}, u32[]{:S(2)}) collective-permute-start(bf16[2,32,256]{2,1,0:T(8,128)(2,1)S(1)} %get-tuple-element.16), channel_id=1, source_target_pairs={{0,1},{1,0},{2,3},{3,2},{4,5},{5,4},{6,7},{7,6},{8,9},{9,8},{10,11... | collective-permute-start | bytes 98312 | tf_op jit(solution)/shard_map/ppermute | solution.py:30
  19.6 7.1 %collective-permute-start.2 = (bf16[2,32,256]{2,1,0:T(8,128)(2,1)S(1)}, bf16[2,32,256]{2,1,0:T(8,128)(2,1)S(1)}, u32[]{:S(2)}, u32[]{:S(2)}) collective-permute-start(bf16[2,32,256]{2,1,0:T(8,128)(2,1)S(1)} %get-tuple-element.17), channel_id=1, source_target_pairs={{0,63},{1,2},{2,1},{3,4},{4,3},{5,6},{6,5},{7,8},{8,7},{9,10},{10,... | collective-permute-start | bytes 98312 | tf_op jit(solution)/shard_map/ppermute | solution.py:35
  29.2 6.8 %collective-permute-start.6 = (f32[16,16]{1,0:T(8,128)S(1)}, f32[16,16]{1,0:T(8,128)S(1)}, u32[]{:S(2)}, u32[]{:S(2)}) collective-permute-start(f32[16,16]{1,0:T(8,128)S(1)} %measure_far.1), channel_id=1, source_target_pairs={{0,63},{1,2},{2,1},{3,4},{4,3},{5,6},{6,5},{7,8},{8,7},{9,10},{10,... | collective-permute-start | bytes 3080 | tf_op jit(solution)/shard_map/ppermute | solution.py:35
  31.6 4.4 %collective-permute-start.5 = (f32[16,16]{1,0:T(8,128)S(1)}, f32[16,16]{1,0:T(8,128)S(1)}, u32[]{:S(2)}, u32[]{:S(2)}) collective-permute-start(f32[16,16]{1,0:T(8,128)S(1)} %measure_far.1), channel_id=1, source_target_pairs={{0,1},{1,0},{2,3},{3,2},{4,5},{5,4},{6,7},{7,6},{8,9},{9,8},{10,11... | collective-permute-start | bytes 3080 | tf_op jit(solution)/shard_map/ppermute | solution.py:30
  36.2 1.2 %copy-start.5 = (f32[2,2,4,16]{3,2,1,0:T(4,128)}, f32[2,2,4,16]{3,2,1,0:T(4,128)S(1)}, u32[]{:S(2)}) copy-start(f32[2,2,4,16]{3,2,1,0:T(4,128)S(1)} %get-tuple-element.13) | copy-start | bytes 3076
  36.2 1.8 %collective-permute-start.7 = (f32[2,2,4]{2,1,0:T(2,128)S(1)}, f32[2,2,4]{2,1,0:T(2,128)S(1)}, u32[]{:S(2)}, u32[]{:S(2)}) collective-permute-start(f32[2,2,4]{2,1,0:T(2,128)S(1)} %get-tuple-element.12), channel_id=1, source_target_pairs={{0,64},{64,0},{128,192},{192,128},{1,65},{65,1},{129,193},{193,129... | collective-permute-start | bytes 200 | tf_op jit(solution)/shard_map/ppermute | solution.py:306
  38.0 3.9 %collective-permute-start.8 = (f32[2,2,4]{2,1,0:T(2,128)S(1)}, f32[2,2,4]{2,1,0:T(2,128)S(1)}, u32[]{:S(2)}, u32[]{:S(2)}) collective-permute-start(f32[2,2,4]{2,1,0:T(2,128)S(1)} %add.89), channel_id=1, source_target_pairs={{0,128},{64,192},{128,0},{192,64},{1,129},{65,193},{129,1},{193,65... | collective-permute-start | bytes 200 | tf_op jit(solution)/shard_map/ppermute | solution.py:308

commit v7 on v6

--- a/solution.py
+++ b/solution.py
@@ -208,33 +208,42 @@
             scores = all_scores[c * 64 : (c + 1) * 64]
             top = jnp.max(scores, axis=0, keepdims=True)
             weights = jnp.exp(scores - top)
-            max_ref[c : c + 1, part] = top
-            sum_ref[c : c + 1, part] = jnp.sum(weights, axis=0, keepdims=True)
-            mom_ref[c : c + 1, part] = jnp.sum(weights * signed, axis=0, keepdims=True)
-
-    lane = lax.broadcasted_iota(jnp.int32, (GC, 128), 1)
+            total = jnp.sum(weights, axis=0, keepdims=True)
+            moment = jnp.sum(weights * signed, axis=0, keepdims=True)
+            for k in range(2):
+                row = (lane_at // 128 + k) * GC + c
+                max_ref[row : row + 1, :] = top[:, k * 128 : (k + 1) * 128]
+                sum_ref[row : row + 1, :] = total[:, k * 128 : (k + 1) * 128]
+                mom_ref[row : row + 1, :] = moment[:, k * 128 : (k + 1) * 128]
+
+    lane = lax.broadcasted_iota(jnp.int32, (pairs * GC, 128), 1)
+    pair_of_row = lax.broadcasted_iota(jnp.int32, (pairs * GC, 128), 0) // GC
     left = lane < 64
     shift = lane % 64
     shift = jnp.where(shift < HALF, shift, shift - P_SIZE).astype(f32)
-    place = lax.broadcasted_iota(jnp.int32, (GC, sections), 1)
-    rows_out = jnp.zeros((GC, sections), f32)
-    cols_out = jnp.zeros((GC, sections), f32)
-    for pair in range(pairs):
-        part = slice(pair * 128, (pair + 1) * 128)
-        top = max_ref[:, part]
-        top_a = jnp.max(jnp.where(left, top, -jnp.inf), axis=1, keepdims=True)
-        top_b = jnp.max(jnp.where(left, -jnp.inf, top), axis=1, keepdims=True)
-        factor = jnp.exp(top - jnp.where(left, top_a, top_b))
-        total = factor * sum_ref[:, part]
-        moment = factor * mom_ref[:, part]
-        for k in range(2):
-            mine = left if k == 0 else jnp.logical_not(left)
-            den = jnp.sum(jnp.where(mine, total, 0.0), axis=1, keepdims=True)
-            along_u = jnp.sum(jnp.where(mine, total * shift, 0.0), axis=1, keepdims=True)
-            along_v = jnp.sum(jnp.where(mine, moment, 0.0), axis=1, keepdims=True)
-            here = place == 2 * pair + k
-            rows_out = jnp.where(here, along_u / den / 8.0, rows_out)
-            cols_out = jnp.where(here, along_v / den / 8.0, cols_out)
+    top = max_ref[...]
+    top_a = jnp.max(jnp.where(left, top, -jnp.inf), axis=1, keepdims=True)
+    top_b = jnp.max(jnp.where(left, -jnp.inf, top), axis=1, keepdims=True)
+    factor = jnp.exp(top - jnp.where(left, top_a, top_b))
+    total = factor * sum_ref[...]
+    moment = factor * mom_ref[...]
+    along = total * shift
+    rows_out = jnp.zeros((pairs * GC, 128), f32)
+    cols_out = jnp.zeros((pairs * GC, 128), f32)
+    for k in range(2):
+        mine = left if k == 0 else jnp.logical_not(left)
+        den = jnp.sum(jnp.where(mine, total, 0.0), axis=1, keepdims=True) * 8.0
+        along_u = jnp.sum(jnp.where(mine, along, 0.0), axis=1, keepdims=True)
+        along_v = jnp.sum(jnp.where(mine, moment, 0.0), axis=1, keepdims=True)
+        here = lane == 2 * pair_of_row + k
+        rows_out = jnp.where(here, along_u / den, rows_out)
+        cols_out = jnp.where(here, along_v / den, cols_out)
+
+    def gather_rows(value):
+        value = sum(value[at : at + 8] for at in range(0, pairs * GC, 8))
+        return (value[0:GC] + value[GC:])[:, :sections]
+
+    rows_out, cols_out = gather_rows(rows_out), gather_rows(cols_out)
     if not is_far:
         out_ref[0:GC, :] = rows_out
         out_ref[GC:, :] = cols_out
@@ -286,7 +295,7 @@
         pltpu.VMEM((GC, 24, 256), f32),
         pltpu.VMEM((GC * (sections * 16 + 16), 256), bf16),
         pltpu.VMEM((256, sections * 64), bf16),
-    ] + [pltpu.VMEM((GC, sections * 64), f32)] * 3
+    ] + [pltpu.VMEM((sections // 2 * GC, 128), f32)] * 3
     operands = (scalars, images, halo, prior, phalo, m_table, w_table, back_k, back_l)
     operands = operands + ((part,) if is_far else ())
     name = "measure_far" if is_far else "measure_near"
@@ -324,7 +333,7 @@
     prior = ring(images[sections - 2 :], "gz", 1)
     far, near = edge_rows(images, odd)
     far, near = swap_far(far), swap_near(near)
-    m_table, w_table, prior = lax.optimization_barrier((*make_tables(scalars), prior))
+    m_table, w_table, images = lax.optimization_barrier((*make_tables(scalars), images))
     pfar, pnear = edge_rows(prior, odd)
     pfar, pnear = swap_far(pfar), swap_near(pnear)
     part = measure_row(scalars, images, near, prior, pnear, m_table, w_table)

time: 42.8 us -> 40.2 us (0.939)
  waiting for transfers between devices: 9.76 us -> 7.21 us
  starting transfers between devices: 19.9 us -> 21.8 us
  local copies, waits for them, and re-layouts: 3.04 us -> 1.9 us
  other arithmetic: 2.95 us -> 2.15 us
    ppermute x3, waiting for transfers between devices: 6.14 us -> 4.59 us  [swap_far(): lax.ppermute(value, 'xy', [(i, (i + 1 if i % 2 else i - 1) % count) for i...]
    ppermute x3, starting transfers between devices: 10.5 us -> 11.9 us  [swap_far(): lax.ppermute(value, 'xy', [(i, (i + 1 if i % 2 else i - 1) % count) for i...]
    ppermute x3, waiting for transfers between devices: 1.85 us -> 1.02 us  [swap_near(): return lax.ppermute(value, 'xy', [(i, i ^ 1) for i in range(count)])]
    select_n x2, other arithmetic: 1.92 us -> 1.12 us  [edge_rows(): return (jnp.where(odd, bottom, top), jnp.where(odd, top, bottom))]
    slice x1, local copies, waits for them, and re-layouts: 1.65 us -> 1 us  [local(): prior = ring(images[sections - 2:], 'gz', 1)]
    unnamed x17, local copies, waits for them, and re-layouts: 1.3 us -> 0.81 us
  transfers between devices with their start and end apart: 9 -> 9, of which waited for: 5 -> 5; matrix products, arithmetic and copies ran while one was open for 6% -> 4% of each run, Pallas kernels for 8% -> 9%
where the time goes in v7:
time: 40.2 us; the launch traced here: 40 us
  starting transfers between devices  21.8 us (54%)
  waiting for transfers between devices  7.21 us (18%)
  Pallas kernels  5.97 us (15%)
  other arithmetic  2.15 us (5%)
  local copies, waits for them, and re-layouts  1.9 us (5%)
  between operations  0.74 us (2%)
    ppermute x3, starting transfers between devices, swap_far(): lax.ppermute(value, 'xy', [(i, (i + 1 if i % 2 else i - 1) % count) for i...  11.9 us
    pallas_call x3, Pallas kernels, call(): pl.pallas_call(kernel, out_shape=out_shape, in_specs=in_specs, out_specs=...  5.97 us
    ppermute x3, waiting for transfers between devices, swap_far(): lax.ppermute(value, 'xy', [(i, (i + 1 if i % 2 else i - 1) % count) for i...  4.59 us
    ppermute x1, starting transfers between devices, ring(): lax.ppermute(value, axis, [(source, (source + steps) % count) for source...  4.38 us
    ppermute x1, starting transfers between devices, earlier_groups(): lax.ppermute(pair, 'gz', [(i, (i + 2) % count) for i in range(count)])  3.13 us
    ppermute x3, starting transfers between devices, swap_near(): return lax.ppermute(value, 'xy', [(i, i ^ 1) for i in range(count)])  1.39 us
    select_n x2, other arithmetic, edge_rows(): return (jnp.where(odd, bottom, top), jnp.where(odd, top, bottom))  1.12 us
    ppermute x1, starting transfers between devices, earlier_groups(): other = lax.ppermute(total, 'gz', [(i, i ^ 1) for i in range(count)])  1.04 us
  transfers between devices with their start and end apart: 9, of which 5 were waited for; matrix products, arithmetic and copies ran while one was open for 4% of the time, Pallas kernels for 9%

profile of v7, /device:TPU:1, one launch (start us, length us, event | category | flops | bytes accessed | tf_op | source)
XLA Modules:
  0.0 40.0 jit_solution(16593617800560584252)
XLA Ops:
  0.6 0.0 copy-start
  0.6 1.0 %slice.45 = bf16[2,128,256]{2,1,0:T(8,128)(2,1)S(1)} slice(bf16[16,128,256]{2,1,0:T(8,128)(2,1)} %own_ref.1), slice={[14:16], [0:128], [0:256]} | slice | bytes 262144 | tf_op jit(solution)/shard_map/slice | solution.py:333
  1.6 4.4 %collective-permute-start.1 = (bf16[2,128,256]{2,1,0:T(8,128)(2,1)S(1)}, bf16[2,128,256]{2,1,0:T(8,128)(2,1)S(1)}, u32[]{:S(2)}, u32[]{:S(2)}) collective-permute-start(bf16[2,128,256]{2,1,0:T(8,128)(2,1)S(1)} %slice.45), channel_id=1, source_target_pairs={{0,64},{64,128},{128,192},{192,0},{1,65},{65,129},{129,193},{193,1... | collective-permute-start | bytes 393224 | tf_op jit(solution)/shard_map/ppermute | solution.py:25
  6.0 1.1 %broadcast_select_fusion = (bf16[16,32,256]{2,1,0:T(8,128)(2,1)S(1)}, bf16[16,32,256]{2,1,0:T(8,128)(2,1)S(1)}) fusion(pred[]{:T(512)} %eq.21, bf16[16,128,256]{2,1,0:T(8,128)(2,1)} %own_ref.1), kind=kLoop, calls=%fused_computation | loop fusion | flops 262144 | bytes 1048577 | tf_op jit(solution)/shard_map/jit(_where)/select_n | solution.py:323
  7.1 1.3 %collective-permute-start.3 = (bf16[16,32,256]{2,1,0:T(8,128)(2,1)S(1)}, bf16[16,32,256]{2,1,0:T(8,128)(2,1)S(1)}, u32[]{:S(2)}, u32[]{:S(2)}) collective-permute-start(bf16[16,32,256]{2,1,0:T(8,128)(2,1)S(1)} %get-tuple-element.14), channel_id=1, source_target_pairs={{0,1},{1,0},{2,3},{3,2},{4,5},{5,4},{6,7},{7,6},{8,9},{9,8},{10,11... | collective-permute-start | bytes 786440 | tf_op jit(solution)/shard_map/ppermute | solution.py:30
  8.4 7.2 %collective-permute-start = (bf16[16,32,256]{2,1,0:T(8,128)(2,1)S(1)}, bf16[16,32,256]{2,1,0:T(8,128)(2,1)S(1)}, u32[]{:S(2)}, u32[]{:S(2)}) collective-permute-start(bf16[16,32,256]{2,1,0:T(8,128)(2,1)S(1)} %get-tuple-element.15), channel_id=1, source_target_pairs={{0,63},{1,2},{2,1},{3,4},{4,3},{5,6},{6,5},{7,8},{8,7},{9,10},{10,... | collective-permute-start | bytes 786440 | tf_op jit(solution)/shard_map/ppermute | solution.py:35
  15.7 0.7 %copy-done.6 = s32[2,4,2]{1,2,0:T(2,128)S(1)} copy-done((s32[2,4,2]{1,2,0:T(2,128)S(1)}, s32[2,4,2]{1,2,0:T(2,128)}, u32[]{:S(2)}) %copy-start.6) | copy-done | bytes 88
  16.3 0.1 copy.12
  16.4 0.1 reshape.31
  16.5 0.1 add_convert_fusion
  16.6 0.0 collective-permute-done.1.prior_ref
  16.6 0.1 collective-permute-start.4
  16.7 0.9 %collective-permute-start.2 = (bf16[2,32,256]{2,1,0:T(8,128)(2,1)S(1)}, bf16[2,32,256]{2,1,0:T(8,128)(2,1)S(1)}, u32[]{:S(2)}, u32[]{:S(2)}) collective-permute-start(bf16[2,32,256]{2,1,0:T(8,128)(2,1)S(1)} %get-tuple-element.17), channel_id=1, source_target_pairs={{0,63},{1,2},{2,1},{3,4},{4,3},{5,6},{6,5},{7,8},{8,7},{9,10},{10,... | collective-permute-start | bytes 98312 | tf_op jit(solution)/shard_map/ppermute | solution.py:35
  17.7 0.1 pad_add_fusion.scalar_ref
  17.7 1.0 %make_tables.1 = (bf16[2,320,256]{2,1,0:T(8,128)(2,1)S(1)}, bf16[8,256,256]{2,1,0:T(8,128)(2,1)S(1)}) custom-call(s32[36]{0:T(128)S(1)} %pad_add_fusion.scalar_ref, f32[72,256]{1,0:T(8,128)S(1)} %copy-done.3, f32[128,128]{1,0:T(8,128)S(1)} %copy-done.4), custom_call_target="tpu_custom_call" | custom-call | tf_op jit(solution)/shard_map/make_tables/pallas_call | solution.py:262
  18.7 1.0 %collective-permute-done.4.phalo_ref = bf16[2,32,256]{2,1,0:T(8,128)(2,1)S(1)} collective-permute-done((bf16[2,32,256]{2,1,0:T(8,128)(2,1)S(1)}, bf16[2,32,256]{2,1,0:T(8,128)(2,1)S(1)}, u32[]{:S(2)}, u32[]{:S(2)}) %collective-permute-start.4) | collective-permute-done | bytes 32800 | tf_op jit(solution)/shard_map/ppermute | solution.py:30
  19.7 0.0 collective-permute-done.3.halo_ref
  19.7 2.5 %measure_near.1.rest_0_ = f32[8,16]{1,0:T(8,128)S(1)} custom-call(s32[36]{0:T(128)S(1)} %pad_add_fusion.scalar_ref, bf16[16,128,256]{2,1,0:T(8,128)(2,1)S(1)} %copy-done, bf16[16,32,256]{2,1,0:T(8,128)(2,1)S(1)} %collective-permute-done.3.halo_ref, bf16[2,128,256]{2,1,0:T(8,128)(2,1)S(1)} %collective-permute-done.1.prior_ref, ...), custom_call_target="tpu_custom_call" | custom-call | tf_op jit(solution)/shard_map/measure_near/pallas_call | solution.py:262
  22.2 1.6 %collective-permute-done.2.phalo_ref = bf16[2,32,256]{2,1,0:T(8,128)(2,1)S(1)} collective-permute-done((bf16[2,32,256]{2,1,0:T(8,128)(2,1)S(1)}, bf16[2,32,256]{2,1,0:T(8,128)(2,1)S(1)}, u32[]{:S(2)}, u32[]{:S(2)}) %collective-permute-start.2) | collective-permute-done | bytes 32800 | tf_op jit(solution)/shard_map/ppermute | solution.py:35
  23.8 0.0 collective-permute-done.halo_ref
  23.8 2.5 %measure_far.1 = f32[16,16]{1,0:T(8,128)S(1)} custom-call(s32[36]{0:T(128)S(1)} %pad_add_fusion.scalar_ref, bf16[16,128,256]{2,1,0:T(8,128)(2,1)S(1)} %copy-done, bf16[16,32,256]{2,1,0:T(8,128)(2,1)S(1)} %collective-permute-done.halo_ref, bf16[2,128,256]{2,1,0:T(8,128)(2,1)S(1)} %collective-permute-done.1.prior_ref, ...), custom_call_target="tpu_custom_call" | custom-call | tf_op jit(solution)/shard_map/measure_far/pallas_call | solution.py:262
  26.3 3.8 %collective-permute-start.6 = (f32[16,16]{1,0:T(8,128)S(1)}, f32[16,16]{1,0:T(8,128)S(1)}, u32[]{:S(2)}, u32[]{:S(2)}) collective-permute-start(f32[16,16]{1,0:T(8,128)S(1)} %measure_far.1), channel_id=1, source_target_pairs={{0,63},{1,2},{2,1},{3,4},{4,3},{5,6},{6,5},{7,8},{8,7},{9,10},{10,... | collective-permute-start | bytes 3080 | tf_op jit(solution)/shard_map/ppermute | solution.py:35
  30.1 0.0 collective-permute-start.5
  30.1 3.0 %collective-permute-done.6 = f32[16,16]{1,0:T(8,128)S(1)} collective-permute-done((f32[16,16]{1,0:T(8,128)S(1)}, f32[16,16]{1,0:T(8,128)S(1)}, u32[]{:S(2)}, u32[]{:S(2)}) %collective-permute-start.6) | collective-permute-done | bytes 1056 | tf_op jit(solution)/shard_map/ppermute | solution.py:35
  33.2 0.1 fusion.4
  33.3 0.1 fusion.16
  33.4 1.0 %collective-permute-start.7 = (f32[2,2,4]{2,1,0:T(2,128)S(1)}, f32[2,2,4]{2,1,0:T(2,128)S(1)}, u32[]{:S(2)}, u32[]{:S(2)}) collective-permute-start(f32[2,2,4]{2,1,0:T(2,128)S(1)} %get-tuple-element.12), channel_id=1, source_target_pairs={{0,64},{64,0},{128,192},{192,128},{1,65},{65,1},{129,193},{193,129... | collective-permute-start | bytes 200 | tf_op jit(solution)/shard_map/ppermute | solution.py:315
  34.4 0.2 fusion.9
  34.6 0.6 %collective-permute-done.7 = f32[2,2,4]{2,1,0:T(2,128)S(1)} collective-permute-done((f32[2,2,4]{2,1,0:T(2,128)S(1)}, f32[2,2,4]{2,1,0:T(2,128)S(1)}, u32[]{:S(2)}, u32[]{:S(2)}) %collective-permute-start.7) | collective-permute-done | bytes 96 | tf_op jit(solution)/shard_map/ppermute | solution.py:315
  35.2 3.1 %collective-permute-start.8 = (f32[2,2,4]{2,1,0:T(2,128)S(1)}, f32[2,2,4]{2,1,0:T(2,128)S(1)}, u32[]{:S(2)}, u32[]{:S(2)}) collective-permute-start(f32[2,2,4]{2,1,0:T(2,128)S(1)} %add.89), channel_id=1, source_target_pairs={{0,128},{64,192},{128,0},{192,64},{1,129},{65,193},{129,1},{193,65... | collective-permute-start | bytes 200 | tf_op jit(solution)/shard_map/ppermute | solution.py:317
  38.4 1.0 %collective-permute-done.8 = f32[2,2,4]{2,1,0:T(2,128)S(1)} collective-permute-done((f32[2,2,4]{2,1,0:T(2,128)S(1)}, f32[2,2,4]{2,1,0:T(2,128)S(1)}, u32[]{:S(2)}, u32[]{:S(2)}) %collective-permute-start.8) | collective-permute-done | bytes 96 | tf_op jit(solution)/shard_map/ppermute | solution.py:317
  39.3 0.7 %add_bitcast_fusion = f32[2,16,2,4]{1,3,2,0:T(4,128)} fusion(f32[2,2,4,16]{3,2,1,0:T(4,128)S(1)} %bitcast.21, f32[2,2,4]{2,1,0:T(2,128)S(1)} %select_add_fusion), kind=kLoop, calls=%fused_computation.21 | loop fusion | flops 256 | bytes 2112 | tf_op jit(solution)/shard_map/transpose | solution.py:356
  (23 shorter events, 0.1 us)
Async XLA Ops:
  0.6 19.1 %copy-start = (bf16[16,128,256]{2,1,0:T(8,128)(2,1)S(1)}, bf16[16,128,256]{2,1,0:T(8,128)(2,1)}, u32[]{:S(2)}) copy-start(bf16[16,128,256]{2,1,0:T(8,128)(2,1)} %own_ref.1) | copy-start | bytes 3145732
  1.6 15.0 %collective-permute-start.1 = (bf16[2,128,256]{2,1,0:T(8,128)(2,1)S(1)}, bf16[2,128,256]{2,1,0:T(8,128)(2,1)S(1)}, u32[]{:S(2)}, u32[]{:S(2)}) collective-permute-start(bf16[2,128,256]{2,1,0:T(8,128)(2,1)S(1)} %slice.45), channel_id=1, source_target_pairs={{0,64},{64,128},{128,192},{192,0},{1,65},{65,129},{129,193},{193,1... | collective-permute-start | bytes 393224 | tf_op jit(solution)/shard_map/ppermute | solution.py:25
  6.0 11.7 %copy-start.3 = (f32[72,256]{1,0:T(8,128)S(1)}, f32[72,256]{1,0:T(8,128)}, u32[]{:S(2)}) copy-start(f32[72,256]{1,0:T(8,128)} %constant.58.clone.cols_ref) | copy-start | bytes 221188
  6.0 11.7 %copy-start.4 = (f32[128,128]{1,0:T(8,128)S(1)}, f32[128,128]{1,0:T(8,128)}, u32[]{:S(2)}) copy-start(f32[128,128]{1,0:T(8,128)} %constant.59.clone.rows_ref) | copy-start | bytes 196612
  7.1 12.6 %collective-permute-start.3 = (bf16[16,32,256]{2,1,0:T(8,128)(2,1)S(1)}, bf16[16,32,256]{2,1,0:T(8,128)(2,1)S(1)}, u32[]{:S(2)}, u32[]{:S(2)}) collective-permute-start(bf16[16,32,256]{2,1,0:T(8,128)(2,1)S(1)} %get-tuple-element.14), channel_id=1, source_target_pairs={{0,1},{1,0},{2,3},{3,2},{4,5},{5,4},{6,7},{7,6},{8,9},{9,8},{10,11... | collective-permute-start | bytes 786440 | tf_op jit(solution)/shard_map/ppermute | solution.py:30
  8.4 15.4 %collective-permute-start = (bf16[16,32,256]{2,1,0:T(8,128)(2,1)S(1)}, bf16[16,32,256]{2,1,0:T(8,128)(2,1)S(1)}, u32[]{:S(2)}, u32[]{:S(2)}) collective-permute-start(bf16[16,32,256]{2,1,0:T(8,128)(2,1)S(1)} %get-tuple-element.15), channel_id=1, source_target_pairs={{0,63},{1,2},{2,1},{3,4},{4,3},{5,6},{6,5},{7,8},{8,7},{9,10},{10,... | collective-permute-start | bytes 786440 | tf_op jit(solution)/shard_map/ppermute | solution.py:35
  15.7 0.7 %copy-start.6 = (s32[2,4,2]{1,2,0:T(2,128)S(1)}, s32[2,4,2]{1,2,0:T(2,128)}, u32[]{:S(2)}) copy-start(s32[2,4,2]{1,2,0:T(2,128)} %param.10) | copy-start | bytes 196
  16.3 1.3 %copy-start.7 = (s32[16]{0:T(128)S(1)}, s32[16]{0:T(128)}, u32[]{:S(2)}) copy-start(s32[16]{0:T(128)} %param.11) | copy-start | bytes 196
  16.6 3.1 %copy-start.1 = (bf16[256,256]{1,0:T(8,128)(2,1)S(1)}, bf16[256,256]{1,0:T(8,128)(2,1)}, u32[]{:S(2)}) copy-start(bf16[256,256]{1,0:T(8,128)(2,1)} %constant.61.clone.back_l_ref) | copy-start | bytes 393220
  16.6 3.1 %copy-start.2 = (bf16[256,256]{1,0:T(8,128)(2,1)S(1)}, bf16[256,256]{1,0:T(8,128)(2,1)}, u32[]{:S(2)}) copy-start(bf16[256,256]{1,0:T(8,128)(2,1)} %constant.60.clone.back_k_ref) | copy-start | bytes 393220
  16.6 3.1 %collective-permute-start.4 = (bf16[2,32,256]{2,1,0:T(8,128)(2,1)S(1)}, bf16[2,32,256]{2,1,0:T(8,128)(2,1)S(1)}, u32[]{:S(2)}, u32[]{:S(2)}) collective-permute-start(bf16[2,32,256]{2,1,0:T(8,128)(2,1)S(1)} %get-tuple-element.16), channel_id=1, source_target_pairs={{0,1},{1,0},{2,3},{3,2},{4,5},{5,4},{6,7},{7,6},{8,9},{9,8},{10,11... | collective-permute-start | bytes 98312 | tf_op jit(solution)/shard_map/ppermute | solution.py:30
  16.7 7.1 %collective-permute-start.2 = (bf16[2,32,256]{2,1,0:T(8,128)(2,1)S(1)}, bf16[2,32,256]{2,1,0:T(8,128)(2,1)S(1)}, u32[]{:S(2)}, u32[]{:S(2)}) collective-permute-start(bf16[2,32,256]{2,1,0:T(8,128)(2,1)S(1)} %get-tuple-element.17), channel_id=1, source_target_pairs={{0,63},{1,2},{2,1},{3,4},{4,3},{5,6},{6,5},{7,8},{8,7},{9,10},{10,... | collective-permute-start | bytes 98312 | tf_op jit(solution)/shard_map/ppermute | solution.py:35
  26.3 6.8 %collective-permute-start.6 = (f32[16,16]{1,0:T(8,128)S(1)}, f32[16,16]{1,0:T(8,128)S(1)}, u32[]{:S(2)}, u32[]{:S(2)}) collective-permute-start(f32[16,16]{1,0:T(8,128)S(1)} %measure_far.1), channel_id=1, source_target_pairs={{0,63},{1,2},{2,1},{3,4},{4,3},{5,6},{6,5},{7,8},{8,7},{9,10},{10,... | collective-permute-start | bytes 3080 | tf_op jit(solution)/shard_map/ppermute | solution.py:35
  30.1 3.0 %collective-permute-start.5 = (f32[16,16]{1,0:T(8,128)S(1)}, f32[16,16]{1,0:T(8,128)S(1)}, u32[]{:S(2)}, u32[]{:S(2)}) collective-permute-start(f32[16,16]{1,0:T(8,128)S(1)} %measure_far.1), channel_id=1, source_target_pairs={{0,1},{1,0},{2,3},{3,2},{4,5},{5,4},{6,7},{7,6},{8,9},{9,8},{10,11... | collective-permute-start | bytes 3080 | tf_op jit(solution)/shard_map/ppermute | solution.py:30
  33.4 1.2 %copy-start.5 = (f32[2,2,4,16]{3,2,1,0:T(4,128)}, f32[2,2,4,16]{3,2,1,0:T(4,128)S(1)}, u32[]{:S(2)}) copy-start(f32[2,2,4,16]{3,2,1,0:T(4,128)S(1)} %get-tuple-element.13) | copy-start | bytes 3076
  33.4 1.9 %collective-permute-start.7 = (f32[2,2,4]{2,1,0:T(2,128)S(1)}, f32[2,2,4]{2,1,0:T(2,128)S(1)}, u32[]{:S(2)}, u32[]{:S(2)}) collective-permute-start(f32[2,2,4]{2,1,0:T(2,128)S(1)} %get-tuple-element.12), channel_id=1, source_target_pairs={{0,64},{64,0},{128,192},{192,128},{1,65},{65,1},{129,193},{193,129... | collective-permute-start | bytes 200 | tf_op jit(solution)/shard_map/ppermute | solution.py:315
  35.2 4.1 %collective-permute-start.8 = (f32[2,2,4]{2,1,0:T(2,128)S(1)}, f32[2,2,4]{2,1,0:T(2,128)S(1)}, u32[]{:S(2)}, u32[]{:S(2)}) collective-permute-start(f32[2,2,4]{2,1,0:T(2,128)S(1)} %add.89), channel_id=1, source_target_pairs={{0,128},{64,192},{128,0},{192,64},{1,129},{65,193},{129,1},{193,65... | collective-permute-start | bytes 200 | tf_op jit(solution)/shard_map/ppermute | solution.py:317
